TPU v7x, 512 devices: a whole 4x8x8 slice. The times are simulated.
512 devices in a mesh: tm: 64 (over x, y, core), lat: 8 (over z).
Axes of the slice: x: 4, y: 8, z: 8, core: 2. Of those that a mesh axis runs over, the one named last changes fastest.
Arguments:
- x_init: float32 [64, 5, 64, 1024], P('tm', None, 'lat'), may hold values from -6 to 6
- background: float32 [5, 64, 1024], P(None, 'lat'), may hold values from -6 to 6
- observed: float32 [64, 64, 1024], P('tm', 'lat'), may hold values from -6 to 6
- diff_lon: float32 [64, 64, 1024], P('tm', 'lat'), may hold values from 0.03 to 0.2
- diff_lat: float32 [64, 64, 1024], P('tm', 'lat'), may hold values from 0.03 to 0.2
- drift: float32 [64, 64, 1024], P('tm', 'lat'), may hold values from -0.3 to 0.3
- coupling: float32 [5, 5], replicated, may hold values from -0.4 to 0.4
- model_var: float32 [5], replicated, may hold values from 0.3 to 3
- obs_level: int32 [64, 64, 8], P('tm', 'lat'), may hold values from 0 to 4
- huber_class: int32 [64, 64, 8], P('tm', 'lat'), may hold values from 0 to 2
Outputs:
- state: float32 [64, 5, 64, 1024], P('tm', None, 'lat')
- multipliers: float32 [64, 5, 64, 1024], P('tm', None, 'lat')
- obs_multipliers: float32 [64, 64, 1024], P('tm', 'lat')
All inputs are finite; a program needn't handle non-finite values.
Results may differ from a plain program's by a relative error of at most 0.0003.
Values sent between devices are 32-bit elements; how exact they have to be, the bound alone decides.
No kernel may reach another device: no remote copies, remote signals or barrier semaphores. Data moves between devices by JAX's collectives and lax.ppermute only.
A program may use at most 64 MiB of HBM per device.

v0:
```python
import jax
import jax.numpy as jnp
from jax import lax
from jax.sharding import Mesh
from jax.sharding import PartitionSpec as P

TILE = 128
STEPS = 4
ITERS = 2
TM = ("tm_0", "tm_1", "tm_2")


def padded_2(cells, sides, width):
    for axis, dim in sides:
        count = lax.axis_size(axis)
        ends = count - 1
        head = lax.slice_in_dim(cells, 0, width, axis=dim)
        tail = lax.slice_in_dim(cells, cells.shape[dim] - width, cells.shape[dim], axis=dim)
        cells = jnp.concatenate(
            [
                lax.ppermute(tail, axis, [(i, (i + 1) % count) for i in range(ends)]),
                cells,
                lax.ppermute(head, axis, [((i + 1) % count, i) for i in range(ends)]),
            ],
            axis=dim,
        )
    return cells


def passed_along(x, axis, by):
    count = lax.axis_size(axis)
    pairs = [(i, i + by) for i in range(count) if 0 <= i + by < count]
    return lax.ppermute(x, axis, pairs)


def from_everyone(x, axis):
    count = lax.axis_size(axis)
    return lax.all_to_all(jnp.broadcast_to(x[None], (count, *x.shape)), axis, 0, 0, tiled=True)


def of_everyone(x, axis):
    return from_everyone(x, axis).sum(axis=0)


def one_axis_at_a_time(x, axes):
    far, near = axes
    return of_everyone(of_everyone(x, near), far)


def local_step(v, north, south, kx, ky, ux, coupling):
    east = jnp.roll(v, -1, 2)
    west = jnp.roll(v, 1, 2)
    mixed = jnp.einsum("lm,mrc->lrc", coupling, v, precision=lax.Precision.HIGHEST)
    return (
        v
        + kx * (east + west - 2.0 * v)
        + ky * (north + south - 2.0 * v)
        + 0.5 * ux * (east - west)
        + mixed
    )


def adjoint_local(w, qnorth, qsouth, kx, ky, ux, coupling):
    p_term = kx * w
    q_term = ky * w
    u_term = ux * w
    mixed = jnp.einsum("lm,lrc->mrc", coupling, w, precision=lax.Precision.HIGHEST)
    lon_part = jnp.roll(p_term, -1, 2) + jnp.roll(p_term, 1, 2) - 2.0 * p_term
    adv_part = 0.5 * (jnp.roll(u_term, 1, 2) - jnp.roll(u_term, -1, 2))
    return w + lon_part + qnorth + qsouth - 2.0 * q_term + adv_part + mixed


def zero_rows(v):
    return jnp.pad(v, ((0, 0), (1, 1), (0, 0)))


def on_device(
    x_init,
    background,
    observed,
    diff_lon,
    diff_lat,
    drift,
    coupling,
    model_var,
    obs_level,
    huber_class,
):
    state = x_init[0]
    kx = diff_lon[0]
    ky = diff_lat[0]
    ux = drift[0]
    levels, rows, cols = state.shape
    tiles = cols // TILE
    level_ids = jnp.arange(levels, dtype=jnp.int32)
    table = (obs_level[0][None] == level_ids[:, None, None]).astype(jnp.float32)
    classes = huber_class[0]
    tile_weight = (1.0 * (classes == 0) + 0.5 * (classes == 1) + 0.25 * (classes == 2)).astype(
        jnp.float32
    )
    weights = (tile_weight[..., None] * jnp.ones((TILE,), jnp.float32)).reshape(rows, cols)
    variance = model_var[:, None, None]
    first_sub = lax.axis_index(TM) == 0
    count = state.size * lax.axis_size(TM) * lax.axis_size("lat")
    stacked = padded_2(jnp.stack([kx, ky, ux]), (("lat", 1),), STEPS)
    wide_kx, wide_ky, wide_ux = (stacked[0], stacked[1], stacked[2])
    global_row = (
        lax.axis_index("lat") * rows - STEPS + jnp.arange(rows + 2 * STEPS, dtype=jnp.int32)
    )
    total_rows = rows * lax.axis_size("lat")
    inside = ((global_row >= 0) & (global_row < total_rows)).astype(jnp.float32)[:, None]
    multipliers = jnp.zeros_like(state)
    obs_multipliers = jnp.zeros_like(observed[0])
    for it in range(ITERS):
        forward_wide = padded_2(state, (("lat", 1),), STEPS)
        for forward_step in range(STEPS):
            forward_padded = zero_rows(forward_wide)
            forward_wide = (
                local_step(
                    forward_wide,
                    forward_padded[:, 2:],
                    forward_padded[:, :-2],
                    wide_kx,
                    wide_ky,
                    wide_ux,
                    coupling,
                )
                * inside
            )
        moved = forward_wide[:, STEPS : STEPS + rows]
        arrived = passed_along(moved, TM, 1)
        prior = jnp.where(first_sub, background, arrived)
        multipliers = multipliers + 0.5 * (state - prior - variance * multipliers)
        picked = jnp.sum(
            state.reshape(levels, rows, tiles, TILE) * table[..., None], axis=0
        ).reshape(rows, cols)
        obs_multipliers = obs_multipliers + 0.5 * (
            weights * (picked - observed[0]) - obs_multipliers
        )
        later = passed_along(multipliers, TM, -1)
        wide = padded_2(later, (("lat", 1),), STEPS)
        for step in range(STEPS):
            padded = zero_rows(wide_ky * wide)
            wide = (
                adjoint_local(
                    wide, padded[:, 2:], padded[:, :-2], wide_kx, wide_ky, wide_ux, coupling
                )
                * inside
            )
        pulled = wide[:, STEPS : STEPS + rows]
        placed = (table[..., None] * obs_multipliers.reshape(rows, tiles, TILE)[None]).reshape(
            levels, rows, cols
        )
        gradient = multipliers - pulled + placed
        total = one_axis_at_a_time(
            jnp.sum(gradient * gradient), (("tm_0", "tm_1"), ("tm_2", "lat"))
        )
        scale = jnp.sqrt(total / count + 1e-06)
        state = state - 0.3 * gradient / scale
    return (state[None], multipliers[None], obs_multipliers[None])


def solution(mesh):
    torus = Mesh(mesh.devices.reshape(4, 8, 2, mesh.shape["lat"]), ("tm_0", "tm_1", "tm_2", "lat"))
    in_specs = (
        P(TM, None, "lat", None),
        P(None, "lat", None),
        P(TM, "lat", None),
        P(TM, "lat", None),
        P(TM, "lat", None),
        P(TM, "lat", None),
        P(),
        P(),
        P(TM, "lat", None),
        P(TM, "lat", None),
    )
    out_specs = (P(TM, None, "lat", None), P(TM, None, "lat", None), P(TM, "lat", None))
    return jax.shard_map(
        on_device, mesh=torus, in_specs=in_specs, out_specs=out_specs, check_vma=False
    )
```

profile of v0, /device:TPU:1, one launch (start us, length us, event | category | flops | bytes accessed | tf_op | source)
XLA Modules:
  0.0 177.5 jit_solution(8875291460545482719)
XLA Ops:
  0.7 0.8 constant_dynamic-update-slice_fusion.2
  1.5 5.0 %collective-permute-start.2 = (f32[3,4,1024]{2,1,0:T(4,128)S(1)}, f32[3,4,1024]{2,1,0:T(4,128)S(1)}, u32[]{:S(2)}, u32[]{:S(2)}) collective-permute-start(f32[3,4,1024]{2,1,0:T(4,128)S(1)} %get-tuple-element.163), channel_id=1, source_target_pairs={{0,1},{1,2},{2,3},{3,4},{4,5},{5,6},{6,7},{8,9},{9,10},{10,11},{11... | collective-permute-start | bytes 147464 | tf_op jit(solution)/shard_map/ppermute | solution.py:21
  6.5 1.3 collective-permute-start.3
  7.9 4.6 %collective-permute-start = (f32[5,4,1024]{2,0,1:T(8,128)S(1)}, f32[5,4,1024]{2,0,1:T(8,128)S(1)}, u32[]{:S(2)}, u32[]{:S(2)}) collective-permute-start(f32[5,4,1024]{2,0,1:T(8,128)S(1)} %get-tuple-element.157), channel_id=1, source_target_pairs={{0,1},{1,2},{2,3},{3,4},{4,5},{5,6},{6,7},{8,9},{9,10},{10,11},{11... | collective-permute-start | bytes 245768 | tf_op jit(solution)/shard_map/ppermute | solution.py:21
  12.6 1.3 collective-permute-start.1
  14.5 4.4 %collective-permute-done.1 = f32[5,4,1024]{2,0,1:T(8,128)S(1)} collective-permute-done((f32[5,4,1024]{2,0,1:T(8,128)S(1)}, f32[5,4,1024]{2,0,1:T(8,128)S(1)}, u32[]{:S(2)}, u32[]{:S(2)}) %collective-permute-start.1) | collective-permute-done | bytes 81952 | tf_op jit(solution)/shard_map/ppermute | solution.py:23
  19.3 0.9 fusion.22
  20.5 0.9 fusion.1
  21.6 0.9 fusion.3
  23.9 5.2 %collective-permute-start.4 = (f32[5,8,1024]{2,0,1:T(8,128)S(1)}, f32[5,8,1024]{2,0,1:T(8,128)S(1)}, u32[]{:S(2)}, u32[]{:S(2)}) collective-permute-start(f32[5,8,1024]{2,0,1:T(8,128)S(1)} %fusion.127), channel_id=1, source_target_pairs={{0,8},{8,16},{16,24},{24,32},{32,40},{40,48},{48,56},{56,64},{64,7... | collective-permute-start | bytes 491528 | tf_op jit(solution)/shard_map/ppermute | solution.py:33
  29.2 3.3 %collective-permute-done.4 = f32[5,8,1024]{2,0,1:T(8,128)S(1)} collective-permute-done((f32[5,8,1024]{2,0,1:T(8,128)S(1)}, f32[5,8,1024]{2,0,1:T(8,128)S(1)}, u32[]{:S(2)}, u32[]{:S(2)}) %collective-permute-start.4) | collective-permute-done | bytes 163872 | tf_op jit(solution)/shard_map/ppermute | solution.py:33
  32.7 1.9 %collective-permute-start.5 = (f32[5,8,1024]{2,0,1:T(8,128)S(1)}, f32[5,8,1024]{2,0,1:T(8,128)S(1)}, u32[]{:S(2)}, u32[]{:S(2)}) collective-permute-start(f32[5,8,1024]{2,0,1:T(8,128)S(1)} %broadcast_multiply_fusion.26), channel_id=1, source_target_pairs={{8,0},{16,8},{24,16},{32,24},{40,32},{48,40},{56,48},{64,56},{72,6... | collective-permute-start | bytes 491528 | tf_op jit(solution)/shard_map/ppermute | solution.py:33
  34.9 6.2 %collective-permute-done.5 = f32[5,8,1024]{2,0,1:T(8,128)S(1)} collective-permute-done((f32[5,8,1024]{2,0,1:T(8,128)S(1)}, f32[5,8,1024]{2,0,1:T(8,128)S(1)}, u32[]{:S(2)}, u32[]{:S(2)}) %collective-permute-start.5) | collective-permute-done | bytes 163872 | tf_op jit(solution)/shard_map/ppermute | solution.py:33
  41.1 5.5 %collective-permute-start.6 = (f32[5,4,1024]{2,0,1:T(8,128)S(1)}, f32[5,4,1024]{2,0,1:T(8,128)S(1)}, u32[]{:S(2)}, u32[]{:S(2)}) collective-permute-start(f32[5,4,1024]{2,0,1:T(8,128)S(1)} %get-tuple-element.156), channel_id=1, source_target_pairs={{0,1},{1,2},{2,3},{3,4},{4,5},{5,6},{6,7},{8,9},{9,10},{10,11},{11... | collective-permute-start | bytes 245768 | tf_op jit(solution)/shard_map/ppermute | solution.py:21
  46.8 1.5 collective-permute-start.7
  48.6 5.4 %collective-permute-done.7 = f32[5,4,1024]{2,0,1:T(8,128)S(1)} collective-permute-done((f32[5,4,1024]{2,0,1:T(8,128)S(1)}, f32[5,4,1024]{2,0,1:T(8,128)S(1)}, u32[]{:S(2)}, u32[]{:S(2)}) %collective-permute-start.7) | collective-permute-done | bytes 81952 | tf_op jit(solution)/shard_map/ppermute | solution.py:23
  54.6 1.3 broadcast_multiply_fusion.6
  56.5 1.4 broadcast_multiply_fusion.5
  58.5 1.2 broadcast_multiply_fusion.21
  61.4 1.1 multiply_reduce_fusion.1
  62.5 0.6 broadcast_in_dim.15
  63.2 13.5 %all_to_all.24 = f32[16,1,1]{2,1,0:T(1,128)S(1)} all-to-all(f32[16,1,1]{2,1,0:T(1,128)S(1)} %broadcast_in_dim.15), channel_id=1, replica_groups=mesh['tm_0'=4,'tm_1'=8,'tm_2'=2,'lat'=8] {'tm_2','lat'}, dimensions={0} | all-to-all | bytes 128 | tf_op jit(solution)/shard_map/all_to_all | solution.py:38
  77.3 0.7 broadcast_in_dim.16
  78.0 18.9 %all_to_all.25 = f32[32,1,1]{2,1,0:T(1,128)S(1)} all-to-all(f32[32,1,1]{2,1,0:T(1,128)S(1)} %broadcast_in_dim.16), channel_id=1, replica_groups=mesh['tm_0'=4,'tm_1'=8,'tm_2'=2,'lat'=8] {'tm_0','tm_1'}, dimensions={0} | all-to-all | bytes 256 | tf_op jit(solution)/shard_map/all_to_all | solution.py:38
  98.5 2.2 %collective-permute-start.8 = (f32[5,4,1024]{2,0,1:T(8,128)S(1)}, f32[5,4,1024]{2,0,1:T(8,128)S(1)}, u32[]{:S(2)}, u32[]{:S(2)}) collective-permute-start(f32[5,4,1024]{2,0,1:T(8,128)S(1)} %get-tuple-element.153), channel_id=1, source_target_pairs={{0,1},{1,2},{2,3},{3,4},{4,5},{5,6},{6,7},{8,9},{9,10},{10,11},{11... | collective-permute-start | bytes 245768 | tf_op jit(solution)/shard_map/ppermute | solution.py:21
  100.8 1.5 collective-permute-start.9
  102.7 3.8 %collective-permute-done.9 = f32[5,4,1024]{2,0,1:T(8,128)S(1)} collective-permute-done((f32[5,4,1024]{2,0,1:T(8,128)S(1)}, f32[5,4,1024]{2,0,1:T(8,128)S(1)}, u32[]{:S(2)}, u32[]{:S(2)}) %collective-permute-start.9) | collective-permute-done | bytes 81952 | tf_op jit(solution)/shard_map/ppermute | solution.py:23
  106.8 0.9 fusion.54
  108.0 0.9 fusion.9
  109.2 0.9 fusion.11
  111.5 5.7 %collective-permute-start.10 = (f32[5,8,1024]{2,0,1:T(8,128)S(1)}, f32[5,8,1024]{2,0,1:T(8,128)S(1)}, u32[]{:S(2)}, u32[]{:S(2)}) collective-permute-start(f32[5,8,1024]{2,0,1:T(8,128)S(1)} %fusion.120), channel_id=1, source_target_pairs={{0,8},{8,16},{16,24},{24,32},{32,40},{40,48},{48,56},{56,64},{64,7... | collective-permute-start | bytes 491528 | tf_op jit(solution)/shard_map/ppermute | solution.py:33
  117.2 3.3 %collective-permute-done.10 = f32[5,8,1024]{2,0,1:T(8,128)S(1)} collective-permute-done((f32[5,8,1024]{2,0,1:T(8,128)S(1)}, f32[5,8,1024]{2,0,1:T(8,128)S(1)}, u32[]{:S(2)}, u32[]{:S(2)}) %collective-permute-start.10) | collective-permute-done | bytes 163872 | tf_op jit(solution)/shard_map/ppermute | solution.py:33
  120.7 1.9 %collective-permute-start.11 = (f32[5,8,1024]{2,0,1:T(8,128)S(1)}, f32[5,8,1024]{2,0,1:T(8,128)S(1)}, u32[]{:S(2)}, u32[]{:S(2)}) collective-permute-start(f32[5,8,1024]{2,0,1:T(8,128)S(1)} %fusion.111), channel_id=1, source_target_pairs={{8,0},{16,8},{24,16},{32,24},{40,32},{48,40},{56,48},{64,56},{72,6... | collective-permute-start | bytes 491528 | tf_op jit(solution)/shard_map/ppermute | solution.py:33
  122.7 6.5 %collective-permute-done.11 = f32[5,8,1024]{2,0,1:T(8,128)S(1)} collective-permute-done((f32[5,8,1024]{2,0,1:T(8,128)S(1)}, f32[5,8,1024]{2,0,1:T(8,128)S(1)}, u32[]{:S(2)}, u32[]{:S(2)}) %collective-permute-start.11) | collective-permute-done | bytes 163872 | tf_op jit(solution)/shard_map/ppermute | solution.py:33
  129.2 2.5 %collective-permute-start.12 = (f32[5,4,1024]{2,0,1:T(8,128)S(1)}, f32[5,4,1024]{2,0,1:T(8,128)S(1)}, u32[]{:S(2)}, u32[]{:S(2)}) collective-permute-start(f32[5,4,1024]{2,0,1:T(8,128)S(1)} %get-tuple-element.152), channel_id=1, source_target_pairs={{0,1},{1,2},{2,3},{3,4},{4,5},{5,6},{6,7},{8,9},{9,10},{10,11},{11... | collective-permute-start | bytes 245768 | tf_op jit(solution)/shard_map/ppermute | solution.py:21
  131.8 1.3 collective-permute-start.13
  133.6 3.8 %collective-permute-done.13 = f32[5,4,1024]{2,0,1:T(8,128)S(1)} collective-permute-done((f32[5,4,1024]{2,0,1:T(8,128)S(1)}, f32[5,4,1024]{2,0,1:T(8,128)S(1)}, u32[]{:S(2)}, u32[]{:S(2)}) %collective-permute-start.13) | collective-permute-done | bytes 81952 | tf_op jit(solution)/shard_map/ppermute | solution.py:23
  138.2 1.4 broadcast_multiply_fusion.2
  140.2 1.4 broadcast_multiply_fusion.1
  142.1 1.2 broadcast_multiply_fusion.25
  145.0 0.9 multiply_reduce_fusion
  146.6 10.9 %all_to_all.26 = f32[16,1,1]{2,1,0:T(1,128)S(1)} all-to-all(f32[16,1,1]{2,1,0:T(1,128)S(1)} %broadcast_in_dim.17), channel_id=1, replica_groups=mesh['tm_0'=4,'tm_1'=8,'tm_2'=2,'lat'=8] {'tm_2','lat'}, dimensions={0} | all-to-all | bytes 128 | tf_op jit(solution)/shard_map/all_to_all | solution.py:38
  158.1 1.3 broadcast_in_dim.18
  159.4 7.3 %all-to-all-start.3 = ((f32[32,1,1]{2,1,0:T(1,128)}), f32[32,1,1]{2,1,0:T(1,128)S(1)}, u32[]{:S(2)}, u32[]{:S(2)}) async-start(f32[32,1,1]{2,1,0:T(1,128)} %broadcast_in_dim.18), calls=%async_computation.3 | async-start | bytes 32768 | tf_op jit(solution)/shard_map/all_to_all | solution.py:38
  166.7 0.7 fusion.152
  167.4 0.8 copy.82
  168.2 7.1 %all-to-all-done.3 = f32[32,1,1]{2,1,0:T(1,128)S(1)} async-done(((f32[32,1,1]{2,1,0:T(1,128)}), f32[32,1,1]{2,1,0:T(1,128)S(1)}, u32[]{:S(2)}, u32[]{:S(2)}) %all-to-all-start.3) | async-done | bytes 160 | tf_op jit(solution)/shard_map/all_to_all | solution.py:38
  176.7 0.8 copy.81
  (126 shorter events, 18.1 us)
Async XLA Ops:
  0.6 18.6 %copy-start = (f32[5,5]{1,0:T(8,128)S(1)}, f32[5,5]{1,0:T(8,128)}, u32[]{:S(2)}) copy-start(f32[5,5]{1,0:T(8,128)} %param.16) | copy-start | bytes 304
  0.6 0.8 copy-start.4
  0.7 0.8 copy-start.5
  1.4 6.3 %copy-start.1 = (f32[1,5,8,1024]{3,2,1,0:T(8,128)S(1)}, f32[1,5,8,1024]{3,2,1,0:T(8,128)}, u32[]{:S(2)}) copy-start(f32[1,5,8,1024]{3,2,1,0:T(8,128)} %param.10) | copy-start | bytes 491524
  1.5 12.5 %collective-permute-start.2 = (f32[3,4,1024]{2,1,0:T(4,128)S(1)}, f32[3,4,1024]{2,1,0:T(4,128)S(1)}, u32[]{:S(2)}, u32[]{:S(2)}) collective-permute-start(f32[3,4,1024]{2,1,0:T(4,128)S(1)} %get-tuple-element.163), channel_id=1, source_target_pairs={{0,1},{1,2},{2,3},{3,4},{4,5},{5,6},{6,7},{8,9},{9,10},{10,11},{11... | collective-permute-start | bytes 147464 | tf_op jit(solution)/shard_map/ppermute | solution.py:21
  6.5 7.5 %collective-permute-start.3 = (f32[3,4,1024]{2,1,0:T(4,128)S(1)}, f32[3,4,1024]{2,1,0:T(4,128)S(1)}, u32[]{:S(2)}, u32[]{:S(2)}) collective-permute-start(f32[3,4,1024]{2,1,0:T(4,128)S(1)} %get-tuple-element.164), channel_id=1, source_target_pairs={{1,0},{2,1},{3,2},{4,3},{5,4},{6,5},{7,6},{9,8},{10,9},{11,10},{12... | collective-permute-start | bytes 147464 | tf_op jit(solution)/shard_map/ppermute | solution.py:23
  7.9 6.6 %collective-permute-start = (f32[5,4,1024]{2,0,1:T(8,128)S(1)}, f32[5,4,1024]{2,0,1:T(8,128)S(1)}, u32[]{:S(2)}, u32[]{:S(2)}) collective-permute-start(f32[5,4,1024]{2,0,1:T(8,128)S(1)} %get-tuple-element.157), channel_id=1, source_target_pairs={{0,1},{1,2},{2,3},{3,4},{4,5},{5,6},{6,7},{8,9},{9,10},{10,11},{11... | collective-permute-start | bytes 245768 | tf_op jit(solution)/shard_map/ppermute | solution.py:21
  12.6 1.3 copy-start.7
  12.6 6.3 %collective-permute-start.1 = (f32[5,4,1024]{2,0,1:T(8,128)S(1)}, f32[5,4,1024]{2,0,1:T(8,128)S(1)}, u32[]{:S(2)}, u32[]{:S(2)}) collective-permute-start(f32[5,4,1024]{2,0,1:T(8,128)S(1)} %get-tuple-element.158), channel_id=1, source_target_pairs={{1,0},{2,1},{3,2},{4,3},{5,4},{6,5},{7,6},{9,8},{10,9},{11,10},{12... | collective-permute-start | bytes 245768 | tf_op jit(solution)/shard_map/ppermute | solution.py:23
  23.7 5.4 %copy-start.8 = (f32[5]{0:T(128)S(1)}, f32[5]{0:T(128)}, u32[]{:S(2)}) copy-start(f32[5]{0:T(128)} %param.17) | copy-start | bytes 64
  23.7 8.7 %copy-start.2 = (f32[5,8,1024]{2,1,0:T(8,128)S(1)}, f32[5,8,1024]{2,1,0:T(8,128)}, u32[]{:S(2)}) copy-start(f32[5,8,1024]{2,1,0:T(8,128)} %param.11) | copy-start | bytes 491524
  23.9 8.5 %collective-permute-start.4 = (f32[5,8,1024]{2,0,1:T(8,128)S(1)}, f32[5,8,1024]{2,0,1:T(8,128)S(1)}, u32[]{:S(2)}, u32[]{:S(2)}) collective-permute-start(f32[5,8,1024]{2,0,1:T(8,128)S(1)} %fusion.127), channel_id=1, source_target_pairs={{0,8},{8,16},{16,24},{24,32},{32,40},{40,48},{48,56},{56,64},{64,7... | collective-permute-start | bytes 491528 | tf_op jit(solution)/shard_map/ppermute | solution.py:33
  32.4 2.2 %copy-start.6 = (s32[1,8,8]{2,1,0:T(8,128)S(1)}, s32[1,8,8]{2,1,0:T(8,128)}, u32[]{:S(2)}) copy-start(s32[1,8,8]{2,1,0:T(8,128)} %param.19) | copy-start | bytes 772
  32.7 8.4 %collective-permute-start.5 = (f32[5,8,1024]{2,0,1:T(8,128)S(1)}, f32[5,8,1024]{2,0,1:T(8,128)S(1)}, u32[]{:S(2)}, u32[]{:S(2)}) collective-permute-start(f32[5,8,1024]{2,0,1:T(8,128)S(1)} %broadcast_multiply_fusion.26), channel_id=1, source_target_pairs={{8,0},{16,8},{24,16},{32,24},{40,32},{48,40},{56,48},{64,56},{72,6... | collective-permute-start | bytes 491528 | tf_op jit(solution)/shard_map/ppermute | solution.py:33
  34.8 11.8 %copy-start.3 = (f32[1,8,1024]{2,1,0:T(8,128)S(1)}, f32[1,8,1024]{2,1,0:T(8,128)}, u32[]{:S(2)}) copy-start(f32[1,8,1024]{2,1,0:T(8,128)} %param.12) | copy-start | bytes 98308
  41.1 7.4 %collective-permute-start.6 = (f32[5,4,1024]{2,0,1:T(8,128)S(1)}, f32[5,4,1024]{2,0,1:T(8,128)S(1)}, u32[]{:S(2)}, u32[]{:S(2)}) collective-permute-start(f32[5,4,1024]{2,0,1:T(8,128)S(1)} %get-tuple-element.156), channel_id=1, source_target_pairs={{0,1},{1,2},{2,3},{3,4},{4,5},{5,6},{6,7},{8,9},{9,10},{10,11},{11... | collective-permute-start | bytes 245768 | tf_op jit(solution)/shard_map/ppermute | solution.py:21
  46.8 7.2 %collective-permute-start.7 = (f32[5,4,1024]{2,0,1:T(8,128)S(1)}, f32[5,4,1024]{2,0,1:T(8,128)S(1)}, u32[]{:S(2)}, u32[]{:S(2)}) collective-permute-start(f32[5,4,1024]{2,0,1:T(8,128)S(1)} %get-tuple-element.155), channel_id=1, source_target_pairs={{1,0},{2,1},{3,2},{4,3},{5,4},{6,5},{7,6},{9,8},{10,9},{11,10},{12... | collective-permute-start | bytes 245768 | tf_op jit(solution)/shard_map/ppermute | solution.py:23
  98.5 4.2 %collective-permute-start.8 = (f32[5,4,1024]{2,0,1:T(8,128)S(1)}, f32[5,4,1024]{2,0,1:T(8,128)S(1)}, u32[]{:S(2)}, u32[]{:S(2)}) collective-permute-start(f32[5,4,1024]{2,0,1:T(8,128)S(1)} %get-tuple-element.153), channel_id=1, source_target_pairs={{0,1},{1,2},{2,3},{3,4},{4,5},{5,6},{6,7},{8,9},{9,10},{10,11},{11... | collective-permute-start | bytes 245768 | tf_op jit(solution)/shard_map/ppermute | solution.py:21
  100.8 5.7 %collective-permute-start.9 = (f32[5,4,1024]{2,0,1:T(8,128)S(1)}, f32[5,4,1024]{2,0,1:T(8,128)S(1)}, u32[]{:S(2)}, u32[]{:S(2)}) collective-permute-start(f32[5,4,1024]{2,0,1:T(8,128)S(1)} %get-tuple-element.154), channel_id=1, source_target_pairs={{1,0},{2,1},{3,2},{4,3},{5,4},{6,5},{7,6},{9,8},{10,9},{11,10},{12... | collective-permute-start | bytes 245768 | tf_op jit(solution)/shard_map/ppermute | solution.py:23
  111.5 9.0 %collective-permute-start.10 = (f32[5,8,1024]{2,0,1:T(8,128)S(1)}, f32[5,8,1024]{2,0,1:T(8,128)S(1)}, u32[]{:S(2)}, u32[]{:S(2)}) collective-permute-start(f32[5,8,1024]{2,0,1:T(8,128)S(1)} %fusion.120), channel_id=1, source_target_pairs={{0,8},{8,16},{16,24},{24,32},{32,40},{40,48},{48,56},{56,64},{64,7... | collective-permute-start | bytes 491528 | tf_op jit(solution)/shard_map/ppermute | solution.py:33
  120.7 8.4 %collective-permute-start.11 = (f32[5,8,1024]{2,0,1:T(8,128)S(1)}, f32[5,8,1024]{2,0,1:T(8,128)S(1)}, u32[]{:S(2)}, u32[]{:S(2)}) collective-permute-start(f32[5,8,1024]{2,0,1:T(8,128)S(1)} %fusion.111), channel_id=1, source_target_pairs={{8,0},{16,8},{24,16},{32,24},{40,32},{48,40},{56,48},{64,56},{72,6... | collective-permute-start | bytes 491528 | tf_op jit(solution)/shard_map/ppermute | solution.py:33
  129.2 4.4 %collective-permute-start.12 = (f32[5,4,1024]{2,0,1:T(8,128)S(1)}, f32[5,4,1024]{2,0,1:T(8,128)S(1)}, u32[]{:S(2)}, u32[]{:S(2)}) collective-permute-start(f32[5,4,1024]{2,0,1:T(8,128)S(1)} %get-tuple-element.152), channel_id=1, source_target_pairs={{0,1},{1,2},{2,3},{3,4},{4,5},{5,6},{6,7},{8,9},{9,10},{10,11},{11... | collective-permute-start | bytes 245768 | tf_op jit(solution)/shard_map/ppermute | solution.py:21
  131.8 5.7 %collective-permute-start.13 = (f32[5,4,1024]{2,0,1:T(8,128)S(1)}, f32[5,4,1024]{2,0,1:T(8,128)S(1)}, u32[]{:S(2)}, u32[]{:S(2)}) collective-permute-start(f32[5,4,1024]{2,0,1:T(8,128)S(1)} %get-tuple-element.151), channel_id=1, source_target_pairs={{1,0},{2,1},{3,2},{4,3},{5,4},{6,5},{7,6},{9,8},{10,9},{11,10},{12... | collective-permute-start | bytes 245768 | tf_op jit(solution)/shard_map/ppermute | solution.py:23
  159.4 15.9 %all-to-all-start.3 = ((f32[32,1,1]{2,1,0:T(1,128)}), f32[32,1,1]{2,1,0:T(1,128)S(1)}, u32[]{:S(2)}, u32[]{:S(2)}) async-start(f32[32,1,1]{2,1,0:T(1,128)} %broadcast_in_dim.18), calls=%async_computation.3 | async-start | bytes 32768 | tf_op jit(solution)/shard_map/all_to_all | solution.py:38
where the time goes:
time: 178 us; the launch traced here: 177 us
  starting transfers between devices  48.7 us (27%)
  waiting for transfers between devices  45.5 us (26%)
  blocking collectives  43.3 us (24%)
  matrix products  15.6 us (9%)
  local copies, waits for them, and re-layouts  13.2 us (7%)
  other arithmetic  8.45 us (5%)
  between operations  2.72 us (2%)
    all_to_all x3, blocking collectives, from_everyone(): lax.all_to_all(jnp.broadcast_to(x[None], (count, *x.shape)), axis, 0, 0,...  43.3 us
    ppermute x5, starting transfers between devices, padded_2(): lax.ppermute(tail, axis, [(i, (i + 1) % count) for i in range(ends)])  19.8 us
    ppermute x4, waiting for transfers between devices, passed_along(): return lax.ppermute(x, axis, pairs)  19.3 us
    ppermute x5, waiting for transfers between devices, padded_2(): lax.ppermute(head, axis, [((i + 1) % count, i) for i in range(ends)])  17.4 us
    ppermute x4, starting transfers between devices, passed_along(): return lax.ppermute(x, axis, pairs)  14.7 us
    dot_general x8, matrix products, adjoint_local(): jnp.einsum('lm,lrc->mrc', coupling, w, precision=lax.Precision.HIGHEST)  9.06 us
    all_to_all x1, starting transfers between devices, from_everyone(): lax.all_to_all(jnp.broadcast_to(x[None], (count, *x.shape)), axis, 0, 0,...  7.32 us
    all_to_all x1, waiting for transfers between devices, from_everyone(): lax.all_to_all(jnp.broadcast_to(x[None], (count, *x.shape)), axis, 0, 0,...  7.1 us
  transfers between devices with their start and end apart: 15, of which 13 were waited for; matrix products, arithmetic and copies ran while one was open for 1% of the time, Pallas kernels for 0%

commit v1 on v0

v1 whole, which is shorter than its diff:
```python
import jax
import jax.numpy as jnp
from jax import lax
from jax.experimental import pallas as pl
from jax.experimental.pallas import tpu as pltpu
from jax.sharding import Mesh
from jax.sharding import PartitionSpec as P

L = 5
TILE = 128
STEPS = 4
ROWS = 8
H = STEPS
W = ROWS + 2 * H
TM = ("tm_0", "tm_1", "tm_2")
FAR = ("tm_0", "tm_1")
NEAR = ("tm_2", "lat")
ROW = (8, TILE)


def lanes():
    return lax.broadcasted_iota(jnp.int32, ROW, 1)


class Shift:
    def __init__(self):
        lane = lanes()
        self.first = lane == 0
        self.last = lane == TILE - 1

    def east(self, v):
        r = pltpu.roll(v, TILE - 1, 1)
        return jnp.where(self.last, pltpu.roll(r, 7, 0), r)

    def west(self, v):
        r = pltpu.roll(v, 1, 1)
        return jnp.where(self.first, pltpu.roll(r, 1, 0), r)


def total(terms):
    while len(terms) > 1:
        terms = [a + b for a, b in zip(terms[::2], terms[1::2])] + (
            [terms[-1]] if len(terms) % 2 else []
        )
    return terms[0]


def centre(ce, cw, ky):
    return (1.0 - (ce + cw)) - 2.0 * ky


def forward(src, coef, c, rows, bufs, dst):
    sh = Shift()
    for step in range(STEPS):
        lo, hi = step + 1, rows - step - 1

        def get(r, step=step):
            if step == 0:
                return [src(l, r) for l in range(L)]
            return [bufs[(step - 1) % 2][l, r] for l in range(L)]

        above, here = get(lo - 1), get(lo)
        for r in range(lo, hi):
            below = get(r + 1)
            ce, cw, ky = coef(0, r), coef(1, r), coef(2, r)
            c0 = centre(ce, cw, ky)
            for l in range(L):
                v = here[l]
                terms = [
                    ce * sh.east(v),
                    cw * sh.west(v),
                    ky * (above[l] + below[l]),
                    c0 * v,
                ] + [c[l][m] * here[m] for m in range(L)]
                out = total(terms)
                if step == STEPS - 1:
                    dst(l, r, out)
                else:
                    bufs[step % 2][l, r] = out
            above, here = here, below


def adjoint(src, coef, c, rows, bufs, dst):
    sh = Shift()
    for step in range(STEPS):
        lo, hi = step + 1, rows - step - 1

        def get(r, step=step):
            if step == 0:
                v = [src(l, r) for l in range(L)]
            else:
                v = [bufs[(step - 1) % 2][l, r] for l in range(L)]
            ky = coef(2, r)
            return v, [ky * w for w in v]

        (_, above), (here, q) = get(lo - 1), get(lo)
        for r in range(lo, hi):
            after, below = get(r + 1)
            ce, cw, ky = coef(0, r), coef(1, r), coef(2, r)
            c0 = centre(ce, cw, ky)
            for l in range(L):
                w = here[l]
                terms = [
                    sh.west(ce * w),
                    sh.east(cw * w),
                    above[l] + below[l],
                    c0 * w,
                ] + [c[m][l] * here[m] for m in range(L)]
                out = total(terms)
                if step == STEPS - 1:
                    dst(l, r, out)
                else:
                    bufs[step % 2][l, r] = out
            above, here, q = q, after, below


def scalars(ref):
    return [[ref[l, m] for m in range(L)] for l in range(L)]


def banded(up, own, down, first):
    def at(k, r):
        part = (up, own, down)[r // ROWS]
        return part[first + k, r % ROWS]

    return at


def not_last():
    j = (lax.axis_index("tm_0") * lax.axis_size("tm_1") + lax.axis_index("tm_1")) * lax.axis_size(
        "tm_2"
    ) + lax.axis_index("tm_2")
    last = lax.axis_size("tm_0") * lax.axis_size("tm_1") * lax.axis_size("tm_2") - 1
    return jnp.where(j == last, 0.0, 1.0), jnp.where(j == 0, 1.0, 0.0)


def split(v):
    return jnp.swapaxes(jnp.stack([v[:, s * TILE : (s + 1) * TILE] for s in range(8)]), 0, 1)


def join_into(ref, index, rows):
    v = jnp.swapaxes(jnp.stack(rows), 0, 1)
    for s in range(8):
        ref[(*index, slice(None), slice(s * TILE, (s + 1) * TILE))] = v[s]


def pack_kernel(x, kx, ky, ux, out):
    for l in range(L):
        out[l] = split(x[l])
    k, u = kx[...], 0.5 * ux[...]
    out[L] = split(k + u)
    out[L + 1] = split(k - u)
    out[L + 2] = split(ky[...])


def aside_kernel(background, observed, bg, obs):
    for l in range(L):
        bg[l] = split(background[l])
    obs[...] = split(observed[...])


def middle_kernel(up, own, down, all_out, x_out):
    for k in range(L + 3):
        for ref, rows, base in ((up, range(H, ROWS), 0), (own, range(ROWS), H), (down, range(H), H + ROWS)):
            for r in rows:
                v = ref[k, r]
                to = base + r - (H if base == 0 else 0)
                all_out[k, to] = v
                if k < L:
                    x_out[k, to] = v


def middle_g_kernel(up, own, down, out):
    for k in range(L):
        out[k, :H] = up[k, H:]
        out[k, H : H + ROWS] = own[k]
        out[k, H + ROWS :] = down[k, :H]


def forward_kernel(c_ref, up, own, down, up_c, own_c, down_c, out, a, b):
    def dst(l, r, v):
        out[l, r - H] = v

    forward(
        banded(up, own, down, 0),
        banded(up_c, own_c, down_c, L),
        scalars(c_ref),
        3 * ROWS,
        (a, b),
        dst,
    )


def picked(level, values):
    out = jnp.zeros(ROW, jnp.float32)
    for l in range(L):
        out = out + jnp.where(level == l, values[l], 0.0)
    return out


def gradient_kernel(
    c_ref, before, after, moved, up, own, down, bg, obs, level, weight, g, d, ahead, o1, a, b
):
    c = scalars(c_ref)
    some, first = not_last()
    half = 0.5 * some
    for l in range(L):
        for r in range(W):
            ahead[l, r] = half * (after[l, r] - moved[l, r])

    def prior(l, r, v):
        d[l, r - H] = 0.5 * (own[l, r - H] - (v + first * bg[l, r - H]))

    forward(lambda l, r: before[l, r], lambda k, r: before[L + k, r], c, W, (a, b), prior)
    coef = banded(up, own, down, L)
    for r in range(ROWS):
        o1[r] = 0.5 * weight[r] * (picked(level[r], [own[l, r] for l in range(L)]) - obs[r])

    def dst(l, r, v):
        r = r - H
        g[l, r] = d[l, r] - v + jnp.where(level[r] == l, o1[r], 0.0)

    adjoint(lambda l, r: ahead[l, r], lambda k, r: coef(k, r + H), c, W, (a, b), dst)


def still_kernel(c_ref, var, d, ahead, own, up, down, level, o1, g0, a, b):
    c = scalars(c_ref)
    keep = [2.0 - 0.5 * var[l] for l in range(L)]
    coef = banded(up, own, down, L)

    def dst(l, r, v):
        r = r - H
        g0[l, r] = keep[l] * d[l, r] - v + jnp.where(level[r] == l, 1.5 * o1[r], 0.0)

    adjoint(lambda l, r: keep[l] * ahead[l, r], lambda k, r: coef(k, r + H), c, W, (a, b), dst)


def curvature_kernel(
    c_ref, coefs, before, after, moved, up, own, down, own_g, level, weight, g0, u, g1, hg, part, ahead, a, b
):
    c = scalars(c_ref)
    some, _ = not_last()
    for l in range(L):
        for r in range(W):
            ahead[l, r] = some * (after[l, r] - moved[l, r])

    def misfit(l, r, v):
        u[l, r - H] = own_g[l, r - H] - v

    forward(lambda l, r: before[l, r], lambda k, r: coefs[L + k, r], c, W, (a, b), misfit)
    coef = banded(up, own, down, L)
    for r in range(ROWS):
        hg[r] = weight[r] * picked(level[r], [own_g[l, r] for l in range(L)])
    sums = [[], [], [], []]

    def dst(l, r, v):
        r = r - H
        one = -0.5 * (u[l, r] - v + jnp.where(level[r] == l, hg[r], 0.0))
        g1[l, r] = one
        zero, first = g0[l, r], own_g[l, r]
        for k, term in enumerate((first * first, zero * zero, zero * one, one * one)):
            sums[k].append(term)
            if len(sums[k]) == 5:
                sums[k] = [total(sums[k])]

    adjoint(lambda l, r: ahead[l, r], lambda k, r: coef(k, r + H), c, W, (a, b), dst)
    lane = lax.broadcasted_iota(jnp.int32, (1, TILE), 1)
    row = jnp.zeros((1, TILE), jnp.float32)
    for k in range(4):
        s = jnp.sum(total(sums[k]))
        row = jnp.where(lane == k, s, row)
    for i in range(part.shape[0]):
        part[i] = row


def again_kernel(parts, out):
    s = total([parts[i] for i in range(parts.shape[0])])
    for i in range(out.shape[0]):
        out[i] = s


def last_kernel(count, parts, var, own, g, g0, g1, d, u, o1, hg, state, multipliers, obs):
    row = total([parts[i] for i in range(parts.shape[0])])
    lane = lax.broadcasted_iota(jnp.int32, (1, TILE), 1)
    sg, s00, s01, s11 = [
        jnp.broadcast_to(jnp.sum(jnp.where(lane == k, row, 0.0), axis=1, keepdims=True), ROW) / count
        for k in range(4)
    ]
    first = 0.3 / jnp.sqrt(sg + 1e-06)
    mean = jnp.maximum(s00 + first * (2.0 * s01 + first * s11), 0.0)
    second = 0.3 / jnp.sqrt(mean + 1e-06)
    for l in range(L):
        keep = 2.0 - 0.5 * var[l]
        join_into(
            state,
            (l,),
            [
                own[l, r] - first * g[l, r] - second * (g0[l, r] + first * g1[l, r])
                for r in range(ROWS)
            ],
        )
        join_into(multipliers, (l,), [keep * d[l, r] - (0.5 * first) * u[l, r] for r in range(ROWS)])
    join_into(obs, (), [1.5 * o1[r] - (0.5 * first) * hg[r] for r in range(ROWS)])


VM = pl.BlockSpec(memory_space=pltpu.VMEM)
SM = pl.BlockSpec(memory_space=pltpu.SMEM)


def call(kernel, outs, smem=0, scratch=(), us=1.0):
    def run(*args):
        n = sum(a.size for a in args)
        return pl.pallas_call(
            kernel,
            out_shape=[jax.ShapeDtypeStruct(s, jnp.float32) for s in outs],
            in_specs=[SM] * smem + [VM] * (len(args) - smem),
            out_specs=[VM] * len(outs),
            scratch_shapes=[pltpu.VMEM(s, jnp.float32) for s in scratch],
            compiler_params=pltpu.CompilerParams(vmem_limit_bytes=16 * 2**20),
            cost_estimate=pl.CostEstimate(flops=int(us * 4e6), bytes_accessed=4 * n, transcendentals=0),
        )(*args)

    return run


def rows_of(k, n):
    return (k, n, *ROW)


def shifted(x, axis, by):
    count = lax.axis_size(axis)
    return lax.ppermute(x, axis, [(i, i + by) for i in range(count) if 0 <= i + by < count])


def exchanged(x, axis):
    return lax.all_to_all(x, axis, 0, 0, tiled=True)


def on_device(
    x_init, background, observed, diff_lon, diff_lat, drift, coupling, model_var, obs_level, huber_class
):
    count = float(
        L * ROWS * 8 * TILE * lax.axis_size(TM) * lax.axis_size("lat")
    )
    two = [rows_of(L, 3 * ROWS)] * 2
    two_w = [rows_of(L, W)] * 2
    (own,) = call(pack_kernel, [rows_of(L + 3, ROWS)])(x_init[0], diff_lon[0], diff_lat[0], drift[0])
    up, down = shifted(own, "lat", 1), shifted(own, "lat", -1)
    bg, obs = call(aside_kernel, [rows_of(L, ROWS), (ROWS, *ROW)])(background, observed[0])
    level = jnp.broadcast_to(obs_level[0][..., None], (ROWS, *ROW))
    classes = huber_class[0]
    weight = 1.0 * (classes == 0) + 0.5 * (classes == 1) + 0.25 * (classes == 2)
    weight = jnp.broadcast_to(weight.astype(jnp.float32)[..., None], (ROWS, *ROW))

    wide, wide_x = call(middle_kernel, [rows_of(L + 3, W), rows_of(L, W)])(up, own, down)
    before, after = shifted(wide, TM, 1), shifted(wide_x, TM, -1)
    (moved,) = call(forward_kernel, [rows_of(L, W)], 1, two, 2.0)(
        coupling, up, own, down, up, own, down
    )
    g, d, ahead, o1 = call(
        gradient_kernel,
        [rows_of(L, ROWS), rows_of(L, ROWS), rows_of(L, W), (ROWS, *ROW)],
        1,
        two_w,
        3.0,
    )(coupling, before, after, moved, up, own, down, bg, obs, level, weight)

    up_g, down_g = shifted(g, "lat", 1), shifted(g, "lat", -1)
    (g0,) = call(still_kernel, [rows_of(L, ROWS)], 2, two_w, 2.0)(
        coupling, model_var, d, ahead, own, up, down, level, o1
    )
    (wide_g,) = call(middle_g_kernel, [rows_of(L, W)])(up_g, g, down_g)
    before_g, after_g = shifted(wide_g, TM, 1), shifted(wide_g, TM, -1)
    (moved_g,) = call(forward_kernel, [rows_of(L, W)], 1, two, 2.0)(
        coupling, up_g, g, down_g, up, own, down
    )
    u, g1, hg, part = call(
        curvature_kernel,
        [rows_of(L, ROWS), rows_of(L, ROWS), (ROWS, *ROW), (lax.axis_size(NEAR), 1, TILE)],
        1,
        [rows_of(L, W)] + two_w,
        3.0,
    )(coupling, before, before_g, after_g, moved_g, up, own, down, g, level, weight, g0)
    (part,) = call(again_kernel, [(lax.axis_size(FAR), 1, TILE)])(exchanged(part, NEAR))
    part = exchanged(part, FAR)

    natural = (L, ROWS, 8 * TILE)

    def finish(var, part, *refs):
        last_kernel(count, part, var, *refs)

    state, multipliers, obs_multipliers = call(finish, [natural, natural, natural[1:]], 1)(
        model_var, part, own, g, g0, g1, d, u, o1, hg
    )
    return (state[None], multipliers[None], obs_multipliers[None])


def solution(mesh):
    torus = Mesh(mesh.devices.reshape(4, 8, 2, mesh.shape["lat"]), (*TM, "lat"))
    band = P(TM, "lat", None)
    in_specs = (
        P(TM, None, "lat", None),
        P(None, "lat", None),
        band,
        band,
        band,
        band,
        P(),
        P(),
        band,
        band,
    )
    out_specs = (P(TM, None, "lat", None), P(TM, None, "lat", None), band)
    return jax.shard_map(
        on_device, mesh=torus, in_specs=in_specs, out_specs=out_specs, check_vma=False
    )
```

time: 178 us -> 96.4 us (0.54)
  waiting for transfers between devices: 45.5 us -> 7.34 us
  starting transfers between devices: 48.7 us -> 28.9 us
  matrix products: 15.6 us -> 0 us
  Pallas kernels: 0 us -> 11 us
  other arithmetic: 8.45 us -> 0.01 us
  local copies, waits for them, and re-layouts: 13.2 us -> 5.93 us
  between operations: 2.72 us -> 0.8 us
    ppermute x14 -> x8, waiting for transfers between devices: 38.4 us -> 7.34 us  [shifted(): lax.ppermute(x, axis, [(i, i + by) for i in range(count) if 0 <= i + by <...]
    dot_general x16 -> x0, matrix products: 15.6 us -> none  [the longest x8 9.06 us: adjoint_local(): jnp.einsum('lm,lrc->mrc', coupling, w, precision=lax.Precision.HIGHEST)]
    ppermute x14 -> x8, starting transfers between devices: 41.4 us -> 28.9 us  [shifted(): lax.ppermute(x, axis, [(i, i + by) for i in range(count) if 0 <= i + by <...]
    pallas_call x0 -> x11, Pallas kernels: none -> 11 us  [run(): pl.pallas_call(kernel, out_shape=[jax.ShapeDtypeStruct(s, jnp.float32) fo...]
    all_to_all x1 -> x0, starting transfers between devices: 7.32 us -> none  [from_everyone(): lax.all_to_all(jnp.broadcast_to(x[None], (count, *x.shape)), axis, 0, 0,...]
    slice x57 -> x0, local copies, waits for them, and re-layouts: 7.21 us -> none  [the longest x16 2.48 us: adjoint_local(): adv_part = 0.5 * (jnp.roll(u_term, 1, 2) - jnp.roll(u_term, -1, 2))]
    all_to_all x1 -> x0, waiting for transfers between devices: 7.1 us -> none  [from_everyone(): lax.all_to_all(jnp.broadcast_to(x[None], (count, *x.shape)), axis, 0, 0,...]
    reduce_sum x8 -> x0, other arithmetic: 4.87 us -> none  [the longest x4 2.5 us: of_everyone(): return from_everyone(x, axis).sum(axis=0)]
  transfers between devices with their start and end apart: 15 -> 8, of which waited for: 13 -> 6; matrix products, arithmetic and copies ran while one was open for 1% -> 0% of each run, Pallas kernels for 0% -> 5%
where the time goes in v1:
time: 96.4 us; the launch traced here: 95.7 us
  blocking collectives  41.7 us (43%)
  starting transfers between devices  28.9 us (30%)
  Pallas kernels  11 us (11%)
  waiting for transfers between devices  7.34 us (8%)
  local copies, waits for them, and re-layouts  5.93 us (6%)
    all_to_all x2, blocking collectives, exchanged(): return lax.all_to_all(x, axis, 0, 0, tiled=True)  41.7 us
    ppermute x8, starting transfers between devices, shifted(): lax.ppermute(x, axis, [(i, i + by) for i in range(count) if 0 <= i + by <...  28.9 us
    pallas_call x11, Pallas kernels, run(): pl.pallas_call(kernel, out_shape=[jax.ShapeDtypeStruct(s, jnp.float32) fo...  11 us
    ppermute x8, waiting for transfers between devices, shifted(): lax.ppermute(x, axis, [(i, i + by) for i in range(count) if 0 <= i + by <...  7.34 us
    unnamed x20, local copies, waits for them, and re-layouts  5.78 us
  transfers between devices with their start and end apart: 8, of which 6 were waited for; matrix products, arithmetic and copies ran while one was open for 0% of the time, Pallas kernels for 5%

profile of v1, /device:TPU:1, one launch (start us, length us, event | category | flops | bytes accessed | tf_op | source)
XLA Modules:
  0.0 95.7 jit_solution(16031852643476949037)
XLA Ops:
  0.6 0.0 copy-start
  0.6 0.9 copy-done
  1.5 0.0 copy-start.3
  1.6 0.8 copy-done.3
  2.3 0.0 copy-start.4
  2.3 0.8 copy-done.4
  3.1 0.0 copy-start.5
  3.1 0.8 copy-done.5
  3.9 0.0 copy-start.1
  3.9 0.0 copy-start.6
  3.9 1.4 %collective-permute-start.1 = (f32[8,8,8,128]{3,2,1,0:T(8,128)S(1)}, f32[8,8,8,128]{3,2,1,0:T(8,128)S(1)}, u32[]{:S(2)}, u32[]{:S(2)}) collective-permute-start(f32[8,8,8,128]{3,2,1,0:T(8,128)S(1)} %shard_map.121.own.own_c.refs_0_), channel_id=1, source_target_pairs={{1,0},{2,1},{3,2},{4,3},{5,4},{6,5},{7,6},{9,8},{10,9},{11,10},{12... | collective-permute-start | bytes 786440 | tf_op jit(solution)/shard_map/ppermute | solution.py:332
  5.3 5.5 %collective-permute-start = (f32[8,8,8,128]{3,2,1,0:T(8,128)S(1)}, f32[8,8,8,128]{3,2,1,0:T(8,128)S(1)}, u32[]{:S(2)}, u32[]{:S(2)}) collective-permute-start(f32[8,8,8,128]{3,2,1,0:T(8,128)S(1)} %shard_map.121.own.own_c.refs_0_), channel_id=1, source_target_pairs={{0,1},{1,2},{2,3},{3,4},{4,5},{5,6},{6,7},{8,9},{9,10},{10,11},{11... | collective-permute-start | bytes 786440 | tf_op jit(solution)/shard_map/ppermute | solution.py:332
  10.8 1.8 %collective-permute-done.1.down.down_c = f32[8,8,8,128]{3,2,1,0:T(8,128)S(1)} collective-permute-done((f32[8,8,8,128]{3,2,1,0:T(8,128)S(1)}, f32[8,8,8,128]{3,2,1,0:T(8,128)S(1)}, u32[]{:S(2)}, u32[]{:S(2)}) %collective-permute-start.1) | collective-permute-done | bytes 262176 | tf_op jit(solution)/shard_map/ppermute | solution.py:332
  12.6 1.5 %collective-permute-done.up.up_c = f32[8,8,8,128]{3,2,1,0:T(8,128)S(1)} collective-permute-done((f32[8,8,8,128]{3,2,1,0:T(8,128)S(1)}, f32[8,8,8,128]{3,2,1,0:T(8,128)S(1)}, u32[]{:S(2)}, u32[]{:S(2)}) %collective-permute-start) | collective-permute-done | bytes 262176 | tf_op jit(solution)/shard_map/ppermute | solution.py:332
  14.1 0.1 shard_map.122
  14.2 6.3 %collective-permute-start.2 = (f32[8,16,8,128]{3,2,1,0:T(8,128)S(1)}, f32[8,16,8,128]{3,2,1,0:T(8,128)S(1)}, u32[]{:S(2)}, u32[]{:S(2)}) collective-permute-start(f32[8,16,8,128]{3,2,1,0:T(8,128)S(1)} %get-tuple-element.18), channel_id=1, source_target_pairs={{0,8},{8,16},{16,24},{24,32},{32,40},{40,48},{48,56},{56,64},{64,7... | collective-permute-start | bytes 1572872 | tf_op jit(solution)/shard_map/ppermute | solution.py:332
  20.5 3.5 %collective-permute-start.3 = (f32[5,16,8,128]{3,2,1,0:T(8,128)S(1)}, f32[5,16,8,128]{3,2,1,0:T(8,128)S(1)}, u32[]{:S(2)}, u32[]{:S(2)}) collective-permute-start(f32[5,16,8,128]{3,2,1,0:T(8,128)S(1)} %get-tuple-element.19), channel_id=1, source_target_pairs={{8,0},{16,8},{24,16},{32,24},{40,32},{48,40},{56,48},{64,56},{72,6... | collective-permute-start | bytes 983048 | tf_op jit(solution)/shard_map/ppermute | solution.py:332
  23.9 0.0 copy-done.1
  24.0 0.0 copy-done.6
  24.0 0.0 copy-start.9
  24.0 0.6 copy-done.9
  24.7 0.0 copy-start.2
  24.7 0.7 copy-done.2
  25.3 1.8 %shard_map.123.moved = f32[5,16,8,128]{3,2,1,0:T(8,128)S(1)} custom-call(f32[5,5]{1,0:T(8,128)S(1)} %copy-done.2, f32[8,8,8,128]{3,2,1,0:T(8,128)S(1)} %collective-permute-done.up.up_c, f32[8,8,8,128]{3,2,1,0:T(8,128)S(1)} %shard_map.121.own.own_c.refs_0_, f32[8,8,8,128]{3,2,1,0:T(8,128)S(1)} %collective-permute-done.1.down.down_c, ...), custom_call_target="tpu_custom_call" | custom-call | flops 8000000 | bytes 1572964 | tf_op jit(solution)/shard_map/pallas_call | solution.py:313
  27.2 1.7 %collective-permute-done.3.after = f32[5,16,8,128]{3,2,1,0:T(8,128)S(1)} collective-permute-done((f32[5,16,8,128]{3,2,1,0:T(8,128)S(1)}, f32[5,16,8,128]{3,2,1,0:T(8,128)S(1)}, u32[]{:S(2)}, u32[]{:S(2)}) %collective-permute-start.3) | collective-permute-done | bytes 327712 | tf_op jit(solution)/shard_map/ppermute | solution.py:332
  28.8 0.0 collective-permute-done.2.before.coefs
  28.8 0.0 copy-start.8
  28.9 0.1 broadcast_in_dim.24.weight
  28.9 0.6 copy-done.8
  29.5 0.1 broadcast_in_dim.23.level
  29.6 2.1 %shard_map.125 = (f32[5,8,8,128]{3,2,1,0:T(8,128)S(1)}, f32[5,8,8,128]{3,2,1,0:T(8,128)S(1)}, f32[5,16,8,128]{3,2,1,0:T(8,128)S(1)}, f32[8,8,128]{2,1,0:T(8,128)S(1)}) custom-call(f32[5,5]{1,0:T(8,128)S(1)} %copy-done.2, f32[8,16,8,128]{3,2,1,0:T(8,128)S(1)} %collective-permute-done.2.before.coefs, f32[5,16,8,128]{3,2,1,0:T(8,128)S(1)} %collective-permute-done.3.after, ...), custom_call_target="tpu_custom_call" | custom-call | flops 12000000 | bytes 2228324 | tf_op jit(solution)/shard_map/pallas_call | solution.py:313
  31.7 1.3 %collective-permute-start.5 = (f32[5,8,8,128]{3,2,1,0:T(8,128)S(1)}, f32[5,8,8,128]{3,2,1,0:T(8,128)S(1)}, u32[]{:S(2)}, u32[]{:S(2)}) collective-permute-start(f32[5,8,8,128]{3,2,1,0:T(8,128)S(1)} %get-tuple-element.22.own.own_g.refs_1_), channel_id=1, source_target_pairs={{1,0},{2,1},{3,2},{4,3},{5,4},{6,5},{7,6},{9,8},{10,9},{11,10},{12... | collective-permute-start | bytes 491528 | tf_op jit(solution)/shard_map/ppermute | solution.py:332
  33.0 4.7 %collective-permute-start.4 = (f32[5,8,8,128]{3,2,1,0:T(8,128)S(1)}, f32[5,8,8,128]{3,2,1,0:T(8,128)S(1)}, u32[]{:S(2)}, u32[]{:S(2)}) collective-permute-start(f32[5,8,8,128]{3,2,1,0:T(8,128)S(1)} %get-tuple-element.22.own.own_g.refs_1_), channel_id=1, source_target_pairs={{0,1},{1,2},{2,3},{3,4},{4,5},{5,6},{6,7},{8,9},{9,10},{10,11},{11... | collective-permute-start | bytes 491528 | tf_op jit(solution)/shard_map/ppermute | solution.py:332
  37.8 0.8 collective-permute-done.5.down
  38.5 1.5 %collective-permute-done.4.up = f32[5,8,8,128]{3,2,1,0:T(8,128)S(1)} collective-permute-done((f32[5,8,8,128]{3,2,1,0:T(8,128)S(1)}, f32[5,8,8,128]{3,2,1,0:T(8,128)S(1)}, u32[]{:S(2)}, u32[]{:S(2)}) %collective-permute-start.4) | collective-permute-done | bytes 163872 | tf_op jit(solution)/shard_map/ppermute | solution.py:332
  40.0 1.9 %collective-permute-start.7 = (f32[5,16,8,128]{3,2,1,0:T(8,128)S(1)}, f32[5,16,8,128]{3,2,1,0:T(8,128)S(1)}, u32[]{:S(2)}, u32[]{:S(2)}) collective-permute-start(f32[5,16,8,128]{3,2,1,0:T(8,128)S(1)} %shard_map.126), channel_id=1, source_target_pairs={{8,0},{16,8},{24,16},{32,24},{40,32},{48,40},{56,48},{64,56},{72,6... | collective-permute-start | bytes 983048 | tf_op jit(solution)/shard_map/ppermute | solution.py:332
  41.9 4.2 %collective-permute-start.6 = (f32[5,16,8,128]{3,2,1,0:T(8,128)S(1)}, f32[5,16,8,128]{3,2,1,0:T(8,128)S(1)}, u32[]{:S(2)}, u32[]{:S(2)}) collective-permute-start(f32[5,16,8,128]{3,2,1,0:T(8,128)S(1)} %shard_map.126), channel_id=1, source_target_pairs={{0,8},{8,16},{16,24},{24,32},{32,40},{40,48},{48,56},{56,64},{64,7... | collective-permute-start | bytes 983048 | tf_op jit(solution)/shard_map/ppermute | solution.py:332
  46.2 0.0 copy-start.7
  46.2 0.6 copy-done.7
  46.8 1.4 %shard_map.128.g0.refs_2_ = f32[5,8,8,128]{3,2,1,0:T(8,128)S(1)} custom-call(f32[5,5]{1,0:T(8,128)S(1)} %copy-done.2, f32[5]{0:T(128)S(1)} %copy-done.7, f32[5,8,8,128]{3,2,1,0:T(8,128)S(1)} %get-tuple-element.23.d.refs_4_, f32[5,16,8,128]{3,2,1,0:T(8,128)S(1)} %get-tuple-element.24.ahead, f32[8,8,8,128]{3,2,1,0:T(8,128)S(1)} %shard_map.121.own.own_c.refs_0_, ...), custom_call_target="tpu_custom_call" | custom-call | flops 8000000 | bytes 1343608 | tf_op jit(solution)/shard_map/pallas_call | solution.py:313
  48.2 1.8 %shard_map.127.moved = f32[5,16,8,128]{3,2,1,0:T(8,128)S(1)} custom-call(f32[5,5]{1,0:T(8,128)S(1)} %copy-done.2, f32[5,8,8,128]{3,2,1,0:T(8,128)S(1)} %collective-permute-done.4.up, f32[5,8,8,128]{3,2,1,0:T(8,128)S(1)} %get-tuple-element.22.own.own_g.refs_1_, f32[5,8,8,128]{3,2,1,0:T(8,128)S(1)} %collective-permute-done.5.down, ...), custom_call_target="tpu_custom_call" | custom-call | flops 8000000 | bytes 1278052 | tf_op jit(solution)/shard_map/pallas_call | solution.py:313
  50.0 0.0 collective-permute-done.7.after
  50.0 0.1 collective-permute-done.6.before
  50.2 2.3 %shard_map.129 = (f32[5,8,8,128]{3,2,1,0:T(8,128)S(1)}, f32[5,8,8,128]{3,2,1,0:T(8,128)S(1)}, f32[8,8,128]{2,1,0:T(8,128)S(1)}, f32[16,1,128]{2,1,0:T(1,128)S(1)}) custom-call(f32[5,5]{1,0:T(8,128)S(1)} %copy-done.2, f32[8,16,8,128]{3,2,1,0:T(8,128)S(1)} %collective-permute-done.2.before.coefs, f32[5,16,8,128]{3,2,1,0:T(8,128)S(1)} %collective-permute-done.6.before, ...), custom_call_target="tpu_custom_call" | custom-call | flops 12000000 | bytes 2687076 | tf_op jit(solution)/shard_map/pallas_call | solution.py:313
  52.4 19.7 %all_to_all.10.parts = f32[16,1,128]{2,1,0:T(1,128)S(1)} all-to-all(f32[16,1,128]{2,1,0:T(1,128)S(1)} %get-tuple-element.26), channel_id=1, replica_groups=mesh['tm_0'=4,'tm_1'=8,'tm_2'=2,'lat'=8] {'tm_2','lat'}, dimensions={0} | all-to-all | bytes 16384 | tf_op jit(solution)/shard_map/all_to_all | solution.py:336
  72.2 22.0 %all_to_all.11.part = f32[32,1,128]{2,1,0:T(1,128)S(1)} all-to-all(f32[32,1,128]{2,1,0:T(1,128)S(1)} %shard_map.130), channel_id=1, replica_groups=mesh['tm_0'=4,'tm_1'=8,'tm_2'=2,'lat'=8] {'tm_0','tm_1'}, dimensions={0} | all-to-all | bytes 32768 | tf_op jit(solution)/shard_map/all_to_all | solution.py:336
  94.2 1.4 %shard_map.131 = (f32[5,8,1024]{2,1,0:T(8,128)}, f32[5,8,1024]{2,1,0:T(8,128)}, f32[8,1024]{1,0:T(8,128)}) custom-call(f32[5]{0:T(128)S(1)} %copy-done.7, f32[32,1,128]{2,1,0:T(1,128)S(1)} %all_to_all.11.part, f32[8,8,8,128]{3,2,1,0:T(8,128)S(1)} %shard_map.121.own.own_c.refs_0_, f32[5,8,8,128]{3,2,1,0:T(8,128)S(1)} %get-tuple-element.22.own.own_g.refs_1_, ...), custom_call_target="tpu_custom_call" | custom-call | flops 4000000 | bytes 1163284 | tf_op jit(solution)/shard_map/pallas_call | solution.py:313
  (5 shorter events, 0.1 us)
Async XLA Ops:
  0.6 0.9 copy-start
  1.5 0.8 copy-start.3
  2.3 0.8 copy-start.4
  3.1 0.8 copy-start.5
  3.9 20.1 %copy-start.1 = (f32[5,8,1024]{2,1,0:T(8,128)S(1)}, f32[5,8,1024]{2,1,0:T(8,128)}, u32[]{:S(2)}) copy-start(f32[5,8,1024]{2,1,0:T(8,128)} %background.1) | copy-start | bytes 491524
  3.9 20.1 %copy-start.6 = (f32[1,8,1024]{2,1,0:T(8,128)S(1)}, f32[1,8,1024]{2,1,0:T(8,128)}, u32[]{:S(2)}) copy-start(f32[1,8,1024]{2,1,0:T(8,128)} %param.12) | copy-start | bytes 98308
  3.9 8.7 %collective-permute-start.1 = (f32[8,8,8,128]{3,2,1,0:T(8,128)S(1)}, f32[8,8,8,128]{3,2,1,0:T(8,128)S(1)}, u32[]{:S(2)}, u32[]{:S(2)}) collective-permute-start(f32[8,8,8,128]{3,2,1,0:T(8,128)S(1)} %shard_map.121.own.own_c.refs_0_), channel_id=1, source_target_pairs={{1,0},{2,1},{3,2},{4,3},{5,4},{6,5},{7,6},{9,8},{10,9},{11,10},{12... | collective-permute-start | bytes 786440 | tf_op jit(solution)/shard_map/ppermute | solution.py:332
  5.3 8.8 %collective-permute-start = (f32[8,8,8,128]{3,2,1,0:T(8,128)S(1)}, f32[8,8,8,128]{3,2,1,0:T(8,128)S(1)}, u32[]{:S(2)}, u32[]{:S(2)}) collective-permute-start(f32[8,8,8,128]{3,2,1,0:T(8,128)S(1)} %shard_map.121.own.own_c.refs_0_), channel_id=1, source_target_pairs={{0,1},{1,2},{2,3},{3,4},{4,5},{5,6},{6,7},{8,9},{9,10},{10,11},{11... | collective-permute-start | bytes 786440 | tf_op jit(solution)/shard_map/ppermute | solution.py:332
  14.2 14.7 %collective-permute-start.2 = (f32[8,16,8,128]{3,2,1,0:T(8,128)S(1)}, f32[8,16,8,128]{3,2,1,0:T(8,128)S(1)}, u32[]{:S(2)}, u32[]{:S(2)}) collective-permute-start(f32[8,16,8,128]{3,2,1,0:T(8,128)S(1)} %get-tuple-element.18), channel_id=1, source_target_pairs={{0,8},{8,16},{16,24},{24,32},{32,40},{40,48},{48,56},{56,64},{64,7... | collective-permute-start | bytes 1572872 | tf_op jit(solution)/shard_map/ppermute | solution.py:332
  20.5 8.4 %collective-permute-start.3 = (f32[5,16,8,128]{3,2,1,0:T(8,128)S(1)}, f32[5,16,8,128]{3,2,1,0:T(8,128)S(1)}, u32[]{:S(2)}, u32[]{:S(2)}) collective-permute-start(f32[5,16,8,128]{3,2,1,0:T(8,128)S(1)} %get-tuple-element.19), channel_id=1, source_target_pairs={{8,0},{16,8},{24,16},{32,24},{40,32},{48,40},{56,48},{64,56},{72,6... | collective-permute-start | bytes 983048 | tf_op jit(solution)/shard_map/ppermute | solution.py:332
  24.0 0.7 copy-start.9
  24.7 0.7 copy-start.2
  28.8 0.7 copy-start.8
  31.7 6.8 %collective-permute-start.5 = (f32[5,8,8,128]{3,2,1,0:T(8,128)S(1)}, f32[5,8,8,128]{3,2,1,0:T(8,128)S(1)}, u32[]{:S(2)}, u32[]{:S(2)}) collective-permute-start(f32[5,8,8,128]{3,2,1,0:T(8,128)S(1)} %get-tuple-element.22.own.own_g.refs_1_), channel_id=1, source_target_pairs={{1,0},{2,1},{3,2},{4,3},{5,4},{6,5},{7,6},{9,8},{10,9},{11,10},{12... | collective-permute-start | bytes 491528 | tf_op jit(solution)/shard_map/ppermute | solution.py:332
  33.0 7.0 %collective-permute-start.4 = (f32[5,8,8,128]{3,2,1,0:T(8,128)S(1)}, f32[5,8,8,128]{3,2,1,0:T(8,128)S(1)}, u32[]{:S(2)}, u32[]{:S(2)}) collective-permute-start(f32[5,8,8,128]{3,2,1,0:T(8,128)S(1)} %get-tuple-element.22.own.own_g.refs_1_), channel_id=1, source_target_pairs={{0,1},{1,2},{2,3},{3,4},{4,5},{5,6},{6,7},{8,9},{9,10},{10,11},{11... | collective-permute-start | bytes 491528 | tf_op jit(solution)/shard_map/ppermute | solution.py:332
  40.0 10.0 %collective-permute-start.7 = (f32[5,16,8,128]{3,2,1,0:T(8,128)S(1)}, f32[5,16,8,128]{3,2,1,0:T(8,128)S(1)}, u32[]{:S(2)}, u32[]{:S(2)}) collective-permute-start(f32[5,16,8,128]{3,2,1,0:T(8,128)S(1)} %shard_map.126), channel_id=1, source_target_pairs={{8,0},{16,8},{24,16},{32,24},{40,32},{48,40},{56,48},{64,56},{72,6... | collective-permute-start | bytes 983048 | tf_op jit(solution)/shard_map/ppermute | solution.py:332
  41.9 8.2 %collective-permute-start.6 = (f32[5,16,8,128]{3,2,1,0:T(8,128)S(1)}, f32[5,16,8,128]{3,2,1,0:T(8,128)S(1)}, u32[]{:S(2)}, u32[]{:S(2)}) collective-permute-start(f32[5,16,8,128]{3,2,1,0:T(8,128)S(1)} %shard_map.126), channel_id=1, source_target_pairs={{0,8},{8,16},{16,24},{24,32},{32,40},{40,48},{48,56},{56,64},{64,7... | collective-permute-start | bytes 983048 | tf_op jit(solution)/shard_map/ppermute | solution.py:332
  46.2 0.7 copy-start.7

commit v2 on v1

v2 whole, which is shorter than its diff:
```python
import jax
import jax.numpy as jnp
from jax import lax
from jax.experimental import pallas as pl
from jax.experimental.pallas import tpu as pltpu
from jax.sharding import Mesh
from jax.sharding import PartitionSpec as P

L = 5
TILE = 128
STEPS = 4
ROWS = 8
H = STEPS
W = ROWS + 2 * H
TM = ("tm_0", "tm_1", "tm_2")
FAR = ("tm_0", "tm_1")
NEAR = ("tm_2", "lat")
ROW = (8, TILE)


def lanes():
    return lax.broadcasted_iota(jnp.int32, ROW, 1)


class Shift:
    def __init__(self):
        lane = lanes()
        self.first = lane == 0
        self.last = lane == TILE - 1

    def east(self, v):
        r = pltpu.roll(v, TILE - 1, 1)
        return jnp.where(self.last, pltpu.roll(r, 7, 0), r)

    def west(self, v):
        r = pltpu.roll(v, 1, 1)
        return jnp.where(self.first, pltpu.roll(r, 1, 0), r)


def total(terms):
    while len(terms) > 1:
        terms = [a + b for a, b in zip(terms[::2], terms[1::2])] + (
            [terms[-1]] if len(terms) % 2 else []
        )
    return terms[0]


def centre(ce, cw, ky):
    return (1.0 - (ce + cw)) - 2.0 * ky


def forward(src, coef, c, rows, bufs, dst):
    sh = Shift()
    for step in range(STEPS):
        lo, hi = step + 1, rows - step - 1

        def get(r, step=step):
            if step == 0:
                return [src(l, r) for l in range(L)]
            return [bufs[(step - 1) % 2][l, r] for l in range(L)]

        above, here = get(lo - 1), get(lo)
        for r in range(lo, hi):
            below = get(r + 1)
            ce, cw, ky = coef(0, r), coef(1, r), coef(2, r)
            c0 = centre(ce, cw, ky)
            for l in range(L):
                v = here[l]
                terms = [
                    ce * sh.east(v),
                    cw * sh.west(v),
                    ky * (above[l] + below[l]),
                    c0 * v,
                ] + [c[L * l + m] * here[m] for m in range(L)]
                out = total(terms)
                if step == STEPS - 1:
                    dst(l, r, out)
                else:
                    bufs[step % 2][l, r] = out
            above, here = here, below


def adjoint(src, coef, c, rows, bufs, dst):
    sh = Shift()
    for step in range(STEPS):
        lo, hi = step + 1, rows - step - 1

        def get(r, step=step):
            if step == 0:
                v = [src(l, r) for l in range(L)]
            else:
                v = [bufs[(step - 1) % 2][l, r] for l in range(L)]
            ky = coef(2, r)
            return v, [ky * w for w in v]

        (_, above), (here, q) = get(lo - 1), get(lo)
        for r in range(lo, hi):
            after, below = get(r + 1)
            ce, cw, ky = coef(0, r), coef(1, r), coef(2, r)
            c0 = centre(ce, cw, ky)
            for l in range(L):
                w = here[l]
                terms = [
                    sh.west(ce * w),
                    sh.east(cw * w),
                    above[l] + below[l],
                    c0 * w,
                ] + [c[L * m + l] * here[m] for m in range(L)]
                out = total(terms)
                if step == STEPS - 1:
                    dst(l, r, out)
                else:
                    bufs[step % 2][l, r] = out
            above, here, q = q, after, below


def banded(up, own, down, first):
    def at(k, r):
        part = (up, own, down)[r // ROWS]
        return part[first + k, r % ROWS]

    return at


def place():
    j, n = 0, 1
    for axis in TM:
        j = j * lax.axis_size(axis) + lax.axis_index(axis)
        n = n * lax.axis_size(axis)
    return jnp.where(j == n - 1, 0.0, 1.0), jnp.where(j == 0, 1.0, 0.0)


def split(v):
    return jnp.swapaxes(jnp.stack([v[:, s * TILE : (s + 1) * TILE] for s in range(8)]), 0, 1)


def join_into(ref, index, rows):
    v = jnp.swapaxes(jnp.stack(rows), 0, 1)
    for s in range(8):
        ref[(*index, slice(None), slice(s * TILE, (s + 1) * TILE))] = v[s]


def pack_kernel(x_far, kx_far, ky_far, ux_far, out, x, k3, sems):
    copies = [
        pltpu.make_async_copy(x_far.at[0], x, sems.at[0]),
        pltpu.make_async_copy(kx_far, k3.at[pl.ds(0, 1)], sems.at[1]),
        pltpu.make_async_copy(ky_far, k3.at[pl.ds(1, 1)], sems.at[2]),
        pltpu.make_async_copy(ux_far, k3.at[pl.ds(2, 1)], sems.at[3]),
    ]
    for copy in copies:
        copy.start()
    for copy in copies[1:]:
        copy.wait()
    k, u = k3[0], 0.5 * k3[2]
    out[L] = split(k + u)
    out[L + 1] = split(k - u)
    out[L + 2] = split(k3[1])
    copies[0].wait()
    for l in range(L):
        out[l] = split(x[l])


def tiles(v):
    return jnp.swapaxes(jnp.stack([jnp.broadcast_to(v[:, s : s + 1], ROW) for s in range(8)]), 0, 1)


def aside_kernel(
    background, observed, coupling, var, obs_level, huber_class, bg, obs, c, keep, level, weight
):
    level[...] = tiles(obs_level[0].astype(jnp.float32))
    h = huber_class[0]
    weight[...] = tiles(jnp.where(h == 0, 1.0, 0.0) + jnp.where(h == 1, 0.5, 0.0) + jnp.where(h == 2, 0.25, 0.0))
    for l in range(L):
        bg[l] = split(background[l])
        keep[l] = jnp.broadcast_to(2.0 - 0.5 * var[:, l : l + 1], ROW)
        for m in range(L):
            c[L * l + m] = jnp.broadcast_to(coupling[l : l + 1, m : m + 1], ROW)
    obs[...] = split(observed[0])


def middle_kernel(up, own, down, out):
    for k in range(L):
        out[k, :H] = up[k, H:]
        out[k, H : H + ROWS] = own[k]
        out[k, H + ROWS :] = down[k, :H]


def forward_kernel(c, up, own, down, up_c, own_c, down_c, out, out_own, a, b):
    def dst(l, r, v):
        out[l, r - H] = v
        if ROWS <= r < 2 * ROWS:
            out_own[l, r - ROWS] = v

    forward(banded(up, own, down, 0), banded(up_c, own_c, down_c, L), c, 3 * ROWS, (a, b), dst)


def picked(level, values):
    out = jnp.where(level == 0, values[0], 0.0)
    for l in range(1, L):
        out = jnp.where(level == float(l), values[l], out)
    return out


def back_kernel(c, after, moved, up, own, down, obs, level, weight, ahead, o1, p, a, b):
    half = 0.5 * place()[0]
    for l in range(L):
        for r in range(W):
            ahead[l, r] = half * (after[l, r] - moved[l, r])
    for r in range(ROWS):
        o1[r] = 0.5 * weight[r] * (picked(level[r], [own[l, r] for l in range(L)]) - obs[r])
    coef = banded(up, own, down, L)

    def dst(l, r, v):
        r = r - H
        p[l, r] = jnp.where(level[r] == float(l), o1[r], 0.0) - v

    adjoint(lambda l, r: ahead[l, r], lambda k, r: coef(k, r + H), c, W, (a, b), dst)


def gradient_kernel(came, own, bg, p, d, g):
    first = place()[1]
    for l in range(L):
        for r in range(ROWS):
            v = 0.5 * (own[l, r] - (came[l, r] + first * bg[l, r]))
            d[l, r] = v
            g[l, r] = v + p[l, r]


def still_kernel(c, keep, d, ahead, up, own, down, level, o1, g0, a, b):
    coef = banded(up, own, down, L)

    def dst(l, r, v):
        r = r - H
        g0[l, r] = keep[l] * d[l, r] - v + jnp.where(level[r] == float(l), 1.5 * o1[r], 0.0)

    adjoint(lambda l, r: keep[l] * ahead[l, r], lambda k, r: coef(k, r + H), c, W, (a, b), dst)


def back_g_kernel(c, after, moved, up, own, down, g, level, weight, g0, hg, p, sums, ahead, a, b):
    some = place()[0]
    for l in range(L):
        for r in range(W):
            ahead[l, r] = some * (after[l, r] - moved[l, r])
    for r in range(ROWS):
        hg[r] = weight[r] * picked(level[r], [g[l, r] for l in range(L)])
    coef = banded(up, own, down, L)

    def dst(l, r, v):
        r = r - H
        p[l, r] = jnp.where(level[r] == float(l), hg[r], 0.0) - v

    adjoint(lambda l, r: ahead[l, r], lambda k, r: coef(k, r + H), c, W, (a, b), dst)
    for k, ref in enumerate((g, g0)):
        sums[k] = total([ref[l, r] * ref[l, r] for l in range(L) for r in range(ROWS)])


def sums_kernel(came, g, g0, p, early, u, g1, part):
    late = [[], []]
    for l in range(L):
        for r in range(ROWS):
            v = g[l, r] - came[l, r]
            u[l, r] = v
            one = -0.5 * (v + p[l, r])
            g1[l, r] = one
            late[0].append(g0[l, r] * one)
            late[1].append(one * one)
        late = [[total(terms)] for terms in late]
    lane = lax.broadcasted_iota(jnp.int32, (1, TILE), 1)
    row = jnp.zeros((1, TILE), jnp.float32)
    for k, v in enumerate((early[0], early[1], late[0][0], late[1][0])):
        s = jnp.sum(jnp.sum(v, axis=0, keepdims=True), axis=1, keepdims=True)
        row = jnp.where(lane == k, s, row)
    for i in range(part.shape[0]):
        part[i] = row


def again_kernel(parts, out):
    s = total([parts[i] for i in range(parts.shape[0])])
    for i in range(out.shape[0]):
        out[i] = s


def last_kernel(
    count, parts, keep, own, g, g0, g1, d, u, o1, hg, state_far, multipliers_far, obs_far, state, multipliers, obs, sems
):
    row = total([parts[i] for i in range(parts.shape[0])])
    lane = lax.broadcasted_iota(jnp.int32, (1, TILE), 1)
    sg, s00, s01, s11 = [
        jnp.broadcast_to(jnp.sum(jnp.where(lane == k, row, 0.0), axis=1, keepdims=True), ROW) / count
        for k in range(4)
    ]
    first = 0.3 / jnp.sqrt(sg + 1e-06)
    mean = jnp.maximum(s00 + first * (2.0 * s01 + first * s11), 0.0)
    second = 0.3 / jnp.sqrt(mean + 1e-06)
    half = 0.5 * first
    copies = []

    def send(here, far):
        copies.append(pltpu.make_async_copy(here, far, sems.at[len(copies)]))
        copies[-1].start()

    join_into(obs, (0,), [1.5 * o1[r] - half * hg[r] for r in range(ROWS)])
    send(obs, obs_far)
    for l in range(L):
        join_into(multipliers, (l,), [keep[l] * d[l, r] - half * u[l, r] for r in range(ROWS)])
        send(multipliers.at[l], multipliers_far.at[0, l])
        join_into(
            state,
            (l,),
            [
                own[l, r] - first * g[l, r] - second * (g0[l, r] + first * g1[l, r])
                for r in range(ROWS)
            ],
        )
        send(state.at[l], state_far.at[0, l])
    for copy in copies:
        copy.wait()


VM = pl.BlockSpec(memory_space=pltpu.VMEM)
FARM = pl.BlockSpec(memory_space=pltpu.HBM)


def call(kernel, outs, scratch=(), us=1.0, far_in=False, far_out=False):
    def run(*args):
        if far_in:
            args = [pltpu.with_memory_space_constraint(a, pltpu.HBM) for a in args]
        return pl.pallas_call(
            kernel,
            out_shape=[jax.ShapeDtypeStruct(s, jnp.float32) for s in outs],
            in_specs=[FARM if far_in else VM] * len(args),
            out_specs=[FARM if far_out else VM] * len(outs),
            scratch_shapes=[pltpu.VMEM(s, jnp.float32) if isinstance(s, tuple) else s for s in scratch],
            compiler_params=pltpu.CompilerParams(vmem_limit_bytes=16 * 2**20),
            cost_estimate=pl.CostEstimate(
                flops=int(us * 4e6), bytes_accessed=sum(4 * a.size for a in args), transcendentals=0
            ),
        )(*args)

    return run


def rows_of(k, n):
    return (k, n, *ROW)


def shifted(x, axis, by):
    count = lax.axis_size(axis)
    return lax.ppermute(x, axis, [(i, i + by) for i in range(count) if 0 <= i + by < count])


def exchanged(x, axis):
    return lax.all_to_all(x, axis, 0, 0, tiled=True)


def on_device(
    x_init, background, observed, diff_lon, diff_lat, drift, coupling, model_var, obs_level, huber_class
):
    band, wide = rows_of(L, ROWS), rows_of(L, W)
    whole = (L, ROWS, 8 * TILE)
    cells = (ROWS, *ROW)
    two, two_w = [rows_of(L, 3 * ROWS)] * 2, [wide] * 2
    count = float(L * ROWS * 8 * TILE * lax.axis_size(TM) * lax.axis_size("lat"))
    (own,) = call(
        pack_kernel,
        [rows_of(L + 3, ROWS)],
        [whole, (3, *whole[1:]), pltpu.SemaphoreType.DMA((4,))],
        far_in=True,
    )(x_init, diff_lon, diff_lat, drift)
    up, down = shifted(own, "lat", 1), shifted(own, "lat", -1)
    bg, obs, c, keep, level, weight = call(
        aside_kernel, [band, cells, (L * L, *ROW), (L, *ROW), cells, cells]
    )(background, observed, coupling, model_var[None], obs_level, huber_class)
    up, down, bg, obs, c, keep, level, weight = lax.optimization_barrier(
        (up, down, bg, obs, c, keep, level, weight)
    )

    (wide_x,) = call(middle_kernel, [wide])(up, own, down)
    after = shifted(wide_x, TM, -1)
    moved, moved_own = call(forward_kernel, [wide, band], two, 2.0)(c, up, own, down, up, own, down)
    came = shifted(moved_own, TM, 1)
    ahead, o1, p = call(back_kernel, [wide, cells, band], two_w, 1.5)(
        c, after, moved, up, own, down, obs, level, weight
    )
    d, g = call(gradient_kernel, [band, band], us=0.2)(came, own, bg, p)

    up_g, down_g = shifted(g, "lat", 1), shifted(g, "lat", -1)
    (g0,) = call(still_kernel, [band], two_w, 1.5)(c, keep, d, ahead, up, own, down, level, o1)
    up_g, down_g, g0 = lax.optimization_barrier((up_g, down_g, g0))
    (wide_g,) = call(middle_kernel, [wide])(up_g, g, down_g)
    after_g = shifted(wide_g, TM, -1)
    moved_g, moved_g_own = call(forward_kernel, [wide, band], two, 2.0)(
        c, up_g, g, down_g, up, own, down
    )
    came_g = shifted(moved_g_own, TM, 1)
    hg, q, early = call(back_g_kernel, [cells, band, (2, *ROW)], [wide] + two_w, 1.5)(
        c, after_g, moved_g, up, own, down, g, level, weight, g0
    )
    u, g1, part = call(sums_kernel, [band, band, (lax.axis_size(NEAR), 1, TILE)], us=0.3)(
        came_g, g, g0, q, early
    )
    (part,) = call(again_kernel, [(lax.axis_size(FAR), 1, TILE)], us=0.1)(exchanged(part, NEAR))
    part = exchanged(part, FAR)

    def finish(*refs):
        last_kernel(count, *refs)

    outs = call(
        finish,
        [(1, *whole), (1, *whole), (1, *whole[1:])],
        [whole, whole, (1, *whole[1:]), pltpu.SemaphoreType.DMA((2 * L + 1,))],
        far_out=True,
    )(part, keep, own, g, g0, g1, d, u, o1, hg)
    return tuple(outs)


def solution(mesh):
    torus = Mesh(mesh.devices.reshape(4, 8, 2, mesh.shape["lat"]), (*TM, "lat"))
    band = P(TM, "lat", None)
    in_specs = (
        P(TM, None, "lat", None),
        P(None, "lat", None),
        band,
        band,
        band,
        band,
        P(),
        P(),
        band,
        band,
    )
    out_specs = (P(TM, None, "lat", None), P(TM, None, "lat", None), band)
    return jax.shard_map(
        on_device, mesh=torus, in_specs=in_specs, out_specs=out_specs, check_vma=False
    )
```

time: 96.4 us -> 86.1 us (0.89)
  waiting for transfers between devices: 7.34 us -> 15.3 us
  blocking collectives: 41.7 us -> 34.6 us
  local copies, waits for them, and re-layouts: 5.93 us -> 0.03 us
  Pallas kernels: 11 us -> 7.33 us
  starting transfers between devices: 28.9 us -> 27.5 us
    ppermute x8, waiting for transfers between devices: 7.34 us -> 15.3 us  [shifted(): lax.ppermute(x, axis, [(i, i + by) for i in range(count) if 0 <= i + by <...]
    all_to_all x2, blocking collectives: 41.7 us -> 34.6 us  [exchanged(): return lax.all_to_all(x, axis, 0, 0, tiled=True)]
    unnamed x20 -> x12, local copies, waits for them, and re-layouts: 5.78 us -> 0.03 us
    pallas_call x11 -> x13, Pallas kernels: 11 us -> 7.33 us  [run(): pl.pallas_call(kernel, out_shape=[jax.ShapeDtypeStruct(s, jnp.float32) fo...]
    ppermute x8, starting transfers between devices: 28.9 us -> 27.5 us  [shifted(): lax.ppermute(x, axis, [(i, i + by) for i in range(count) if 0 <= i + by <...]
  transfers between devices with their start and end apart: 8 -> 8, of which waited for: 6 -> 6; matrix products, arithmetic and copies ran while one was open for 0% -> 0% of each run, Pallas kernels for 5% -> 6%
where the time goes in v2:
time: 86.1 us; the launch traced here: 85.7 us
  blocking collectives  34.6 us (40%)
  starting transfers between devices  27.5 us (32%)
  waiting for transfers between devices  15.3 us (18%)
  Pallas kernels  7.33 us (9%)
    all_to_all x2, blocking collectives, exchanged(): return lax.all_to_all(x, axis, 0, 0, tiled=True)  34.6 us
    ppermute x8, starting transfers between devices, shifted(): lax.ppermute(x, axis, [(i, i + by) for i in range(count) if 0 <= i + by <...  27.5 us
    ppermute x8, waiting for transfers between devices, shifted(): lax.ppermute(x, axis, [(i, i + by) for i in range(count) if 0 <= i + by <...  15.3 us
    pallas_call x13, Pallas kernels, run(): pl.pallas_call(kernel, out_shape=[jax.ShapeDtypeStruct(s, jnp.float32) fo...  7.33 us
  transfers between devices with their start and end apart: 8, of which 6 were waited for; matrix products, arithmetic and copies ran while one was open for 0% of the time, Pallas kernels for 6%

profile of v2, /device:TPU:1, one launch (start us, length us, event | category | flops | bytes accessed | tf_op | source)
XLA Modules:
  0.0 85.7 jit_solution(15383802193555683865)
XLA Ops:
  0.6 0.0 copy-start
  0.6 0.0 copy-start.1
  0.7 0.0 copy-start.2
  0.7 0.0 copy-start.3
  0.7 0.0 copy-start.4
  0.7 1.1 %shard_map.121.own.own_c.refs_2_ = f32[8,8,8,128]{3,2,1,0:T(8,128)S(1)} custom-call(f32[1,5,8,1024]{3,2,1,0:T(8,128)} %x_far.1, f32[1,8,1024]{2,1,0:T(8,128)} %kx_far.1, f32[1,8,1024]{2,1,0:T(8,128)} %ky_far.1, f32[1,8,1024]{2,1,0:T(8,128)} %ux_far.1), custom_call_target="tpu_custom_call" | custom-call | flops 4000000 | bytes 262144 | tf_op jit(solution)/shard_map/pallas_call | solution.py:328
  1.8 0.0 copy-start.5
  1.8 4.8 %collective-permute-start = (f32[8,8,8,128]{3,2,1,0:T(8,128)S(1)}, f32[8,8,8,128]{3,2,1,0:T(8,128)S(1)}, u32[]{:S(2)}, u32[]{:S(2)}) collective-permute-start(f32[8,8,8,128]{3,2,1,0:T(8,128)S(1)} %shard_map.121.own.own_c.refs_2_), channel_id=1, source_target_pairs={{0,1},{1,2},{2,3},{3,4},{4,5},{5,6},{6,7},{8,9},{9,10},{10,11},{11... | collective-permute-start | bytes 786440 | tf_op jit(solution)/shard_map/ppermute | solution.py:349
  6.6 1.3 %collective-permute-start.1 = (f32[8,8,8,128]{3,2,1,0:T(8,128)S(1)}, f32[8,8,8,128]{3,2,1,0:T(8,128)S(1)}, u32[]{:S(2)}, u32[]{:S(2)}) collective-permute-start(f32[8,8,8,128]{3,2,1,0:T(8,128)S(1)} %shard_map.121.own.own_c.refs_2_), channel_id=1, source_target_pairs={{1,0},{2,1},{3,2},{4,3},{5,4},{6,5},{7,6},{9,8},{10,9},{11,10},{12... | collective-permute-start | bytes 786440 | tf_op jit(solution)/shard_map/ppermute | solution.py:349
  7.9 0.0 copy-done
  7.9 0.0 copy-done.1
  7.9 0.0 copy-done.2
  8.0 0.0 copy-done.3
  8.0 0.0 copy-done.4
  8.0 0.0 copy-done.5
  8.0 0.1 shard_map.122
  8.1 1.8 %collective-permute-done.up.up_c = f32[8,8,8,128]{3,2,1,0:T(8,128)S(1)} collective-permute-done((f32[8,8,8,128]{3,2,1,0:T(8,128)S(1)}, f32[8,8,8,128]{3,2,1,0:T(8,128)S(1)}, u32[]{:S(2)}, u32[]{:S(2)}) %collective-permute-start) | collective-permute-done | bytes 262176 | tf_op jit(solution)/shard_map/ppermute | solution.py:349
  9.9 4.5 %collective-permute-done.1.down.down_c = f32[8,8,8,128]{3,2,1,0:T(8,128)S(1)} collective-permute-done((f32[8,8,8,128]{3,2,1,0:T(8,128)S(1)}, f32[8,8,8,128]{3,2,1,0:T(8,128)S(1)}, u32[]{:S(2)}, u32[]{:S(2)}) %collective-permute-start.1) | collective-permute-done | bytes 262176 | tf_op jit(solution)/shard_map/ppermute | solution.py:349
  14.4 5.8 %collective-permute-start.3 = (f32[5,16,8,128]{3,2,1,0:T(8,128)S(1)}, f32[5,16,8,128]{3,2,1,0:T(8,128)S(1)}, u32[]{:S(2)}, u32[]{:S(2)}) collective-permute-start(f32[5,16,8,128]{3,2,1,0:T(8,128)S(1)} %shard_map.124), channel_id=1, source_target_pairs={{8,0},{16,8},{24,16},{32,24},{40,32},{48,40},{56,48},{64,56},{72,6... | collective-permute-start | bytes 983048 | tf_op jit(solution)/shard_map/ppermute | solution.py:349
  20.2 1.2 %shard_map.123 = (f32[5,16,8,128]{3,2,1,0:T(8,128)S(1)}, f32[5,8,8,128]{3,2,1,0:T(8,128)S(1)}) custom-call(f32[25,8,128]{2,1,0:T(8,128)S(1)} %get-tuple-element.41.c, f32[8,8,8,128]{3,2,1,0:T(8,128)S(1)} %collective-permute-done.up.up_c, f32[8,8,8,128]{3,2,1,0:T(8,128)S(1)} %shard_map.121.own.own_c.refs_2_, ...), custom_call_target="tpu_custom_call" | custom-call | flops 8000000 | bytes 1675264 | tf_op jit(solution)/shard_map/pallas_call | solution.py:328
  21.4 2.7 %collective-permute-start.2 = (f32[5,8,8,128]{3,2,1,0:T(8,128)S(1)}, f32[5,8,8,128]{3,2,1,0:T(8,128)S(1)}, u32[]{:S(2)}, u32[]{:S(2)}) collective-permute-start(f32[5,8,8,128]{3,2,1,0:T(8,128)S(1)} %get-tuple-element.44), channel_id=1, source_target_pairs={{0,8},{8,16},{16,24},{24,32},{32,40},{40,48},{48,56},{56,64},{64,7... | collective-permute-start | bytes 491528 | tf_op jit(solution)/shard_map/ppermute | solution.py:349
  24.2 1.6 %collective-permute-done.3.after = f32[5,16,8,128]{3,2,1,0:T(8,128)S(1)} collective-permute-done((f32[5,16,8,128]{3,2,1,0:T(8,128)S(1)}, f32[5,16,8,128]{3,2,1,0:T(8,128)S(1)}, u32[]{:S(2)}, u32[]{:S(2)}) %collective-permute-start.3) | collective-permute-done | bytes 327712 | tf_op jit(solution)/shard_map/ppermute | solution.py:349
  25.7 0.8 shard_map.125
  26.5 0.0 collective-permute-done.2.came
  26.5 0.1 shard_map.126
  26.6 4.0 %collective-permute-start.4 = (f32[5,8,8,128]{3,2,1,0:T(8,128)S(1)}, f32[5,8,8,128]{3,2,1,0:T(8,128)S(1)}, u32[]{:S(2)}, u32[]{:S(2)}) collective-permute-start(f32[5,8,8,128]{3,2,1,0:T(8,128)S(1)} %get-tuple-element.51.own.g.refs_3_), channel_id=1, source_target_pairs={{0,1},{1,2},{2,3},{3,4},{4,5},{5,6},{6,7},{8,9},{9,10},{10,11},{11... | collective-permute-start | bytes 491528 | tf_op jit(solution)/shard_map/ppermute | solution.py:349
  30.6 1.3 %collective-permute-start.5 = (f32[5,8,8,128]{3,2,1,0:T(8,128)S(1)}, f32[5,8,8,128]{3,2,1,0:T(8,128)S(1)}, u32[]{:S(2)}, u32[]{:S(2)}) collective-permute-start(f32[5,8,8,128]{3,2,1,0:T(8,128)S(1)} %get-tuple-element.51.own.g.refs_3_), channel_id=1, source_target_pairs={{1,0},{2,1},{3,2},{4,3},{5,4},{6,5},{7,6},{9,8},{10,9},{11,10},{12... | collective-permute-start | bytes 491528 | tf_op jit(solution)/shard_map/ppermute | solution.py:349
  31.9 0.8 shard_map.127.g0.refs_4_
  32.7 0.3 collective-permute-done.4.up
  33.0 5.7 %collective-permute-done.5.down = f32[5,8,8,128]{3,2,1,0:T(8,128)S(1)} collective-permute-done((f32[5,8,8,128]{3,2,1,0:T(8,128)S(1)}, f32[5,8,8,128]{3,2,1,0:T(8,128)S(1)}, u32[]{:S(2)}, u32[]{:S(2)}) %collective-permute-start.5) | collective-permute-done | bytes 163872 | tf_op jit(solution)/shard_map/ppermute | solution.py:349
  38.7 1.9 %collective-permute-start.7 = (f32[5,16,8,128]{3,2,1,0:T(8,128)S(1)}, f32[5,16,8,128]{3,2,1,0:T(8,128)S(1)}, u32[]{:S(2)}, u32[]{:S(2)}) collective-permute-start(f32[5,16,8,128]{3,2,1,0:T(8,128)S(1)} %shard_map.129), channel_id=1, source_target_pairs={{8,0},{16,8},{24,16},{32,24},{40,32},{48,40},{56,48},{64,56},{72,6... | collective-permute-start | bytes 983048 | tf_op jit(solution)/shard_map/ppermute | solution.py:349
  40.6 1.3 %shard_map.128 = (f32[5,16,8,128]{3,2,1,0:T(8,128)S(1)}, f32[5,8,8,128]{3,2,1,0:T(8,128)S(1)}) custom-call(f32[25,8,128]{2,1,0:T(8,128)S(1)} %get-tuple-element.41.c, f32[5,8,8,128]{3,2,1,0:T(8,128)S(1)} %collective-permute-done.4.up, f32[5,8,8,128]{3,2,1,0:T(8,128)S(1)} %get-tuple-element.51.own.g.refs_3_, ...), custom_call_target="tpu_custom_call" | custom-call | flops 8000000 | bytes 1380352 | tf_op jit(solution)/shard_map/pallas_call | solution.py:328
  41.9 5.7 %collective-permute-start.6 = (f32[5,8,8,128]{3,2,1,0:T(8,128)S(1)}, f32[5,8,8,128]{3,2,1,0:T(8,128)S(1)}, u32[]{:S(2)}, u32[]{:S(2)}) collective-permute-start(f32[5,8,8,128]{3,2,1,0:T(8,128)S(1)} %get-tuple-element.58), channel_id=1, source_target_pairs={{0,8},{8,16},{16,24},{24,32},{32,40},{40,48},{48,56},{56,64},{64,7... | collective-permute-start | bytes 491528 | tf_op jit(solution)/shard_map/ppermute | solution.py:349
  47.6 1.6 %collective-permute-done.7.after = f32[5,16,8,128]{3,2,1,0:T(8,128)S(1)} collective-permute-done((f32[5,16,8,128]{3,2,1,0:T(8,128)S(1)}, f32[5,16,8,128]{3,2,1,0:T(8,128)S(1)}, u32[]{:S(2)}, u32[]{:S(2)}) %collective-permute-start.7) | collective-permute-done | bytes 327712 | tf_op jit(solution)/shard_map/ppermute | solution.py:349
  49.1 0.8 shard_map.130
  50.0 0.0 collective-permute-done.6.came
  50.0 0.1 shard_map.131
  50.1 13.2 %all_to_all.10.parts = f32[16,1,128]{2,1,0:T(1,128)S(1)} all-to-all(f32[16,1,128]{2,1,0:T(1,128)S(1)} %get-tuple-element.63), channel_id=1, replica_groups=mesh['tm_0'=4,'tm_1'=8,'tm_2'=2,'lat'=8] {'tm_2','lat'}, dimensions={0} | all-to-all | bytes 16384 | tf_op jit(solution)/shard_map/all_to_all | solution.py:353
  63.4 21.4 %all_to_all.11.refs_0_ = f32[32,1,128]{2,1,0:T(1,128)S(1)} all-to-all(f32[32,1,128]{2,1,0:T(1,128)S(1)} %shard_map.132), channel_id=1, replica_groups=mesh['tm_0'=4,'tm_1'=8,'tm_2'=2,'lat'=8] {'tm_0','tm_1'}, dimensions={0} | all-to-all | bytes 32768 | tf_op jit(solution)/shard_map/all_to_all | solution.py:353
  84.7 0.9 %shard_map.133 = (f32[1,5,8,1024]{3,2,1,0:T(8,128)}, f32[1,5,8,1024]{3,2,1,0:T(8,128)}, f32[1,8,1024]{2,1,0:T(8,128)}) custom-call(f32[32,1,128]{2,1,0:T(1,128)S(1)} %all_to_all.11.refs_0_, f32[5,8,128]{2,1,0:T(8,128)S(1)} %get-tuple-element.52.keep.refs_1_, f32[8,8,8,128]{3,2,1,0:T(8,128)S(1)} %shard_map.121.own.own_c.refs_2_, ...), custom_call_target="tpu_custom_call" | custom-call | flops 4000000 | bytes 1183744 | tf_op jit(solution)/shard_map/pallas_call | solution.py:328
  (3 shorter events, 0.1 us)
Async XLA Ops:
  0.6 7.3 %copy-start = (f32[5,8,1024]{2,1,0:T(8,128)S(1)}, f32[5,8,1024]{2,1,0:T(8,128)}, u32[]{:S(2)}) copy-start(f32[5,8,1024]{2,1,0:T(8,128)} %background.1) | copy-start | bytes 491524
  0.6 7.3 %copy-start.1 = (f32[1,8,1024]{2,1,0:T(8,128)S(1)}, f32[1,8,1024]{2,1,0:T(8,128)}, u32[]{:S(2)}) copy-start(f32[1,8,1024]{2,1,0:T(8,128)} %observed.1) | copy-start | bytes 98308
  0.7 7.3 %copy-start.2 = (f32[5,5]{1,0:T(8,128)S(1)}, f32[5,5]{1,0:T(8,128)}, u32[]{:S(2)}) copy-start(f32[5,5]{1,0:T(8,128)} %coupling.1) | copy-start | bytes 304
  0.7 7.3 %copy-start.3 = (s32[1,8,8]{2,1,0:T(8,128)S(1)}, s32[1,8,8]{2,1,0:T(8,128)}, u32[]{:S(2)}) copy-start(s32[1,8,8]{2,1,0:T(8,128)} %obs_level.1) | copy-start | bytes 772
  0.7 7.3 %copy-start.4 = (s32[1,8,8]{2,1,0:T(8,128)S(1)}, s32[1,8,8]{2,1,0:T(8,128)}, u32[]{:S(2)}) copy-start(s32[1,8,8]{2,1,0:T(8,128)} %huber_class.1) | copy-start | bytes 772
  1.8 6.2 %copy-start.5 = (f32[5]{0:T(128)S(1)}, f32[5]{0:T(128)}, u32[]{:S(2)}) copy-start(f32[5]{0:T(128)} %param.17) | copy-start | bytes 64
  1.8 8.1 %collective-permute-start = (f32[8,8,8,128]{3,2,1,0:T(8,128)S(1)}, f32[8,8,8,128]{3,2,1,0:T(8,128)S(1)}, u32[]{:S(2)}, u32[]{:S(2)}) collective-permute-start(f32[8,8,8,128]{3,2,1,0:T(8,128)S(1)} %shard_map.121.own.own_c.refs_2_), channel_id=1, source_target_pairs={{0,1},{1,2},{2,3},{3,4},{4,5},{5,6},{6,7},{8,9},{9,10},{10,11},{11... | collective-permute-start | bytes 786440 | tf_op jit(solution)/shard_map/ppermute | solution.py:349
  6.6 7.7 %collective-permute-start.1 = (f32[8,8,8,128]{3,2,1,0:T(8,128)S(1)}, f32[8,8,8,128]{3,2,1,0:T(8,128)S(1)}, u32[]{:S(2)}, u32[]{:S(2)}) collective-permute-start(f32[8,8,8,128]{3,2,1,0:T(8,128)S(1)} %shard_map.121.own.own_c.refs_2_), channel_id=1, source_target_pairs={{1,0},{2,1},{3,2},{4,3},{5,4},{6,5},{7,6},{9,8},{10,9},{11,10},{12... | collective-permute-start | bytes 786440 | tf_op jit(solution)/shard_map/ppermute | solution.py:349
  14.4 11.3 %collective-permute-start.3 = (f32[5,16,8,128]{3,2,1,0:T(8,128)S(1)}, f32[5,16,8,128]{3,2,1,0:T(8,128)S(1)}, u32[]{:S(2)}, u32[]{:S(2)}) collective-permute-start(f32[5,16,8,128]{3,2,1,0:T(8,128)S(1)} %shard_map.124), channel_id=1, source_target_pairs={{8,0},{16,8},{24,16},{32,24},{40,32},{48,40},{56,48},{64,56},{72,6... | collective-permute-start | bytes 983048 | tf_op jit(solution)/shard_map/ppermute | solution.py:349
  21.4 5.1 %collective-permute-start.2 = (f32[5,8,8,128]{3,2,1,0:T(8,128)S(1)}, f32[5,8,8,128]{3,2,1,0:T(8,128)S(1)}, u32[]{:S(2)}, u32[]{:S(2)}) collective-permute-start(f32[5,8,8,128]{3,2,1,0:T(8,128)S(1)} %get-tuple-element.44), channel_id=1, source_target_pairs={{0,8},{8,16},{16,24},{24,32},{32,40},{40,48},{48,56},{56,64},{64,7... | collective-permute-start | bytes 491528 | tf_op jit(solution)/shard_map/ppermute | solution.py:349
  26.6 6.4 %collective-permute-start.4 = (f32[5,8,8,128]{3,2,1,0:T(8,128)S(1)}, f32[5,8,8,128]{3,2,1,0:T(8,128)S(1)}, u32[]{:S(2)}, u32[]{:S(2)}) collective-permute-start(f32[5,8,8,128]{3,2,1,0:T(8,128)S(1)} %get-tuple-element.51.own.g.refs_3_), channel_id=1, source_target_pairs={{0,1},{1,2},{2,3},{3,4},{4,5},{5,6},{6,7},{8,9},{9,10},{10,11},{11... | collective-permute-start | bytes 491528 | tf_op jit(solution)/shard_map/ppermute | solution.py:349
  30.6 8.0 %collective-permute-start.5 = (f32[5,8,8,128]{3,2,1,0:T(8,128)S(1)}, f32[5,8,8,128]{3,2,1,0:T(8,128)S(1)}, u32[]{:S(2)}, u32[]{:S(2)}) collective-permute-start(f32[5,8,8,128]{3,2,1,0:T(8,128)S(1)} %get-tuple-element.51.own.g.refs_3_), channel_id=1, source_target_pairs={{1,0},{2,1},{3,2},{4,3},{5,4},{6,5},{7,6},{9,8},{10,9},{11,10},{12... | collective-permute-start | bytes 491528 | tf_op jit(solution)/shard_map/ppermute | solution.py:349
  38.7 10.4 %collective-permute-start.7 = (f32[5,16,8,128]{3,2,1,0:T(8,128)S(1)}, f32[5,16,8,128]{3,2,1,0:T(8,128)S(1)}, u32[]{:S(2)}, u32[]{:S(2)}) collective-permute-start(f32[5,16,8,128]{3,2,1,0:T(8,128)S(1)} %shard_map.129), channel_id=1, source_target_pairs={{8,0},{16,8},{24,16},{32,24},{40,32},{48,40},{56,48},{64,56},{72,6... | collective-permute-start | bytes 983048 | tf_op jit(solution)/shard_map/ppermute | solution.py:349
  41.9 8.1 %collective-permute-start.6 = (f32[5,8,8,128]{3,2,1,0:T(8,128)S(1)}, f32[5,8,8,128]{3,2,1,0:T(8,128)S(1)}, u32[]{:S(2)}, u32[]{:S(2)}) collective-permute-start(f32[5,8,8,128]{3,2,1,0:T(8,128)S(1)} %get-tuple-element.58), channel_id=1, source_target_pairs={{0,8},{8,16},{16,24},{24,32},{32,40},{40,48},{48,56},{56,64},{64,7... | collective-permute-start | bytes 491528 | tf_op jit(solution)/shard_map/ppermute | solution.py:349

commit v3 on v2

--- a/solution.py
+++ b/solution.py
@@ -165,8 +165,9 @@
 
 
 def aside_kernel(
-    background, observed, coupling, var, obs_level, huber_class, bg, obs, c, keep, level, weight
+    own, background, observed, coupling, var, obs_level, huber_class, x, bg, obs, c, keep, level, weight
 ):
+    x[...] = own[:L]
     level[...] = tiles(obs_level[0].astype(jnp.float32))
     h = huber_class[0]
     weight[...] = tiles(jnp.where(h == 0, 1.0, 0.0) + jnp.where(h == 1, 0.5, 0.0) + jnp.where(h == 2, 0.25, 0.0))
@@ -178,20 +179,53 @@
     obs[...] = split(observed[0])
 
 
-def middle_kernel(up, own, down, out):
+def odd(axis):
+    return lax.rem(lax.axis_index(axis), 2) == 1
+
+
+def forward_kernel(c, first, second, own, up, down, moved, one, two, a, b):
+    upper = odd("lat")
+    for k in range(L + 3):
+        for r in range(ROWS):
+            up[k, r] = jnp.where(upper, second[k, r], first[k, r])
+            down[k, r] = jnp.where(upper, first[k, r], second[k, r])
+    send(c, up, own, down, up, own, down, moved, one, two, a, b)
+
+
+def forward_g_kernel(c, first, second, own, up_c, own_c, down_c, moved, one, two, up, down, a, b):
+    upper = odd("lat")
     for k in range(L):
-        out[k, :H] = up[k, H:]
-        out[k, H : H + ROWS] = own[k]
-        out[k, H + ROWS :] = down[k, :H]
-
-
-def forward_kernel(c, up, own, down, up_c, own_c, down_c, out, out_own, a, b):
+        for r in range(ROWS):
+            up[k, r] = jnp.where(upper, second[k, r], first[k, r])
+            down[k, r] = jnp.where(upper, first[k, r], second[k, r])
+    send(c, up, own, down, up_c, own_c, down_c, moved, one, two, a, b)
+
+
+def send(c, up, own, down, up_c, own_c, down_c, moved, one, two, a, b):
+    ahead = odd(TM[-1])
+
     def dst(l, r, v):
-        out[l, r - H] = v
+        moved[l, r - H] = v
         if ROWS <= r < 2 * ROWS:
-            out_own[l, r - ROWS] = v
+            r = r - ROWS
+            halo = up[l, H + r] if r < H else down[l, r - H]
+            one[l, r] = jnp.where(ahead, v, halo)
+            two[l, r] = jnp.where(ahead, halo, v)
 
     forward(banded(up, own, down, 0), banded(up_c, own_c, down_c, L), c, 3 * ROWS, (a, b), dst)
+
+
+def receive(one, two, after, moved, factor, out):
+    ahead = odd(TM[-1])
+    for l in range(L):
+        for r in range(W):
+            if H <= r < H + ROWS:
+                v = after[l, r - H]
+            else:
+                at = r if r < H else r - ROWS
+                v = jnp.where(ahead, one[l, at], two[l, at])
+            out[l, r] = factor * (v - moved[l, r])
+    return lambda l, r: jnp.where(ahead, two[l, r], one[l, r])
 
 
 def picked(level, values):
@@ -201,32 +235,26 @@
     return out
 
 
-def back_kernel(c, after, moved, up, own, down, obs, level, weight, ahead, o1, p, a, b):
-    half = 0.5 * place()[0]
-    for l in range(L):
-        for r in range(W):
-            ahead[l, r] = half * (after[l, r] - moved[l, r])
+def back_kernel(
+    c, one, two, after, moved, up, own, down, bg, obs, level, weight, ahead, o1, d, g, a, b
+):
+    some, first = place()
+    came = receive(one, two, after, moved, 0.5 * some, ahead)
     for r in range(ROWS):
         o1[r] = 0.5 * weight[r] * (picked(level[r], [own[l, r] for l in range(L)]) - obs[r])
     coef = banded(up, own, down, L)
 
     def dst(l, r, v):
         r = r - H
-        p[l, r] = jnp.where(level[r] == float(l), o1[r], 0.0) - v
+        one = 0.5 * (own[l, r] - (came(l, r) + first * bg[l, r]))
+        d[l, r] = one
+        g[l, r] = one - v + jnp.where(level[r] == float(l), o1[r], 0.0)
 
     adjoint(lambda l, r: ahead[l, r], lambda k, r: coef(k, r + H), c, W, (a, b), dst)
 
 
-def gradient_kernel(came, own, bg, p, d, g):
-    first = place()[1]
-    for l in range(L):
-        for r in range(ROWS):
-            v = 0.5 * (own[l, r] - (came[l, r] + first * bg[l, r]))
-            d[l, r] = v
-            g[l, r] = v + p[l, r]
-
-
-def still_kernel(c, keep, d, ahead, up, own, down, level, o1, g0, a, b):
+def still_kernel(c, keep, d, ahead, up, own, down, level, o1, g, g0, g_out, a, b):
+    g_out[...] = g[...]
     coef = banded(up, own, down, L)
 
     def dst(l, r, v):
@@ -236,39 +264,31 @@
     adjoint(lambda l, r: keep[l] * ahead[l, r], lambda k, r: coef(k, r + H), c, W, (a, b), dst)
 
 
-def back_g_kernel(c, after, moved, up, own, down, g, level, weight, g0, hg, p, sums, ahead, a, b):
-    some = place()[0]
-    for l in range(L):
-        for r in range(W):
-            ahead[l, r] = some * (after[l, r] - moved[l, r])
+def back_g_kernel(
+    c, one, two, after, moved, up, own, down, g, level, weight, g0, u, g1, hg, part, ahead, a, b
+):
+    came = receive(one, two, after, moved, place()[0], ahead)
     for r in range(ROWS):
         hg[r] = weight[r] * picked(level[r], [g[l, r] for l in range(L)])
     coef = banded(up, own, down, L)
+    sums = [[], [], [], []]
 
     def dst(l, r, v):
         r = r - H
-        p[l, r] = jnp.where(level[r] == float(l), hg[r], 0.0) - v
+        now = g[l, r] - came(l, r)
+        u[l, r] = now
+        one = -0.5 * (now - v + jnp.where(level[r] == float(l), hg[r], 0.0))
+        g1[l, r] = one
+        for k, term in enumerate((g[l, r] * g[l, r], g0[l, r] * g0[l, r], g0[l, r] * one, one * one)):
+            sums[k].append(term)
+            if len(sums[k]) == L:
+                sums[k] = [total(sums[k])]
 
     adjoint(lambda l, r: ahead[l, r], lambda k, r: coef(k, r + H), c, W, (a, b), dst)
-    for k, ref in enumerate((g, g0)):
-        sums[k] = total([ref[l, r] * ref[l, r] for l in range(L) for r in range(ROWS)])
-
-
-def sums_kernel(came, g, g0, p, early, u, g1, part):
-    late = [[], []]
-    for l in range(L):
-        for r in range(ROWS):
-            v = g[l, r] - came[l, r]
-            u[l, r] = v
-            one = -0.5 * (v + p[l, r])
-            g1[l, r] = one
-            late[0].append(g0[l, r] * one)
-            late[1].append(one * one)
-        late = [[total(terms)] for terms in late]
     lane = lax.broadcasted_iota(jnp.int32, (1, TILE), 1)
     row = jnp.zeros((1, TILE), jnp.float32)
-    for k, v in enumerate((early[0], early[1], late[0][0], late[1][0])):
-        s = jnp.sum(jnp.sum(v, axis=0, keepdims=True), axis=1, keepdims=True)
+    for k in range(4):
+        s = jnp.sum(jnp.sum(total(sums[k]), axis=0, keepdims=True), axis=1, keepdims=True)
         row = jnp.where(lane == k, s, row)
     for i in range(part.shape[0]):
         part[i] = row
@@ -349,6 +369,16 @@
     return lax.ppermute(x, axis, [(i, i + by) for i in range(count) if 0 <= i + by < count])
 
 
+def swapped(*args):
+    *arrays, axis = args
+    count = lax.axis_size(axis)
+    out = []
+    for x, start in zip((arrays[0], arrays[-1]), (1, 0)):
+        lows = range(start, count - 1, 2)
+        out.append(lax.ppermute(x, axis, [p for i in lows for p in ((i, i + 1), (i + 1, i))]))
+    return out
+
+
 def exchanged(x, axis):
     return lax.all_to_all(x, axis, 0, 0, tiled=True)
 
@@ -367,38 +397,38 @@
         [whole, (3, *whole[1:]), pltpu.SemaphoreType.DMA((4,))],
         far_in=True,
     )(x_init, diff_lon, diff_lat, drift)
-    up, down = shifted(own, "lat", 1), shifted(own, "lat", -1)
-    bg, obs, c, keep, level, weight = call(
-        aside_kernel, [band, cells, (L * L, *ROW), (L, *ROW), cells, cells]
-    )(background, observed, coupling, model_var[None], obs_level, huber_class)
-    up, down, bg, obs, c, keep, level, weight = lax.optimization_barrier(
-        (up, down, bg, obs, c, keep, level, weight)
-    )
-
-    (wide_x,) = call(middle_kernel, [wide])(up, own, down)
-    after = shifted(wide_x, TM, -1)
-    moved, moved_own = call(forward_kernel, [wide, band], two, 2.0)(c, up, own, down, up, own, down)
-    came = shifted(moved_own, TM, 1)
-    ahead, o1, p = call(back_kernel, [wide, cells, band], two_w, 1.5)(
-        c, after, moved, up, own, down, obs, level, weight
-    )
-    d, g = call(gradient_kernel, [band, band], us=0.2)(came, own, bg, p)
-
-    up_g, down_g = shifted(g, "lat", 1), shifted(g, "lat", -1)
-    (g0,) = call(still_kernel, [band], two_w, 1.5)(c, keep, d, ahead, up, own, down, level, o1)
-    up_g, down_g, g0 = lax.optimization_barrier((up_g, down_g, g0))
-    (wide_g,) = call(middle_kernel, [wide])(up_g, g, down_g)
-    after_g = shifted(wide_g, TM, -1)
-    moved_g, moved_g_own = call(forward_kernel, [wide, band], two, 2.0)(
-        c, up_g, g, down_g, up, own, down
-    )
-    came_g = shifted(moved_g_own, TM, 1)
-    hg, q, early = call(back_g_kernel, [cells, band, (2, *ROW)], [wide] + two_w, 1.5)(
-        c, after_g, moved_g, up, own, down, g, level, weight, g0
-    )
-    u, g1, part = call(sums_kernel, [band, band, (lax.axis_size(NEAR), 1, TILE)], us=0.3)(
-        came_g, g, g0, q, early
-    )
+    first, second = swapped(own, "lat")
+    x, bg, obs, c, keep, level, weight = call(
+        aside_kernel, [band, band, cells, (L * L, *ROW), (L, *ROW), cells, cells]
+    )(own, background, observed, coupling, model_var[None], obs_level, huber_class)
+    after = shifted(x, TM, -1)
+    first, second, bg, obs, c, keep, level, weight = lax.optimization_barrier(
+        (first, second, bg, obs, c, keep, level, weight)
+    )
+
+    three = rows_of(L + 3, ROWS)
+    up, down, moved, *sent = call(forward_kernel, [three, three, wide, band, band], two, 2.0)(
+        c, first, second, own
+    )
+    ahead, o1, d, g = call(back_kernel, [wide, cells, band, band], two_w, 1.5)(
+        c, *swapped(*sent, TM), after, moved, up, own, down, bg, obs, level, weight
+    )
+
+    first, second = swapped(g, "lat")
+    g0, g_copy = call(still_kernel, [band, band], two_w, 1.5)(
+        c, keep, d, ahead, up, own, down, level, o1, g
+    )
+    after_g = shifted(g_copy, TM, -1)
+    first, second, g0 = lax.optimization_barrier((first, second, g0))
+    moved_g, *sent = call(forward_g_kernel, [wide, band, band], [band, band] + two, 2.0)(
+        c, first, second, g, up, own, down
+    )
+    u, g1, hg, part = call(
+        back_g_kernel,
+        [band, band, cells, (lax.axis_size(NEAR), 1, TILE)],
+        [wide] + two_w,
+        1.5,
+    )(c, *swapped(*sent, TM), after_g, moved_g, up, own, down, g, level, weight, g0)
     (part,) = call(again_kernel, [(lax.axis_size(FAR), 1, TILE)], us=0.1)(exchanged(part, NEAR))
     part = exchanged(part, FAR)
 

time: 86.1 us -> 84.6 us (0.983)
  waiting for transfers between devices: 15.3 us -> 2.96 us
  starting transfers between devices: 27.5 us -> 34 us
  blocking collectives: 34.6 us -> 39 us
    ppermute x0 -> x8, starting transfers between devices: none -> 25.7 us  [swapped(): lax.ppermute(x, axis, [p for i in lows for p in ((i, i + 1), (i + 1, i))])]
    ppermute x8 -> x2, starting transfers between devices: 27.5 us -> 8.22 us  [shifted(): lax.ppermute(x, axis, [(i, i + by) for i in range(count) if 0 <= i + by <...]
    ppermute x8 -> x2, waiting for transfers between devices: 15.3 us -> 0.01 us  [shifted(): lax.ppermute(x, axis, [(i, i + by) for i in range(count) if 0 <= i + by <...]
    all_to_all x2, blocking collectives: 34.6 us -> 39 us  [exchanged(): return lax.all_to_all(x, axis, 0, 0, tiled=True)]
    ppermute x0 -> x8, waiting for transfers between devices: none -> 2.95 us  [swapped(): lax.ppermute(x, axis, [p for i in lows for p in ((i, i + 1), (i + 1, i))])]
    pallas_call x13 -> x9, Pallas kernels: 7.33 us -> 7.31 us  [run(): pl.pallas_call(kernel, out_shape=[jax.ShapeDtypeStruct(s, jnp.float32) fo...]
  transfers between devices with their start and end apart: 8 -> 10, of which waited for: 6 -> 5; matrix products, arithmetic and copies ran while one was open for 0% -> 0% of each run, Pallas kernels for 6% -> 4%
where the time goes in v3:
time: 84.6 us; the launch traced here: 84.1 us
  blocking collectives  39 us (46%)
  starting transfers between devices  34 us (40%)
  Pallas kernels  7.31 us (9%)
  waiting for transfers between devices  2.96 us (3%)
  between operations  0.87 us (1%)
    all_to_all x2, blocking collectives, exchanged(): return lax.all_to_all(x, axis, 0, 0, tiled=True)  39 us
    ppermute x8, starting transfers between devices, swapped(): lax.ppermute(x, axis, [p for i in lows for p in ((i, i + 1), (i + 1, i))])  25.7 us
    ppermute x2, starting transfers between devices, shifted(): lax.ppermute(x, axis, [(i, i + by) for i in range(count) if 0 <= i + by <...  8.22 us
    pallas_call x9, Pallas kernels, run(): pl.pallas_call(kernel, out_shape=[jax.ShapeDtypeStruct(s, jnp.float32) fo...  7.31 us
    ppermute x8, waiting for transfers between devices, swapped(): lax.ppermute(x, axis, [p for i in lows for p in ((i, i + 1), (i + 1, i))])  2.95 us
  transfers between devices with their start and end apart: 10, of which 5 were waited for; matrix products, arithmetic and copies ran while one was open for 0% of the time, Pallas kernels for 4%

profile of v3, /device:TPU:1, one launch (start us, length us, event | category | flops | bytes accessed | tf_op | source)
XLA Modules:
  0.0 84.1 jit_solution(3228477797132527613)
XLA Ops:
  0.6 0.0 copy-start.1
  0.6 0.0 copy-start
  0.7 0.0 copy-start.2
  0.7 0.0 copy-start.3
  0.7 0.0 copy-start.4
  0.7 1.1 %shard_map.121.own.own_c.refs_2_ = f32[8,8,8,128]{3,2,1,0:T(8,128)S(1)} custom-call(f32[1,5,8,1024]{3,2,1,0:T(8,128)} %x_far.1, f32[1,8,1024]{2,1,0:T(8,128)} %kx_far.1, f32[1,8,1024]{2,1,0:T(8,128)} %ky_far.1, f32[1,8,1024]{2,1,0:T(8,128)} %ux_far.1), custom_call_target="tpu_custom_call" | custom-call | flops 4000000 | bytes 262144 | tf_op jit(solution)/shard_map/pallas_call | solution.py:348
  1.8 0.0 copy-start.5
  1.8 4.8 %collective-permute-start.1 = (f32[8,8,8,128]{3,2,1,0:T(8,128)S(1)}, f32[8,8,8,128]{3,2,1,0:T(8,128)S(1)}, u32[]{:S(2)}, u32[]{:S(2)}) collective-permute-start(f32[8,8,8,128]{3,2,1,0:T(8,128)S(1)} %shard_map.121.own.own_c.refs_2_), channel_id=1, source_target_pairs={{0,1},{1,0},{2,3},{3,2},{4,5},{5,4},{6,7},{7,6},{8,9},{9,8},{10,11... | collective-permute-start | bytes 786440 | tf_op jit(solution)/shard_map/ppermute | solution.py:378
  6.6 0.7 collective-permute-start
  7.3 0.0 copy-done.1
  7.3 0.0 copy-done
  7.3 0.0 copy-done.2
  7.3 0.0 copy-done.3
  7.3 0.0 copy-done.4
  7.3 0.0 copy-done.5
  7.4 0.1 shard_map.122
  7.5 5.9 %collective-permute-start.4 = (f32[5,8,8,128]{3,2,1,0:T(8,128)S(1)}, f32[5,8,8,128]{3,2,1,0:T(8,128)S(1)}, u32[]{:S(2)}, u32[]{:S(2)}) collective-permute-start(f32[5,8,8,128]{3,2,1,0:T(8,128)S(1)} %get-tuple-element.50), channel_id=1, source_target_pairs={{8,0},{16,8},{24,16},{32,24},{40,32},{48,40},{56,48},{64,56},{72,6... | collective-permute-start | bytes 491528 | tf_op jit(solution)/shard_map/ppermute | solution.py:369
  13.4 0.0 collective-permute-done.1.second
  13.4 0.0 collective-permute-done.first
  13.4 1.3 %shard_map.123 = (f32[8,8,8,128]{3,2,1,0:T(8,128)S(1)}, f32[8,8,8,128]{3,2,1,0:T(8,128)S(1)}, f32[5,16,8,128]{3,2,1,0:T(8,128)S(1)}, f32[5,8,8,128]{3,2,1,0:T(8,128)S(1)}, f32[5,8,8,128]{3,2,1,0:T(8,128)S(1)}) custom-call(f32[25,8,128]{2,1,0:T(8,128)S(1)} %get-tuple-element.45.c, f32[8,8,8,128]{3,2,1,0:T(8,128)S(1)} %collective-permute-done.first, ...), custom_call_target="tpu_custom_call" | custom-call | flops 8000000 | bytes 888832 | tf_op jit(solution)/shard_map/pallas_call | solution.py:348
  14.7 3.5 %collective-permute-start.2 = (f32[5,8,8,128]{3,2,1,0:T(8,128)S(1)}, f32[5,8,8,128]{3,2,1,0:T(8,128)S(1)}, u32[]{:S(2)}, u32[]{:S(2)}) collective-permute-start(f32[5,8,8,128]{3,2,1,0:T(8,128)S(1)} %get-tuple-element.48), channel_id=1, source_target_pairs={{8,16},{16,8},{24,32},{32,24},{40,48},{48,40},{56,64},{64,56},{72,... | collective-permute-start | bytes 491528 | tf_op jit(solution)/shard_map/ppermute | solution.py:378
  18.2 2.6 %collective-permute-start.3 = (f32[5,8,8,128]{3,2,1,0:T(8,128)S(1)}, f32[5,8,8,128]{3,2,1,0:T(8,128)S(1)}, u32[]{:S(2)}, u32[]{:S(2)}) collective-permute-start(f32[5,8,8,128]{3,2,1,0:T(8,128)S(1)} %get-tuple-element.49), channel_id=1, source_target_pairs={{0,8},{8,0},{16,24},{24,16},{32,40},{40,32},{48,56},{56,48},{64,72... | collective-permute-start | bytes 491528 | tf_op jit(solution)/shard_map/ppermute | solution.py:378
  20.8 0.0 collective-permute-done.4.after
  20.8 0.5 collective-permute-done.2.one
  21.3 0.5 collective-permute-done.3.two
  21.8 0.8 %shard_map.124 = (f32[5,16,8,128]{3,2,1,0:T(8,128)S(1)}, f32[8,8,128]{2,1,0:T(8,128)S(1)}, f32[5,8,8,128]{3,2,1,0:T(8,128)S(1)}, f32[5,8,8,128]{3,2,1,0:T(8,128)S(1)}) custom-call(f32[25,8,128]{2,1,0:T(8,128)S(1)} %get-tuple-element.45.c, f32[5,8,8,128]{3,2,1,0:T(8,128)S(1)} %collective-permute-done.2.one, f32[5,8,8,128]{3,2,1,0:T(8,128)S(1)} %collective-permute-done.3.two, ...), custom_call_target="tpu_custom_call" | custom-call | flops 6000000 | bytes 1970176 | tf_op jit(solution)/shard_map/pallas_call | solution.py:348
  22.7 7.7 %collective-permute-start.6 = (f32[5,8,8,128]{3,2,1,0:T(8,128)S(1)}, f32[5,8,8,128]{3,2,1,0:T(8,128)S(1)}, u32[]{:S(2)}, u32[]{:S(2)}) collective-permute-start(f32[5,8,8,128]{3,2,1,0:T(8,128)S(1)} %get-tuple-element.58.g.own.refs_3_), channel_id=1, source_target_pairs={{0,1},{1,0},{2,3},{3,2},{4,5},{5,4},{6,7},{7,6},{8,9},{9,8},{10,11... | collective-permute-start | bytes 491528 | tf_op jit(solution)/shard_map/ppermute | solution.py:378
  30.4 0.7 collective-permute-start.5
  31.1 0.8 shard_map.125
  31.9 2.3 %collective-permute-start.9 = (f32[5,8,8,128]{3,2,1,0:T(8,128)S(1)}, f32[5,8,8,128]{3,2,1,0:T(8,128)S(1)}, u32[]{:S(2)}, u32[]{:S(2)}) collective-permute-start(f32[5,8,8,128]{3,2,1,0:T(8,128)S(1)} %get-tuple-element.68), channel_id=1, source_target_pairs={{8,0},{16,8},{24,16},{32,24},{40,32},{48,40},{56,48},{64,56},{72,6... | collective-permute-start | bytes 491528 | tf_op jit(solution)/shard_map/ppermute | solution.py:369
  34.2 0.6 collective-permute-done.6.second
  34.8 0.0 collective-permute-done.5.first
  34.8 1.3 %shard_map.126 = (f32[5,16,8,128]{3,2,1,0:T(8,128)S(1)}, f32[5,8,8,128]{3,2,1,0:T(8,128)S(1)}, f32[5,8,8,128]{3,2,1,0:T(8,128)S(1)}) custom-call(f32[25,8,128]{2,1,0:T(8,128)S(1)} %get-tuple-element.45.c, f32[5,8,8,128]{3,2,1,0:T(8,128)S(1)} %collective-permute-done.5.first, f32[5,8,8,128]{3,2,1,0:T(8,128)S(1)} %collective-permute-done.6.second, ...), custom_call_target="tpu_custom_call" | custom-call | flops 8000000 | bytes 1380352 | tf_op jit(solution)/shard_map/pallas_call | solution.py:348
  36.1 3.8 %collective-permute-start.7 = (f32[5,8,8,128]{3,2,1,0:T(8,128)S(1)}, f32[5,8,8,128]{3,2,1,0:T(8,128)S(1)}, u32[]{:S(2)}, u32[]{:S(2)}) collective-permute-start(f32[5,8,8,128]{3,2,1,0:T(8,128)S(1)} %get-tuple-element.66), channel_id=1, source_target_pairs={{8,16},{16,8},{24,32},{32,24},{40,48},{48,40},{56,64},{64,56},{72,... | collective-permute-start | bytes 491528 | tf_op jit(solution)/shard_map/ppermute | solution.py:378
  39.9 1.9 %collective-permute-start.8 = (f32[5,8,8,128]{3,2,1,0:T(8,128)S(1)}, f32[5,8,8,128]{3,2,1,0:T(8,128)S(1)}, u32[]{:S(2)}, u32[]{:S(2)}) collective-permute-start(f32[5,8,8,128]{3,2,1,0:T(8,128)S(1)} %get-tuple-element.67), channel_id=1, source_target_pairs={{0,8},{8,0},{16,24},{24,16},{32,40},{40,32},{48,56},{56,48},{64,72... | collective-permute-start | bytes 491528 | tf_op jit(solution)/shard_map/ppermute | solution.py:378
  41.8 0.0 collective-permute-done.9.after
  41.8 1.0 %collective-permute-done.7.one = f32[5,8,8,128]{3,2,1,0:T(8,128)S(1)} collective-permute-done((f32[5,8,8,128]{3,2,1,0:T(8,128)S(1)}, f32[5,8,8,128]{3,2,1,0:T(8,128)S(1)}, u32[]{:S(2)}, u32[]{:S(2)}) %collective-permute-start.7) | collective-permute-done | bytes 163872 | tf_op jit(solution)/shard_map/ppermute | solution.py:378
  42.9 0.3 collective-permute-done.8.two
  43.2 1.0 %shard_map.127 = (f32[5,8,8,128]{3,2,1,0:T(8,128)S(1)}, f32[5,8,8,128]{3,2,1,0:T(8,128)S(1)}, f32[8,8,128]{2,1,0:T(8,128)S(1)}, f32[16,1,128]{2,1,0:T(1,128)S(1)}) custom-call(f32[25,8,128]{2,1,0:T(8,128)S(1)} %get-tuple-element.45.c, f32[5,8,8,128]{3,2,1,0:T(8,128)S(1)} %collective-permute-done.7.one, f32[5,8,8,128]{3,2,1,0:T(8,128)S(1)} %collective-permute-done.8.two, ...), custom_call_target="tpu_custom_call" | custom-call | flops 6000000 | bytes 2101248 | tf_op jit(solution)/shard_map/pallas_call | solution.py:348
  44.2 19.4 %all_to_all.10.parts = f32[16,1,128]{2,1,0:T(1,128)S(1)} all-to-all(f32[16,1,128]{2,1,0:T(1,128)S(1)} %get-tuple-element.71), channel_id=1, replica_groups=mesh['tm_0'=4,'tm_1'=8,'tm_2'=2,'lat'=8] {'tm_2','lat'}, dimensions={0} | all-to-all | bytes 16384 | tf_op jit(solution)/shard_map/all_to_all | solution.py:383
  63.6 19.6 %all_to_all.11.refs_0_ = f32[32,1,128]{2,1,0:T(1,128)S(1)} all-to-all(f32[32,1,128]{2,1,0:T(1,128)S(1)} %shard_map.128), channel_id=1, replica_groups=mesh['tm_0'=4,'tm_1'=8,'tm_2'=2,'lat'=8] {'tm_0','tm_1'}, dimensions={0} | all-to-all | bytes 32768 | tf_op jit(solution)/shard_map/all_to_all | solution.py:383
  83.2 0.9 %shard_map.129 = (f32[1,5,8,1024]{3,2,1,0:T(8,128)}, f32[1,5,8,1024]{3,2,1,0:T(8,128)}, f32[1,8,1024]{2,1,0:T(8,128)}) custom-call(f32[32,1,128]{2,1,0:T(1,128)S(1)} %all_to_all.11.refs_0_, f32[5,8,128]{2,1,0:T(8,128)S(1)} %get-tuple-element.59.keep.refs_1_, f32[8,8,8,128]{3,2,1,0:T(8,128)S(1)} %shard_map.121.own.own_c.refs_2_, ...), custom_call_target="tpu_custom_call" | custom-call | flops 4000000 | bytes 1183744 | tf_op jit(solution)/shard_map/pallas_call | solution.py:348
  (1 shorter events, 0.0 us)
Async XLA Ops:
  0.6 6.7 %copy-start.1 = (f32[1,8,1024]{2,1,0:T(8,128)S(1)}, f32[1,8,1024]{2,1,0:T(8,128)}, u32[]{:S(2)}) copy-start(f32[1,8,1024]{2,1,0:T(8,128)} %observed.1) | copy-start | bytes 98308
  0.6 6.7 %copy-start = (f32[5,8,1024]{2,1,0:T(8,128)S(1)}, f32[5,8,1024]{2,1,0:T(8,128)}, u32[]{:S(2)}) copy-start(f32[5,8,1024]{2,1,0:T(8,128)} %background.1) | copy-start | bytes 491524
  0.7 6.7 %copy-start.2 = (f32[5,5]{1,0:T(8,128)S(1)}, f32[5,5]{1,0:T(8,128)}, u32[]{:S(2)}) copy-start(f32[5,5]{1,0:T(8,128)} %coupling.1) | copy-start | bytes 304
  0.7 6.7 %copy-start.3 = (s32[1,8,8]{2,1,0:T(8,128)S(1)}, s32[1,8,8]{2,1,0:T(8,128)}, u32[]{:S(2)}) copy-start(s32[1,8,8]{2,1,0:T(8,128)} %obs_level.1) | copy-start | bytes 772
  0.7 6.7 %copy-start.4 = (s32[1,8,8]{2,1,0:T(8,128)S(1)}, s32[1,8,8]{2,1,0:T(8,128)}, u32[]{:S(2)}) copy-start(s32[1,8,8]{2,1,0:T(8,128)} %huber_class.1) | copy-start | bytes 772
  1.8 5.6 %copy-start.5 = (f32[5]{0:T(128)S(1)}, f32[5]{0:T(128)}, u32[]{:S(2)}) copy-start(f32[5]{0:T(128)} %param.17) | copy-start | bytes 64
  1.8 11.6 %collective-permute-start.1 = (f32[8,8,8,128]{3,2,1,0:T(8,128)S(1)}, f32[8,8,8,128]{3,2,1,0:T(8,128)S(1)}, u32[]{:S(2)}, u32[]{:S(2)}) collective-permute-start(f32[8,8,8,128]{3,2,1,0:T(8,128)S(1)} %shard_map.121.own.own_c.refs_2_), channel_id=1, source_target_pairs={{0,1},{1,0},{2,3},{3,2},{4,5},{5,4},{6,7},{7,6},{8,9},{9,8},{10,11... | collective-permute-start | bytes 786440 | tf_op jit(solution)/shard_map/ppermute | solution.py:378
  6.6 6.8 %collective-permute-start = (f32[8,8,8,128]{3,2,1,0:T(8,128)S(1)}, f32[8,8,8,128]{3,2,1,0:T(8,128)S(1)}, u32[]{:S(2)}, u32[]{:S(2)}) collective-permute-start(f32[8,8,8,128]{3,2,1,0:T(8,128)S(1)} %shard_map.121.own.own_c.refs_2_), channel_id=1, source_target_pairs={{1,2},{2,1},{3,4},{4,3},{5,6},{6,5},{9,10},{10,9},{11,12},{12,11},... | collective-permute-start | bytes 786440 | tf_op jit(solution)/shard_map/ppermute | solution.py:378
  7.5 13.3 %collective-permute-start.4 = (f32[5,8,8,128]{3,2,1,0:T(8,128)S(1)}, f32[5,8,8,128]{3,2,1,0:T(8,128)S(1)}, u32[]{:S(2)}, u32[]{:S(2)}) collective-permute-start(f32[5,8,8,128]{3,2,1,0:T(8,128)S(1)} %get-tuple-element.50), channel_id=1, source_target_pairs={{8,0},{16,8},{24,16},{32,24},{40,32},{48,40},{56,48},{64,56},{72,6... | collective-permute-start | bytes 491528 | tf_op jit(solution)/shard_map/ppermute | solution.py:369
  14.7 6.6 %collective-permute-start.2 = (f32[5,8,8,128]{3,2,1,0:T(8,128)S(1)}, f32[5,8,8,128]{3,2,1,0:T(8,128)S(1)}, u32[]{:S(2)}, u32[]{:S(2)}) collective-permute-start(f32[5,8,8,128]{3,2,1,0:T(8,128)S(1)} %get-tuple-element.48), channel_id=1, source_target_pairs={{8,16},{16,8},{24,32},{32,24},{40,48},{48,40},{56,64},{64,56},{72,... | collective-permute-start | bytes 491528 | tf_op jit(solution)/shard_map/ppermute | solution.py:378
  18.2 3.6 %collective-permute-start.3 = (f32[5,8,8,128]{3,2,1,0:T(8,128)S(1)}, f32[5,8,8,128]{3,2,1,0:T(8,128)S(1)}, u32[]{:S(2)}, u32[]{:S(2)}) collective-permute-start(f32[5,8,8,128]{3,2,1,0:T(8,128)S(1)} %get-tuple-element.49), channel_id=1, source_target_pairs={{0,8},{8,0},{16,24},{24,16},{32,40},{40,32},{48,56},{56,48},{64,72... | collective-permute-start | bytes 491528 | tf_op jit(solution)/shard_map/ppermute | solution.py:378
  22.7 12.2 %collective-permute-start.6 = (f32[5,8,8,128]{3,2,1,0:T(8,128)S(1)}, f32[5,8,8,128]{3,2,1,0:T(8,128)S(1)}, u32[]{:S(2)}, u32[]{:S(2)}) collective-permute-start(f32[5,8,8,128]{3,2,1,0:T(8,128)S(1)} %get-tuple-element.58.g.own.refs_3_), channel_id=1, source_target_pairs={{0,1},{1,0},{2,3},{3,2},{4,5},{5,4},{6,7},{7,6},{8,9},{9,8},{10,11... | collective-permute-start | bytes 491528 | tf_op jit(solution)/shard_map/ppermute | solution.py:378
  30.4 4.4 %collective-permute-start.5 = (f32[5,8,8,128]{3,2,1,0:T(8,128)S(1)}, f32[5,8,8,128]{3,2,1,0:T(8,128)S(1)}, u32[]{:S(2)}, u32[]{:S(2)}) collective-permute-start(f32[5,8,8,128]{3,2,1,0:T(8,128)S(1)} %get-tuple-element.58.g.own.refs_3_), channel_id=1, source_target_pairs={{1,2},{2,1},{3,4},{4,3},{5,6},{6,5},{9,10},{10,9},{11,12},{12,11},... | collective-permute-start | bytes 491528 | tf_op jit(solution)/shard_map/ppermute | solution.py:378
  31.9 10.0 %collective-permute-start.9 = (f32[5,8,8,128]{3,2,1,0:T(8,128)S(1)}, f32[5,8,8,128]{3,2,1,0:T(8,128)S(1)}, u32[]{:S(2)}, u32[]{:S(2)}) collective-permute-start(f32[5,8,8,128]{3,2,1,0:T(8,128)S(1)} %get-tuple-element.68), channel_id=1, source_target_pairs={{8,0},{16,8},{24,16},{32,24},{40,32},{48,40},{56,48},{64,56},{72,6... | collective-permute-start | bytes 491528 | tf_op jit(solution)/shard_map/ppermute | solution.py:369
  36.1 6.8 %collective-permute-start.7 = (f32[5,8,8,128]{3,2,1,0:T(8,128)S(1)}, f32[5,8,8,128]{3,2,1,0:T(8,128)S(1)}, u32[]{:S(2)}, u32[]{:S(2)}) collective-permute-start(f32[5,8,8,128]{3,2,1,0:T(8,128)S(1)} %get-tuple-element.66), channel_id=1, source_target_pairs={{8,16},{16,8},{24,32},{32,24},{40,48},{48,40},{56,64},{64,56},{72,... | collective-permute-start | bytes 491528 | tf_op jit(solution)/shard_map/ppermute | solution.py:378
  39.9 3.3 %collective-permute-start.8 = (f32[5,8,8,128]{3,2,1,0:T(8,128)S(1)}, f32[5,8,8,128]{3,2,1,0:T(8,128)S(1)}, u32[]{:S(2)}, u32[]{:S(2)}) collective-permute-start(f32[5,8,8,128]{3,2,1,0:T(8,128)S(1)} %get-tuple-element.67), channel_id=1, source_target_pairs={{0,8},{8,0},{16,24},{24,16},{32,40},{40,32},{48,56},{56,48},{64,72... | collective-permute-start | bytes 491528 | tf_op jit(solution)/shard_map/ppermute | solution.py:378

commit v4 on v3

--- a/solution.py
+++ b/solution.py
@@ -183,48 +183,65 @@
     return lax.rem(lax.axis_index(axis), 2) == 1
 
 
+def sides(first, second, fields, up, down):
+    below = lax.rem(lax.axis_index("lat") + lax.axis_index(TM[-1]), 2) == 1
+    for k in range(fields):
+        for r in range(ROWS):
+            up[k, r] = jnp.where(below, second[k, r], first[k, r])
+            down[k, r] = jnp.where(below, first[k, r], second[k, r])
+
+
 def forward_kernel(c, first, second, own, up, down, moved, one, two, a, b):
-    upper = odd("lat")
-    for k in range(L + 3):
-        for r in range(ROWS):
-            up[k, r] = jnp.where(upper, second[k, r], first[k, r])
-            down[k, r] = jnp.where(upper, first[k, r], second[k, r])
+    sides(first, second, L + 3, up, down)
     send(c, up, own, down, up, own, down, moved, one, two, a, b)
 
 
-def forward_g_kernel(c, first, second, own, up_c, own_c, down_c, moved, one, two, up, down, a, b):
-    upper = odd("lat")
-    for k in range(L):
-        for r in range(ROWS):
-            up[k, r] = jnp.where(upper, second[k, r], first[k, r])
-            down[k, r] = jnp.where(upper, first[k, r], second[k, r])
+def forward_g_kernel(c, first, second, own, up_c, own_c, down_c, up, down, moved, one, two, a, b):
+    sides(first, second, L, up, down)
     send(c, up, own, down, up_c, own_c, down_c, moved, one, two, a, b)
 
 
 def send(c, up, own, down, up_c, own_c, down_c, moved, one, two, a, b):
     ahead = odd(TM[-1])
+    field, coef = banded(up, own, down, 0), banded(up_c, own_c, down_c, L)
 
     def dst(l, r, v):
-        moved[l, r - H] = v
-        if ROWS <= r < 2 * ROWS:
-            r = r - ROWS
-            halo = up[l, H + r] if r < H else down[l, r - H]
-            one[l, r] = jnp.where(ahead, v, halo)
-            two[l, r] = jnp.where(ahead, halo, v)
-
-    forward(banded(up, own, down, 0), banded(up_c, own_c, down_c, L), c, 3 * ROWS, (a, b), dst)
-
-
-def receive(one, two, after, moved, factor, out):
+        r = r - H
+        moved[l, r] = v
+        halo = up[l, H + r] if r < H else down[l, r - H]
+        one[l, r] = jnp.where(ahead, v, halo)
+        two[l, r] = jnp.where(ahead, halo, v)
+
+    forward(lambda l, r: field(l, r + H), lambda k, r: coef(k, r + H), c, W, (a, b), dst)
+
+
+def halo_kernel(c, up, own, down, up_c, own_c, down_c, moved, a, b):
+    field, coef = banded(up, own, down, 0), banded(up_c, own_c, down_c, L)
+    for first, to in ((0, 0), (ROWS + H, H)):
+
+        def dst(l, r, v, to=to):
+            moved[l, to + r - H] = v
+
+        forward(
+            lambda l, r, first=first: field(l, first + r),
+            lambda k, r, first=first: coef(k, first + r),
+            c,
+            3 * H,
+            (a, b),
+            dst,
+        )
+
+
+def receive(one, two, after, moved, moved_halo, factor, out):
     ahead = odd(TM[-1])
     for l in range(L):
         for r in range(W):
             if H <= r < H + ROWS:
-                v = after[l, r - H]
+                v = after[l, r - H] - moved[l, r - H]
             else:
                 at = r if r < H else r - ROWS
-                v = jnp.where(ahead, one[l, at], two[l, at])
-            out[l, r] = factor * (v - moved[l, r])
+                v = jnp.where(ahead, one[l, at], two[l, at]) - moved_halo[l, at]
+            out[l, r] = factor * v
     return lambda l, r: jnp.where(ahead, two[l, r], one[l, r])
 
 
@@ -236,10 +253,10 @@
 
 
 def back_kernel(
-    c, one, two, after, moved, up, own, down, bg, obs, level, weight, ahead, o1, d, g, a, b
+    c, one, two, after, moved, moved_halo, up, own, down, bg, obs, level, weight, ahead, o1, d, g, a, b
 ):
     some, first = place()
-    came = receive(one, two, after, moved, 0.5 * some, ahead)
+    came = receive(one, two, after, moved, moved_halo, 0.5 * some, ahead)
     for r in range(ROWS):
         o1[r] = 0.5 * weight[r] * (picked(level[r], [own[l, r] for l in range(L)]) - obs[r])
     coef = banded(up, own, down, L)
@@ -265,9 +282,9 @@
 
 
 def back_g_kernel(
-    c, one, two, after, moved, up, own, down, g, level, weight, g0, u, g1, hg, part, ahead, a, b
+    c, one, two, after, moved, moved_halo, up, own, down, g, level, weight, g0, u, g1, hg, part, ahead, a, b
 ):
-    came = receive(one, two, after, moved, place()[0], ahead)
+    came = receive(one, two, after, moved, moved_halo, place()[0], ahead)
     for r in range(ROWS):
         hg[r] = weight[r] * picked(level[r], [g[l, r] for l in range(L)])
     coef = banded(up, own, down, L)
@@ -369,13 +386,25 @@
     return lax.ppermute(x, axis, [(i, i + by) for i in range(count) if 0 <= i + by < count])
 
 
-def swapped(*args):
-    *arrays, axis = args
-    count = lax.axis_size(axis)
+def both_ways(lows):
+    return [p for i in lows for p in ((i, i + 1), (i + 1, i))]
+
+
+def swapped(one, two):
+    count = lax.axis_size(TM)
+    return [
+        lax.ppermute(x, TM, both_ways(range(start, count - 1, 2))) for x, start in ((one, 1), (two, 0))
+    ]
+
+
+def swapped_rows(x):
+    cores, count = lax.axis_size(TM[-1]), lax.axis_size("lat")
     out = []
-    for x, start in zip((arrays[0], arrays[-1]), (1, 0)):
-        lows = range(start, count - 1, 2)
-        out.append(lax.ppermute(x, axis, [p for i in lows for p in ((i, i + 1), (i + 1, i))]))
+    for turn in range(2):
+        lows = [
+            core * count + i for core in range(cores) for i in range((core + turn + 1) % 2, count - 1, 2)
+        ]
+        out.append(lax.ppermute(x, (TM[-1], "lat"), both_ways(lows)))
     return out
 
 
@@ -389,7 +418,7 @@
     band, wide = rows_of(L, ROWS), rows_of(L, W)
     whole = (L, ROWS, 8 * TILE)
     cells = (ROWS, *ROW)
-    two, two_w = [rows_of(L, 3 * ROWS)] * 2, [wide] * 2
+    two_w = [wide] * 2
     count = float(L * ROWS * 8 * TILE * lax.axis_size(TM) * lax.axis_size("lat"))
     (own,) = call(
         pack_kernel,
@@ -397,7 +426,7 @@
         [whole, (3, *whole[1:]), pltpu.SemaphoreType.DMA((4,))],
         far_in=True,
     )(x_init, diff_lon, diff_lat, drift)
-    first, second = swapped(own, "lat")
+    first, second = swapped_rows(own)
     x, bg, obs, c, keep, level, weight = call(
         aside_kernel, [band, band, cells, (L * L, *ROW), (L, *ROW), cells, cells]
     )(own, background, observed, coupling, model_var[None], obs_level, huber_class)
@@ -407,28 +436,33 @@
     )
 
     three = rows_of(L + 3, ROWS)
-    up, down, moved, *sent = call(forward_kernel, [three, three, wide, band, band], two, 2.0)(
+    short = [rows_of(L, 3 * H)] * 2
+    up, down, moved, *sent = call(forward_kernel, [three, three, band, band, band], two_w)(
         c, first, second, own
     )
+    swaps = swapped(*sent)
+    (moved_halo,) = call(halo_kernel, [band], short)(c, up, own, down, up, own, down)
     ahead, o1, d, g = call(back_kernel, [wide, cells, band, band], two_w, 1.5)(
-        c, *swapped(*sent, TM), after, moved, up, own, down, bg, obs, level, weight
-    )
-
-    first, second = swapped(g, "lat")
+        c, *swaps, after, moved, moved_halo, up, own, down, bg, obs, level, weight
+    )
+
+    first, second = swapped_rows(g)
     g0, g_copy = call(still_kernel, [band, band], two_w, 1.5)(
         c, keep, d, ahead, up, own, down, level, o1, g
     )
     after_g = shifted(g_copy, TM, -1)
     first, second, g0 = lax.optimization_barrier((first, second, g0))
-    moved_g, *sent = call(forward_g_kernel, [wide, band, band], [band, band] + two, 2.0)(
+    up_g, down_g, moved_g, *sent = call(forward_g_kernel, [band] * 5, two_w)(
         c, first, second, g, up, own, down
     )
+    swaps = swapped(*sent)
+    (moved_g_halo,) = call(halo_kernel, [band], short)(c, up_g, g, down_g, up, own, down)
     u, g1, hg, part = call(
         back_g_kernel,
         [band, band, cells, (lax.axis_size(NEAR), 1, TILE)],
         [wide] + two_w,
         1.5,
-    )(c, *swapped(*sent, TM), after_g, moved_g, up, own, down, g, level, weight, g0)
+    )(c, *swaps, after_g, moved_g, moved_g_halo, up, own, down, g, level, weight, g0)
     (part,) = call(again_kernel, [(lax.axis_size(FAR), 1, TILE)], us=0.1)(exchanged(part, NEAR))
     part = exchanged(part, FAR)
 

time: 84.6 us -> 82.1 us (0.970)
  starting transfers between devices: 34 us -> 29.9 us
  waiting for transfers between devices: 2.96 us -> 5.49 us
  blocking collectives: 39 us -> 37.3 us
    ppermute x2, starting transfers between devices: 8.22 us -> 4.47 us  [shifted(): lax.ppermute(x, axis, [(i, i + by) for i in range(count) if 0 <= i + by <...]
    ppermute x8, waiting for transfers between devices: 2.95 us -> 5.48 us  [the longest x4 3.19 us: swapped_rows(): out.append(lax.ppermute(x, (TM[-1], 'lat'), both_ways(lows)))]
    all_to_all x2, blocking collectives: 39 us -> 37.3 us  [exchanged(): return lax.all_to_all(x, axis, 0, 0, tiled=True)]
    pallas_call x9 -> x11, Pallas kernels: 7.31 us -> 8.08 us  [run(): pl.pallas_call(kernel, out_shape=[jax.ShapeDtypeStruct(s, jnp.float32) fo...]
  transfers between devices with their start and end apart: 10 -> 10, of which waited for: 5 -> 4; matrix products, arithmetic and copies ran while one was open for 0% -> 0% of each run, Pallas kernels for 4% -> 5%
where the time goes in v4:
time: 82.1 us; the launch traced here: 81.7 us
  blocking collectives  37.3 us (45%)
  starting transfers between devices  29.9 us (36%)
  Pallas kernels  8.08 us (10%)
  waiting for transfers between devices  5.49 us (7%)
  between operations  0.88 us (1%)
    all_to_all x2, blocking collectives, exchanged(): return lax.all_to_all(x, axis, 0, 0, tiled=True)  37.3 us
    ppermute x4, starting transfers between devices, swapped_rows(): out.append(lax.ppermute(x, (TM[-1], 'lat'), both_ways(lows)))  16 us
    ppermute x4, starting transfers between devices, swapped(): lax.ppermute(x, TM, both_ways(range(start, count - 1, 2)))  9.43 us
    pallas_call x11, Pallas kernels, run(): pl.pallas_call(kernel, out_shape=[jax.ShapeDtypeStruct(s, jnp.float32) fo...  8.08 us
    ppermute x2, starting transfers between devices, shifted(): lax.ppermute(x, axis, [(i, i + by) for i in range(count) if 0 <= i + by <...  4.47 us
    ppermute x4, waiting for transfers between devices, swapped_rows(): out.append(lax.ppermute(x, (TM[-1], 'lat'), both_ways(lows)))  3.19 us
    ppermute x4, waiting for transfers between devices, swapped(): lax.ppermute(x, TM, both_ways(range(start, count - 1, 2)))  2.29 us
  transfers between devices with their start and end apart: 10, of which 4 were waited for; matrix products, arithmetic and copies ran while one was open for 0% of the time, Pallas kernels for 5%

profile of v4, /device:TPU:1, one launch (start us, length us, event | category | flops | bytes accessed | tf_op | source)
XLA Modules:
  0.0 81.7 jit_solution(14432254259092533869)
XLA Ops:
  0.6 0.0 copy-start.1
  0.6 0.0 copy-start
  0.7 0.0 copy-start.2
  0.7 0.0 copy-start.3
  0.7 0.0 copy-start.4
  0.7 1.1 %shard_map.121.own.own_c.refs_2_ = f32[8,8,8,128]{3,2,1,0:T(8,128)S(1)} custom-call(f32[1,5,8,1024]{3,2,1,0:T(8,128)} %x_far.1, f32[1,8,1024]{2,1,0:T(8,128)} %kx_far.1, f32[1,8,1024]{2,1,0:T(8,128)} %ky_far.1, f32[1,8,1024]{2,1,0:T(8,128)} %ux_far.1), custom_call_target="tpu_custom_call" | custom-call | flops 4000000 | bytes 262144 | tf_op jit(solution)/shard_map/pallas_call | solution.py:365
  1.8 0.0 copy-start.5
  1.8 0.7 collective-permute-start.1
  2.5 8.2 %collective-permute-start = (f32[8,8,8,128]{3,2,1,0:T(8,128)S(1)}, f32[8,8,8,128]{3,2,1,0:T(8,128)S(1)}, u32[]{:S(2)}, u32[]{:S(2)}) collective-permute-start(f32[8,8,8,128]{3,2,1,0:T(8,128)S(1)} %shard_map.121.own.own_c.refs_2_), channel_id=1, source_target_pairs={{1,2},{2,1},{3,4},{4,3},{5,6},{6,5},{8,9},{9,8},{10,11},{11,10},{1... | collective-permute-start | bytes 786440 | tf_op jit(solution)/shard_map/ppermute | solution.py:407
  10.6 0.0 copy-done.1
  10.6 0.0 copy-done
  10.6 0.0 copy-done.2
  10.6 0.0 copy-done.3
  10.7 0.0 copy-done.4
  10.7 0.0 copy-done.5
  10.7 0.1 shard_map.122
  10.8 2.6 %collective-permute-start.4 = (f32[5,8,8,128]{3,2,1,0:T(8,128)S(1)}, f32[5,8,8,128]{3,2,1,0:T(8,128)S(1)}, u32[]{:S(2)}, u32[]{:S(2)}) collective-permute-start(f32[5,8,8,128]{3,2,1,0:T(8,128)S(1)} %get-tuple-element.52), channel_id=1, source_target_pairs={{8,0},{16,8},{24,16},{32,24},{40,32},{48,40},{56,48},{64,56},{72,6... | collective-permute-start | bytes 491528 | tf_op jit(solution)/shard_map/ppermute | solution.py:386
  13.4 0.0 collective-permute-done.1.second
  13.4 3.2 %collective-permute-done.first = f32[8,8,8,128]{3,2,1,0:T(8,128)S(1)} collective-permute-done((f32[8,8,8,128]{3,2,1,0:T(8,128)S(1)}, f32[8,8,8,128]{3,2,1,0:T(8,128)S(1)}, u32[]{:S(2)}, u32[]{:S(2)}) %collective-permute-start) | collective-permute-done | bytes 262176 | tf_op jit(solution)/shard_map/ppermute | solution.py:407
  16.6 0.8 shard_map.123
  17.4 1.9 %collective-permute-start.2 = (f32[5,8,8,128]{3,2,1,0:T(8,128)S(1)}, f32[5,8,8,128]{3,2,1,0:T(8,128)S(1)}, u32[]{:S(2)}, u32[]{:S(2)}) collective-permute-start(f32[5,8,8,128]{3,2,1,0:T(8,128)S(1)} %get-tuple-element.50), channel_id=1, source_target_pairs={{8,16},{16,8},{24,32},{32,24},{40,48},{48,40},{56,64},{64,56},{72,... | collective-permute-start | bytes 491528 | tf_op jit(solution)/shard_map/ppermute | solution.py:396
  19.3 1.9 %collective-permute-start.3 = (f32[5,8,8,128]{3,2,1,0:T(8,128)S(1)}, f32[5,8,8,128]{3,2,1,0:T(8,128)S(1)}, u32[]{:S(2)}, u32[]{:S(2)}) collective-permute-start(f32[5,8,8,128]{3,2,1,0:T(8,128)S(1)} %get-tuple-element.51), channel_id=1, source_target_pairs={{0,8},{8,0},{16,24},{24,16},{32,40},{40,32},{48,56},{56,48},{64,72... | collective-permute-start | bytes 491528 | tf_op jit(solution)/shard_map/ppermute | solution.py:396
  21.2 0.9 %shard_map.124.moved_halo = f32[5,8,8,128]{3,2,1,0:T(8,128)S(1)} custom-call(f32[25,8,128]{2,1,0:T(8,128)S(1)} %get-tuple-element.47.c, f32[8,8,8,128]{3,2,1,0:T(8,128)S(1)} %get-tuple-element.54.up.up_c, f32[8,8,8,128]{3,2,1,0:T(8,128)S(1)} %shard_map.121.own.own_c.refs_2_, f32[8,8,8,128]{3,2,1,0:T(8,128)S(1)} %get-tuple-element.55.down.down_c, ...), custom_call_target="tpu_custom_call" | custom-call | flops 4000000 | bytes 1675264 | tf_op jit(solution)/shard_map/pallas_call | solution.py:365
  22.1 0.0 collective-permute-done.4.after
  22.2 1.8 %collective-permute-done.2.one = f32[5,8,8,128]{3,2,1,0:T(8,128)S(1)} collective-permute-done((f32[5,8,8,128]{3,2,1,0:T(8,128)S(1)}, f32[5,8,8,128]{3,2,1,0:T(8,128)S(1)}, u32[]{:S(2)}, u32[]{:S(2)}) %collective-permute-start.2) | collective-permute-done | bytes 163872 | tf_op jit(solution)/shard_map/ppermute | solution.py:396
  24.0 0.0 collective-permute-done.3.two
  24.0 0.9 %shard_map.125 = (f32[5,16,8,128]{3,2,1,0:T(8,128)S(1)}, f32[8,8,128]{2,1,0:T(8,128)S(1)}, f32[5,8,8,128]{3,2,1,0:T(8,128)S(1)}, f32[5,8,8,128]{3,2,1,0:T(8,128)S(1)}) custom-call(f32[25,8,128]{2,1,0:T(8,128)S(1)} %get-tuple-element.47.c, f32[5,8,8,128]{3,2,1,0:T(8,128)S(1)} %collective-permute-done.2.one, f32[5,8,8,128]{3,2,1,0:T(8,128)S(1)} %collective-permute-done.3.two, ...), custom_call_target="tpu_custom_call" | custom-call | flops 6000000 | bytes 1970176 | tf_op jit(solution)/shard_map/pallas_call | solution.py:365
  24.9 0.7 collective-permute-start.6
  25.5 6.5 %collective-permute-start.5 = (f32[5,8,8,128]{3,2,1,0:T(8,128)S(1)}, f32[5,8,8,128]{3,2,1,0:T(8,128)S(1)}, u32[]{:S(2)}, u32[]{:S(2)}) collective-permute-start(f32[5,8,8,128]{3,2,1,0:T(8,128)S(1)} %get-tuple-element.60.g.own.refs_3_), channel_id=1, source_target_pairs={{1,2},{2,1},{3,4},{4,3},{5,6},{6,5},{8,9},{9,8},{10,11},{11,10},{1... | collective-permute-start | bytes 491528 | tf_op jit(solution)/shard_map/ppermute | solution.py:407
  32.0 0.8 shard_map.126
  32.8 1.9 %collective-permute-start.9 = (f32[5,8,8,128]{3,2,1,0:T(8,128)S(1)}, f32[5,8,8,128]{3,2,1,0:T(8,128)S(1)}, u32[]{:S(2)}, u32[]{:S(2)}) collective-permute-start(f32[5,8,8,128]{3,2,1,0:T(8,128)S(1)} %get-tuple-element.70), channel_id=1, source_target_pairs={{8,0},{16,8},{24,16},{32,24},{40,32},{48,40},{56,48},{64,56},{72,6... | collective-permute-start | bytes 491528 | tf_op jit(solution)/shard_map/ppermute | solution.py:386
  34.7 0.0 collective-permute-done.6.second
  34.7 0.0 collective-permute-done.5.first
  34.8 0.8 shard_map.127
  35.5 3.6 %collective-permute-start.7 = (f32[5,8,8,128]{3,2,1,0:T(8,128)S(1)}, f32[5,8,8,128]{3,2,1,0:T(8,128)S(1)}, u32[]{:S(2)}, u32[]{:S(2)}) collective-permute-start(f32[5,8,8,128]{3,2,1,0:T(8,128)S(1)} %get-tuple-element.68), channel_id=1, source_target_pairs={{8,16},{16,8},{24,32},{32,24},{40,48},{48,40},{56,64},{64,56},{72,... | collective-permute-start | bytes 491528 | tf_op jit(solution)/shard_map/ppermute | solution.py:396
  39.2 1.9 %collective-permute-start.8 = (f32[5,8,8,128]{3,2,1,0:T(8,128)S(1)}, f32[5,8,8,128]{3,2,1,0:T(8,128)S(1)}, u32[]{:S(2)}, u32[]{:S(2)}) collective-permute-start(f32[5,8,8,128]{3,2,1,0:T(8,128)S(1)} %get-tuple-element.69), channel_id=1, source_target_pairs={{0,8},{8,0},{16,24},{24,16},{32,40},{40,32},{48,56},{56,48},{64,72... | collective-permute-start | bytes 491528 | tf_op jit(solution)/shard_map/ppermute | solution.py:396
  41.1 0.9 %shard_map.128.moved_halo = f32[5,8,8,128]{3,2,1,0:T(8,128)S(1)} custom-call(f32[25,8,128]{2,1,0:T(8,128)S(1)} %get-tuple-element.47.c, f32[5,8,8,128]{3,2,1,0:T(8,128)S(1)} %get-tuple-element.72.up, f32[5,8,8,128]{3,2,1,0:T(8,128)S(1)} %get-tuple-element.60.g.own.refs_3_, f32[5,8,8,128]{3,2,1,0:T(8,128)S(1)} %get-tuple-element.73.down, ...), custom_call_target="tpu_custom_call" | custom-call | flops 4000000 | bytes 1380352 | tf_op jit(solution)/shard_map/pallas_call | solution.py:365
  42.0 0.0 collective-permute-done.9.after
  42.0 0.1 collective-permute-done.7.one
  42.2 0.3 collective-permute-done.8.two
  42.5 0.9 %shard_map.129 = (f32[5,8,8,128]{3,2,1,0:T(8,128)S(1)}, f32[5,8,8,128]{3,2,1,0:T(8,128)S(1)}, f32[8,8,128]{2,1,0:T(8,128)S(1)}, f32[16,1,128]{2,1,0:T(1,128)S(1)}) custom-call(f32[25,8,128]{2,1,0:T(8,128)S(1)} %get-tuple-element.47.c, f32[5,8,8,128]{3,2,1,0:T(8,128)S(1)} %collective-permute-done.7.one, f32[5,8,8,128]{3,2,1,0:T(8,128)S(1)} %collective-permute-done.8.two, ...), custom_call_target="tpu_custom_call" | custom-call | flops 6000000 | bytes 2101248 | tf_op jit(solution)/shard_map/pallas_call | solution.py:365
  43.4 16.7 %all_to_all.10.parts = f32[16,1,128]{2,1,0:T(1,128)S(1)} all-to-all(f32[16,1,128]{2,1,0:T(1,128)S(1)} %get-tuple-element.75), channel_id=1, replica_groups=mesh['tm_0'=4,'tm_1'=8,'tm_2'=2,'lat'=8] {'tm_2','lat'}, dimensions={0} | all-to-all | bytes 16384 | tf_op jit(solution)/shard_map/all_to_all | solution.py:412
  60.1 20.6 %all_to_all.11.refs_0_ = f32[32,1,128]{2,1,0:T(1,128)S(1)} all-to-all(f32[32,1,128]{2,1,0:T(1,128)S(1)} %shard_map.130), channel_id=1, replica_groups=mesh['tm_0'=4,'tm_1'=8,'tm_2'=2,'lat'=8] {'tm_0','tm_1'}, dimensions={0} | all-to-all | bytes 32768 | tf_op jit(solution)/shard_map/all_to_all | solution.py:412
  80.7 0.9 %shard_map.131 = (f32[1,5,8,1024]{3,2,1,0:T(8,128)}, f32[1,5,8,1024]{3,2,1,0:T(8,128)}, f32[1,8,1024]{2,1,0:T(8,128)}) custom-call(f32[32,1,128]{2,1,0:T(1,128)S(1)} %all_to_all.11.refs_0_, f32[5,8,128]{2,1,0:T(8,128)S(1)} %get-tuple-element.61.keep.refs_1_, f32[8,8,8,128]{3,2,1,0:T(8,128)S(1)} %shard_map.121.own.own_c.refs_2_, ...), custom_call_target="tpu_custom_call" | custom-call | flops 4000000 | bytes 1183744 | tf_op jit(solution)/shard_map/pallas_call | solution.py:365
  (1 shorter events, 0.0 us)
Async XLA Ops:
  0.6 10.0 %copy-start.1 = (f32[1,8,1024]{2,1,0:T(8,128)S(1)}, f32[1,8,1024]{2,1,0:T(8,128)}, u32[]{:S(2)}) copy-start(f32[1,8,1024]{2,1,0:T(8,128)} %observed.1) | copy-start | bytes 98308
  0.6 10.0 %copy-start = (f32[5,8,1024]{2,1,0:T(8,128)S(1)}, f32[5,8,1024]{2,1,0:T(8,128)}, u32[]{:S(2)}) copy-start(f32[5,8,1024]{2,1,0:T(8,128)} %background.1) | copy-start | bytes 491524
  0.7 10.0 %copy-start.2 = (f32[5,5]{1,0:T(8,128)S(1)}, f32[5,5]{1,0:T(8,128)}, u32[]{:S(2)}) copy-start(f32[5,5]{1,0:T(8,128)} %coupling.1) | copy-start | bytes 304
  0.7 10.0 %copy-start.3 = (s32[1,8,8]{2,1,0:T(8,128)S(1)}, s32[1,8,8]{2,1,0:T(8,128)}, u32[]{:S(2)}) copy-start(s32[1,8,8]{2,1,0:T(8,128)} %obs_level.1) | copy-start | bytes 772
  0.7 10.0 %copy-start.4 = (s32[1,8,8]{2,1,0:T(8,128)S(1)}, s32[1,8,8]{2,1,0:T(8,128)}, u32[]{:S(2)}) copy-start(s32[1,8,8]{2,1,0:T(8,128)} %huber_class.1) | copy-start | bytes 772
  1.8 8.9 %copy-start.5 = (f32[5]{0:T(128)S(1)}, f32[5]{0:T(128)}, u32[]{:S(2)}) copy-start(f32[5]{0:T(128)} %param.17) | copy-start | bytes 64
  1.8 11.6 %collective-permute-start.1 = (f32[8,8,8,128]{3,2,1,0:T(8,128)S(1)}, f32[8,8,8,128]{3,2,1,0:T(8,128)S(1)}, u32[]{:S(2)}, u32[]{:S(2)}) collective-permute-start(f32[8,8,8,128]{3,2,1,0:T(8,128)S(1)} %shard_map.121.own.own_c.refs_2_), channel_id=1, source_target_pairs={{0,1},{1,0},{2,3},{3,2},{4,5},{5,4},{6,7},{7,6},{9,10},{10,9},{11,... | collective-permute-start | bytes 786440 | tf_op jit(solution)/shard_map/ppermute | solution.py:407
  2.5 14.1 %collective-permute-start = (f32[8,8,8,128]{3,2,1,0:T(8,128)S(1)}, f32[8,8,8,128]{3,2,1,0:T(8,128)S(1)}, u32[]{:S(2)}, u32[]{:S(2)}) collective-permute-start(f32[8,8,8,128]{3,2,1,0:T(8,128)S(1)} %shard_map.121.own.own_c.refs_2_), channel_id=1, source_target_pairs={{1,2},{2,1},{3,4},{4,3},{5,6},{6,5},{8,9},{9,8},{10,11},{11,10},{1... | collective-permute-start | bytes 786440 | tf_op jit(solution)/shard_map/ppermute | solution.py:407
  10.8 11.3 %collective-permute-start.4 = (f32[5,8,8,128]{3,2,1,0:T(8,128)S(1)}, f32[5,8,8,128]{3,2,1,0:T(8,128)S(1)}, u32[]{:S(2)}, u32[]{:S(2)}) collective-permute-start(f32[5,8,8,128]{3,2,1,0:T(8,128)S(1)} %get-tuple-element.52), channel_id=1, source_target_pairs={{8,0},{16,8},{24,16},{32,24},{40,32},{48,40},{56,48},{64,56},{72,6... | collective-permute-start | bytes 491528 | tf_op jit(solution)/shard_map/ppermute | solution.py:386
  17.4 6.6 %collective-permute-start.2 = (f32[5,8,8,128]{3,2,1,0:T(8,128)S(1)}, f32[5,8,8,128]{3,2,1,0:T(8,128)S(1)}, u32[]{:S(2)}, u32[]{:S(2)}) collective-permute-start(f32[5,8,8,128]{3,2,1,0:T(8,128)S(1)} %get-tuple-element.50), channel_id=1, source_target_pairs={{8,16},{16,8},{24,32},{32,24},{40,48},{48,40},{56,64},{64,56},{72,... | collective-permute-start | bytes 491528 | tf_op jit(solution)/shard_map/ppermute | solution.py:396
  19.3 4.7 %collective-permute-start.3 = (f32[5,8,8,128]{3,2,1,0:T(8,128)S(1)}, f32[5,8,8,128]{3,2,1,0:T(8,128)S(1)}, u32[]{:S(2)}, u32[]{:S(2)}) collective-permute-start(f32[5,8,8,128]{3,2,1,0:T(8,128)S(1)} %get-tuple-element.51), channel_id=1, source_target_pairs={{0,8},{8,0},{16,24},{24,16},{32,40},{40,32},{48,56},{56,48},{64,72... | collective-permute-start | bytes 491528 | tf_op jit(solution)/shard_map/ppermute | solution.py:396
  24.9 9.9 %collective-permute-start.6 = (f32[5,8,8,128]{3,2,1,0:T(8,128)S(1)}, f32[5,8,8,128]{3,2,1,0:T(8,128)S(1)}, u32[]{:S(2)}, u32[]{:S(2)}) collective-permute-start(f32[5,8,8,128]{3,2,1,0:T(8,128)S(1)} %get-tuple-element.60.g.own.refs_3_), channel_id=1, source_target_pairs={{0,1},{1,0},{2,3},{3,2},{4,5},{5,4},{6,7},{7,6},{9,10},{10,9},{11,... | collective-permute-start | bytes 491528 | tf_op jit(solution)/shard_map/ppermute | solution.py:407
  25.5 9.2 %collective-permute-start.5 = (f32[5,8,8,128]{3,2,1,0:T(8,128)S(1)}, f32[5,8,8,128]{3,2,1,0:T(8,128)S(1)}, u32[]{:S(2)}, u32[]{:S(2)}) collective-permute-start(f32[5,8,8,128]{3,2,1,0:T(8,128)S(1)} %get-tuple-element.60.g.own.refs_3_), channel_id=1, source_target_pairs={{1,2},{2,1},{3,4},{4,3},{5,6},{6,5},{8,9},{9,8},{10,11},{11,10},{1... | collective-permute-start | bytes 491528 | tf_op jit(solution)/shard_map/ppermute | solution.py:407
  32.8 9.2 %collective-permute-start.9 = (f32[5,8,8,128]{3,2,1,0:T(8,128)S(1)}, f32[5,8,8,128]{3,2,1,0:T(8,128)S(1)}, u32[]{:S(2)}, u32[]{:S(2)}) collective-permute-start(f32[5,8,8,128]{3,2,1,0:T(8,128)S(1)} %get-tuple-element.70), channel_id=1, source_target_pairs={{8,0},{16,8},{24,16},{32,24},{40,32},{48,40},{56,48},{64,56},{72,6... | collective-permute-start | bytes 491528 | tf_op jit(solution)/shard_map/ppermute | solution.py:386
  35.5 6.6 %collective-permute-start.7 = (f32[5,8,8,128]{3,2,1,0:T(8,128)S(1)}, f32[5,8,8,128]{3,2,1,0:T(8,128)S(1)}, u32[]{:S(2)}, u32[]{:S(2)}) collective-permute-start(f32[5,8,8,128]{3,2,1,0:T(8,128)S(1)} %get-tuple-element.68), channel_id=1, source_target_pairs={{8,16},{16,8},{24,32},{32,24},{40,48},{48,40},{56,64},{64,56},{72,... | collective-permute-start | bytes 491528 | tf_op jit(solution)/shard_map/ppermute | solution.py:396
  39.2 3.3 %collective-permute-start.8 = (f32[5,8,8,128]{3,2,1,0:T(8,128)S(1)}, f32[5,8,8,128]{3,2,1,0:T(8,128)S(1)}, u32[]{:S(2)}, u32[]{:S(2)}) collective-permute-start(f32[5,8,8,128]{3,2,1,0:T(8,128)S(1)} %get-tuple-element.69), channel_id=1, source_target_pairs={{0,8},{8,0},{16,24},{24,16},{32,40},{40,32},{48,56},{56,48},{64,72... | collective-permute-start | bytes 491528 | tf_op jit(solution)/shard_map/ppermute | solution.py:396

commit v5 on v4

--- a/solution.py
+++ b/solution.py
@@ -408,8 +408,12 @@
     return out
 
 
-def exchanged(x, axis):
-    return lax.all_to_all(x, axis, 0, 0, tiled=True)
+def exchanged(x, axes):
+    order = [0]
+    for axis in axes:
+        n = lax.axis_size(axis)
+        order = [n * i + (k + n // 2) % n for i in order for k in range(n)]
+    return lax.all_to_all(x, axes, 0, 0, axis_index_groups=[order], tiled=True)
 
 
 def on_device(

time: 82.1 us -> 74 us (0.901)
  blocking collectives: 37.3 us -> 28.6 us
    all_to_all x2, blocking collectives: 37.3 us -> 28.6 us  [exchanged(): return lax.all_to_all(x, axes, 0, 0, axis_index_groups=[order], tiled=True)]
  transfers between devices with their start and end apart: 10 -> 10, of which waited for: 4 -> 4; matrix products, arithmetic and copies ran while one was open for 0% -> 0% of each run, Pallas kernels for 5% -> 6%
where the time goes in v5:
time: 74 us; the launch traced here: 73 us
  starting transfers between devices  29.9 us (40%)
  blocking collectives  28.6 us (39%)
  Pallas kernels  8.08 us (11%)
  waiting for transfers between devices  5.49 us (7%)
  between operations  0.88 us (1%)
    all_to_all x2, blocking collectives, exchanged(): return lax.all_to_all(x, axes, 0, 0, axis_index_groups=[order], tiled=True)  28.6 us
    ppermute x4, starting transfers between devices, swapped_rows(): out.append(lax.ppermute(x, (TM[-1], 'lat'), both_ways(lows)))  16 us
    ppermute x4, starting transfers between devices, swapped(): lax.ppermute(x, TM, both_ways(range(start, count - 1, 2)))  9.43 us
    pallas_call x11, Pallas kernels, run(): pl.pallas_call(kernel, out_shape=[jax.ShapeDtypeStruct(s, jnp.float32) fo...  8.08 us
    ppermute x2, starting transfers between devices, shifted(): lax.ppermute(x, axis, [(i, i + by) for i in range(count) if 0 <= i + by <...  4.47 us
    ppermute x4, waiting for transfers between devices, swapped_rows(): out.append(lax.ppermute(x, (TM[-1], 'lat'), both_ways(lows)))  3.19 us
    ppermute x4, waiting for transfers between devices, swapped(): lax.ppermute(x, TM, both_ways(range(start, count - 1, 2)))  2.29 us
  transfers between devices with their start and end apart: 10, of which 4 were waited for; matrix products, arithmetic and copies ran while one was open for 0% of the time, Pallas kernels for 6%

profile of v5, /device:TPU:1, one launch (start us, length us, event | category | flops | bytes accessed | tf_op | source)
XLA Modules:
  0.0 73.0 jit_solution(10907487450464266978)
XLA Ops:
  0.6 0.0 copy-start.1
  0.6 0.0 copy-start
  0.7 0.0 copy-start.2
  0.7 0.0 copy-start.3
  0.7 0.0 copy-start.4
  0.7 1.1 %shard_map.121.own.own_c.refs_2_ = f32[8,8,8,128]{3,2,1,0:T(8,128)S(1)} custom-call(f32[1,5,8,1024]{3,2,1,0:T(8,128)} %x_far.1, f32[1,8,1024]{2,1,0:T(8,128)} %kx_far.1, f32[1,8,1024]{2,1,0:T(8,128)} %ky_far.1, f32[1,8,1024]{2,1,0:T(8,128)} %ux_far.1), custom_call_target="tpu_custom_call" | custom-call | flops 4000000 | bytes 262144 | tf_op jit(solution)/shard_map/pallas_call | solution.py:365
  1.8 0.0 copy-start.5
  1.8 0.7 collective-permute-start.1
  2.5 8.2 %collective-permute-start = (f32[8,8,8,128]{3,2,1,0:T(8,128)S(1)}, f32[8,8,8,128]{3,2,1,0:T(8,128)S(1)}, u32[]{:S(2)}, u32[]{:S(2)}) collective-permute-start(f32[8,8,8,128]{3,2,1,0:T(8,128)S(1)} %shard_map.121.own.own_c.refs_2_), channel_id=1, source_target_pairs={{1,2},{2,1},{3,4},{4,3},{5,6},{6,5},{8,9},{9,8},{10,11},{11,10},{1... | collective-permute-start | bytes 786440 | tf_op jit(solution)/shard_map/ppermute | solution.py:407
  10.6 0.0 copy-done.1
  10.6 0.0 copy-done
  10.6 0.0 copy-done.2
  10.6 0.0 copy-done.3
  10.7 0.0 copy-done.4
  10.7 0.0 copy-done.5
  10.7 0.1 shard_map.122
  10.8 2.6 %collective-permute-start.4 = (f32[5,8,8,128]{3,2,1,0:T(8,128)S(1)}, f32[5,8,8,128]{3,2,1,0:T(8,128)S(1)}, u32[]{:S(2)}, u32[]{:S(2)}) collective-permute-start(f32[5,8,8,128]{3,2,1,0:T(8,128)S(1)} %get-tuple-element.52), channel_id=1, source_target_pairs={{8,0},{16,8},{24,16},{32,24},{40,32},{48,40},{56,48},{64,56},{72,6... | collective-permute-start | bytes 491528 | tf_op jit(solution)/shard_map/ppermute | solution.py:386
  13.4 0.0 collective-permute-done.1.second
  13.4 3.2 %collective-permute-done.first = f32[8,8,8,128]{3,2,1,0:T(8,128)S(1)} collective-permute-done((f32[8,8,8,128]{3,2,1,0:T(8,128)S(1)}, f32[8,8,8,128]{3,2,1,0:T(8,128)S(1)}, u32[]{:S(2)}, u32[]{:S(2)}) %collective-permute-start) | collective-permute-done | bytes 262176 | tf_op jit(solution)/shard_map/ppermute | solution.py:407
  16.6 0.8 %shard_map.123 = (f32[8,8,8,128]{3,2,1,0:T(8,128)S(1)}, f32[8,8,8,128]{3,2,1,0:T(8,128)S(1)}, f32[5,8,8,128]{3,2,1,0:T(8,128)S(1)}, f32[5,8,8,128]{3,2,1,0:T(8,128)S(1)}, f32[5,8,8,128]{3,2,1,0:T(8,128)S(1)}) custom-call(f32[25,8,128]{2,1,0:T(8,128)S(1)} %get-tuple-element.47.c, f32[8,8,8,128]{3,2,1,0:T(8,128)S(1)} %collective-permute-done.first, ...), custom_call_target="tpu_custom_call" | custom-call | flops 4000000 | bytes 888832 | tf_op jit(solution)/shard_map/pallas_call | solution.py:365
  17.4 1.9 %collective-permute-start.2 = (f32[5,8,8,128]{3,2,1,0:T(8,128)S(1)}, f32[5,8,8,128]{3,2,1,0:T(8,128)S(1)}, u32[]{:S(2)}, u32[]{:S(2)}) collective-permute-start(f32[5,8,8,128]{3,2,1,0:T(8,128)S(1)} %get-tuple-element.50), channel_id=1, source_target_pairs={{8,16},{16,8},{24,32},{32,24},{40,48},{48,40},{56,64},{64,56},{72,... | collective-permute-start | bytes 491528 | tf_op jit(solution)/shard_map/ppermute | solution.py:396
  19.3 1.9 %collective-permute-start.3 = (f32[5,8,8,128]{3,2,1,0:T(8,128)S(1)}, f32[5,8,8,128]{3,2,1,0:T(8,128)S(1)}, u32[]{:S(2)}, u32[]{:S(2)}) collective-permute-start(f32[5,8,8,128]{3,2,1,0:T(8,128)S(1)} %get-tuple-element.51), channel_id=1, source_target_pairs={{0,8},{8,0},{16,24},{24,16},{32,40},{40,32},{48,56},{56,48},{64,72... | collective-permute-start | bytes 491528 | tf_op jit(solution)/shard_map/ppermute | solution.py:396
  21.2 0.9 %shard_map.124.moved_halo = f32[5,8,8,128]{3,2,1,0:T(8,128)S(1)} custom-call(f32[25,8,128]{2,1,0:T(8,128)S(1)} %get-tuple-element.47.c, f32[8,8,8,128]{3,2,1,0:T(8,128)S(1)} %get-tuple-element.54.up.up_c, f32[8,8,8,128]{3,2,1,0:T(8,128)S(1)} %shard_map.121.own.own_c.refs_2_, f32[8,8,8,128]{3,2,1,0:T(8,128)S(1)} %get-tuple-element.55.down.down_c, ...), custom_call_target="tpu_custom_call" | custom-call | flops 4000000 | bytes 1675264 | tf_op jit(solution)/shard_map/pallas_call | solution.py:365
  22.1 0.0 collective-permute-done.4.after
  22.2 1.8 %collective-permute-done.2.one = f32[5,8,8,128]{3,2,1,0:T(8,128)S(1)} collective-permute-done((f32[5,8,8,128]{3,2,1,0:T(8,128)S(1)}, f32[5,8,8,128]{3,2,1,0:T(8,128)S(1)}, u32[]{:S(2)}, u32[]{:S(2)}) %collective-permute-start.2) | collective-permute-done | bytes 163872 | tf_op jit(solution)/shard_map/ppermute | solution.py:396
  24.0 0.0 collective-permute-done.3.two
  24.0 0.9 %shard_map.125 = (f32[5,16,8,128]{3,2,1,0:T(8,128)S(1)}, f32[8,8,128]{2,1,0:T(8,128)S(1)}, f32[5,8,8,128]{3,2,1,0:T(8,128)S(1)}, f32[5,8,8,128]{3,2,1,0:T(8,128)S(1)}) custom-call(f32[25,8,128]{2,1,0:T(8,128)S(1)} %get-tuple-element.47.c, f32[5,8,8,128]{3,2,1,0:T(8,128)S(1)} %collective-permute-done.2.one, f32[5,8,8,128]{3,2,1,0:T(8,128)S(1)} %collective-permute-done.3.two, ...), custom_call_target="tpu_custom_call" | custom-call | flops 6000000 | bytes 1970176 | tf_op jit(solution)/shard_map/pallas_call | solution.py:365
  24.9 0.7 collective-permute-start.6
  25.5 6.5 %collective-permute-start.5 = (f32[5,8,8,128]{3,2,1,0:T(8,128)S(1)}, f32[5,8,8,128]{3,2,1,0:T(8,128)S(1)}, u32[]{:S(2)}, u32[]{:S(2)}) collective-permute-start(f32[5,8,8,128]{3,2,1,0:T(8,128)S(1)} %get-tuple-element.60.g.own.refs_3_), channel_id=1, source_target_pairs={{1,2},{2,1},{3,4},{4,3},{5,6},{6,5},{8,9},{9,8},{10,11},{11,10},{1... | collective-permute-start | bytes 491528 | tf_op jit(solution)/shard_map/ppermute | solution.py:407
  32.0 0.8 %shard_map.126 = (f32[5,8,8,128]{3,2,1,0:T(8,128)S(1)}, f32[5,8,8,128]{3,2,1,0:T(8,128)S(1)}) custom-call(f32[25,8,128]{2,1,0:T(8,128)S(1)} %get-tuple-element.47.c, f32[5,8,128]{2,1,0:T(8,128)S(1)} %get-tuple-element.61.keep.refs_1_, f32[5,8,8,128]{3,2,1,0:T(8,128)S(1)} %get-tuple-element.62.d.refs_6_, f32[5,16,8,128]{3,2,1,0:T(8,128)S(1)} %get-tuple-element.63.ahead, ...), custom_call_target="tpu_custom_call" | custom-call | flops 6000000 | bytes 1630208 | tf_op jit(solution)/shard_map/pallas_call | solution.py:365
  32.8 1.9 %collective-permute-start.9 = (f32[5,8,8,128]{3,2,1,0:T(8,128)S(1)}, f32[5,8,8,128]{3,2,1,0:T(8,128)S(1)}, u32[]{:S(2)}, u32[]{:S(2)}) collective-permute-start(f32[5,8,8,128]{3,2,1,0:T(8,128)S(1)} %get-tuple-element.70), channel_id=1, source_target_pairs={{8,0},{16,8},{24,16},{32,24},{40,32},{48,40},{56,48},{64,56},{72,6... | collective-permute-start | bytes 491528 | tf_op jit(solution)/shard_map/ppermute | solution.py:386
  34.7 0.0 collective-permute-done.6.second
  34.7 0.0 collective-permute-done.5.first
  34.8 0.8 %shard_map.127 = (f32[5,8,8,128]{3,2,1,0:T(8,128)S(1)}, f32[5,8,8,128]{3,2,1,0:T(8,128)S(1)}, f32[5,8,8,128]{3,2,1,0:T(8,128)S(1)}, f32[5,8,8,128]{3,2,1,0:T(8,128)S(1)}, f32[5,8,8,128]{3,2,1,0:T(8,128)S(1)}) custom-call(f32[25,8,128]{2,1,0:T(8,128)S(1)} %get-tuple-element.47.c, f32[5,8,8,128]{3,2,1,0:T(8,128)S(1)} %collective-permute-done.5.first, ...), custom_call_target="tpu_custom_call" | custom-call | flops 4000000 | bytes 1380352 | tf_op jit(solution)/shard_map/pallas_call | solution.py:365
  35.5 3.6 %collective-permute-start.7 = (f32[5,8,8,128]{3,2,1,0:T(8,128)S(1)}, f32[5,8,8,128]{3,2,1,0:T(8,128)S(1)}, u32[]{:S(2)}, u32[]{:S(2)}) collective-permute-start(f32[5,8,8,128]{3,2,1,0:T(8,128)S(1)} %get-tuple-element.68), channel_id=1, source_target_pairs={{8,16},{16,8},{24,32},{32,24},{40,48},{48,40},{56,64},{64,56},{72,... | collective-permute-start | bytes 491528 | tf_op jit(solution)/shard_map/ppermute | solution.py:396
  39.2 1.9 %collective-permute-start.8 = (f32[5,8,8,128]{3,2,1,0:T(8,128)S(1)}, f32[5,8,8,128]{3,2,1,0:T(8,128)S(1)}, u32[]{:S(2)}, u32[]{:S(2)}) collective-permute-start(f32[5,8,8,128]{3,2,1,0:T(8,128)S(1)} %get-tuple-element.69), channel_id=1, source_target_pairs={{0,8},{8,0},{16,24},{24,16},{32,40},{40,32},{48,56},{56,48},{64,72... | collective-permute-start | bytes 491528 | tf_op jit(solution)/shard_map/ppermute | solution.py:396
  41.1 0.9 %shard_map.128.moved_halo = f32[5,8,8,128]{3,2,1,0:T(8,128)S(1)} custom-call(f32[25,8,128]{2,1,0:T(8,128)S(1)} %get-tuple-element.47.c, f32[5,8,8,128]{3,2,1,0:T(8,128)S(1)} %get-tuple-element.72.up, f32[5,8,8,128]{3,2,1,0:T(8,128)S(1)} %get-tuple-element.60.g.own.refs_3_, f32[5,8,8,128]{3,2,1,0:T(8,128)S(1)} %get-tuple-element.73.down, ...), custom_call_target="tpu_custom_call" | custom-call | flops 4000000 | bytes 1380352 | tf_op jit(solution)/shard_map/pallas_call | solution.py:365
  42.0 0.0 collective-permute-done.9.after
  42.0 0.1 collective-permute-done.7.one
  42.2 0.3 collective-permute-done.8.two
  42.5 0.9 %shard_map.129 = (f32[5,8,8,128]{3,2,1,0:T(8,128)S(1)}, f32[5,8,8,128]{3,2,1,0:T(8,128)S(1)}, f32[8,8,128]{2,1,0:T(8,128)S(1)}, f32[16,1,128]{2,1,0:T(1,128)S(1)}) custom-call(f32[25,8,128]{2,1,0:T(8,128)S(1)} %get-tuple-element.47.c, f32[5,8,8,128]{3,2,1,0:T(8,128)S(1)} %collective-permute-done.7.one, f32[5,8,8,128]{3,2,1,0:T(8,128)S(1)} %collective-permute-done.8.two, ...), custom_call_target="tpu_custom_call" | custom-call | flops 6000000 | bytes 2101248 | tf_op jit(solution)/shard_map/pallas_call | solution.py:365
  43.4 12.7 %all_to_all.10.parts = f32[16,1,128]{2,1,0:T(1,128)S(1)} all-to-all(f32[16,1,128]{2,1,0:T(1,128)S(1)} %get-tuple-element.75), channel_id=1, replica_groups={{12,13,14,15,8,9,10,11,4,5,6,7,0,1,2,3},{28,29,30,31,24,25,26,27,20,21,..., dimensions={0} | all-to-all | bytes 16384 | tf_op jit(solution)/shard_map/all_to_all | solution.py:416
  56.1 15.9 %all_to_all.11.refs_0_ = f32[32,1,128]{2,1,0:T(1,128)S(1)} all-to-all(f32[32,1,128]{2,1,0:T(1,128)S(1)} %shard_map.130), channel_id=1, replica_groups={{320,336,352,368,256,272,288,304,448,464,480,496,384,400,416,432,64,80,..., dimensions={0} | all-to-all | bytes 32768 | tf_op jit(solution)/shard_map/all_to_all | solution.py:416
  72.0 0.9 %shard_map.131 = (f32[1,5,8,1024]{3,2,1,0:T(8,128)}, f32[1,5,8,1024]{3,2,1,0:T(8,128)}, f32[1,8,1024]{2,1,0:T(8,128)}) custom-call(f32[32,1,128]{2,1,0:T(1,128)S(1)} %all_to_all.11.refs_0_, f32[5,8,128]{2,1,0:T(8,128)S(1)} %get-tuple-element.61.keep.refs_1_, f32[8,8,8,128]{3,2,1,0:T(8,128)S(1)} %shard_map.121.own.own_c.refs_2_, ...), custom_call_target="tpu_custom_call" | custom-call | flops 4000000 | bytes 1183744 | tf_op jit(solution)/shard_map/pallas_call | solution.py:365
  (1 shorter events, 0.0 us)
Async XLA Ops:
  0.6 10.0 %copy-start.1 = (f32[1,8,1024]{2,1,0:T(8,128)S(1)}, f32[1,8,1024]{2,1,0:T(8,128)}, u32[]{:S(2)}) copy-start(f32[1,8,1024]{2,1,0:T(8,128)} %observed.1) | copy-start | bytes 98308
  0.6 10.0 %copy-start = (f32[5,8,1024]{2,1,0:T(8,128)S(1)}, f32[5,8,1024]{2,1,0:T(8,128)}, u32[]{:S(2)}) copy-start(f32[5,8,1024]{2,1,0:T(8,128)} %background.1) | copy-start | bytes 491524
  0.7 10.0 %copy-start.2 = (f32[5,5]{1,0:T(8,128)S(1)}, f32[5,5]{1,0:T(8,128)}, u32[]{:S(2)}) copy-start(f32[5,5]{1,0:T(8,128)} %coupling.1) | copy-start | bytes 304
  0.7 10.0 %copy-start.3 = (s32[1,8,8]{2,1,0:T(8,128)S(1)}, s32[1,8,8]{2,1,0:T(8,128)}, u32[]{:S(2)}) copy-start(s32[1,8,8]{2,1,0:T(8,128)} %obs_level.1) | copy-start | bytes 772
  0.7 10.0 %copy-start.4 = (s32[1,8,8]{2,1,0:T(8,128)S(1)}, s32[1,8,8]{2,1,0:T(8,128)}, u32[]{:S(2)}) copy-start(s32[1,8,8]{2,1,0:T(8,128)} %huber_class.1) | copy-start | bytes 772
  1.8 8.9 %copy-start.5 = (f32[5]{0:T(128)S(1)}, f32[5]{0:T(128)}, u32[]{:S(2)}) copy-start(f32[5]{0:T(128)} %param.17) | copy-start | bytes 64
  1.8 11.6 %collective-permute-start.1 = (f32[8,8,8,128]{3,2,1,0:T(8,128)S(1)}, f32[8,8,8,128]{3,2,1,0:T(8,128)S(1)}, u32[]{:S(2)}, u32[]{:S(2)}) collective-permute-start(f32[8,8,8,128]{3,2,1,0:T(8,128)S(1)} %shard_map.121.own.own_c.refs_2_), channel_id=1, source_target_pairs={{0,1},{1,0},{2,3},{3,2},{4,5},{5,4},{6,7},{7,6},{9,10},{10,9},{11,... | collective-permute-start | bytes 786440 | tf_op jit(solution)/shard_map/ppermute | solution.py:407
  2.5 14.1 %collective-permute-start = (f32[8,8,8,128]{3,2,1,0:T(8,128)S(1)}, f32[8,8,8,128]{3,2,1,0:T(8,128)S(1)}, u32[]{:S(2)}, u32[]{:S(2)}) collective-permute-start(f32[8,8,8,128]{3,2,1,0:T(8,128)S(1)} %shard_map.121.own.own_c.refs_2_), channel_id=1, source_target_pairs={{1,2},{2,1},{3,4},{4,3},{5,6},{6,5},{8,9},{9,8},{10,11},{11,10},{1... | collective-permute-start | bytes 786440 | tf_op jit(solution)/shard_map/ppermute | solution.py:407
  10.8 11.3 %collective-permute-start.4 = (f32[5,8,8,128]{3,2,1,0:T(8,128)S(1)}, f32[5,8,8,128]{3,2,1,0:T(8,128)S(1)}, u32[]{:S(2)}, u32[]{:S(2)}) collective-permute-start(f32[5,8,8,128]{3,2,1,0:T(8,128)S(1)} %get-tuple-element.52), channel_id=1, source_target_pairs={{8,0},{16,8},{24,16},{32,24},{40,32},{48,40},{56,48},{64,56},{72,6... | collective-permute-start | bytes 491528 | tf_op jit(solution)/shard_map/ppermute | solution.py:386
  17.4 6.6 %collective-permute-start.2 = (f32[5,8,8,128]{3,2,1,0:T(8,128)S(1)}, f32[5,8,8,128]{3,2,1,0:T(8,128)S(1)}, u32[]{:S(2)}, u32[]{:S(2)}) collective-permute-start(f32[5,8,8,128]{3,2,1,0:T(8,128)S(1)} %get-tuple-element.50), channel_id=1, source_target_pairs={{8,16},{16,8},{24,32},{32,24},{40,48},{48,40},{56,64},{64,56},{72,... | collective-permute-start | bytes 491528 | tf_op jit(solution)/shard_map/ppermute | solution.py:396
  19.3 4.7 %collective-permute-start.3 = (f32[5,8,8,128]{3,2,1,0:T(8,128)S(1)}, f32[5,8,8,128]{3,2,1,0:T(8,128)S(1)}, u32[]{:S(2)}, u32[]{:S(2)}) collective-permute-start(f32[5,8,8,128]{3,2,1,0:T(8,128)S(1)} %get-tuple-element.51), channel_id=1, source_target_pairs={{0,8},{8,0},{16,24},{24,16},{32,40},{40,32},{48,56},{56,48},{64,72... | collective-permute-start | bytes 491528 | tf_op jit(solution)/shard_map/ppermute | solution.py:396
  24.9 9.9 %collective-permute-start.6 = (f32[5,8,8,128]{3,2,1,0:T(8,128)S(1)}, f32[5,8,8,128]{3,2,1,0:T(8,128)S(1)}, u32[]{:S(2)}, u32[]{:S(2)}) collective-permute-start(f32[5,8,8,128]{3,2,1,0:T(8,128)S(1)} %get-tuple-element.60.g.own.refs_3_), channel_id=1, source_target_pairs={{0,1},{1,0},{2,3},{3,2},{4,5},{5,4},{6,7},{7,6},{9,10},{10,9},{11,... | collective-permute-start | bytes 491528 | tf_op jit(solution)/shard_map/ppermute | solution.py:407
  25.5 9.2 %collective-permute-start.5 = (f32[5,8,8,128]{3,2,1,0:T(8,128)S(1)}, f32[5,8,8,128]{3,2,1,0:T(8,128)S(1)}, u32[]{:S(2)}, u32[]{:S(2)}) collective-permute-start(f32[5,8,8,128]{3,2,1,0:T(8,128)S(1)} %get-tuple-element.60.g.own.refs_3_), channel_id=1, source_target_pairs={{1,2},{2,1},{3,4},{4,3},{5,6},{6,5},{8,9},{9,8},{10,11},{11,10},{1... | collective-permute-start | bytes 491528 | tf_op jit(solution)/shard_map/ppermute | solution.py:407
  32.8 9.2 %collective-permute-start.9 = (f32[5,8,8,128]{3,2,1,0:T(8,128)S(1)}, f32[5,8,8,128]{3,2,1,0:T(8,128)S(1)}, u32[]{:S(2)}, u32[]{:S(2)}) collective-permute-start(f32[5,8,8,128]{3,2,1,0:T(8,128)S(1)} %get-tuple-element.70), channel_id=1, source_target_pairs={{8,0},{16,8},{24,16},{32,24},{40,32},{48,40},{56,48},{64,56},{72,6... | collective-permute-start | bytes 491528 | tf_op jit(solution)/shard_map/ppermute | solution.py:386
  35.5 6.6 %collective-permute-start.7 = (f32[5,8,8,128]{3,2,1,0:T(8,128)S(1)}, f32[5,8,8,128]{3,2,1,0:T(8,128)S(1)}, u32[]{:S(2)}, u32[]{:S(2)}) collective-permute-start(f32[5,8,8,128]{3,2,1,0:T(8,128)S(1)} %get-tuple-element.68), channel_id=1, source_target_pairs={{8,16},{16,8},{24,32},{32,24},{40,48},{48,40},{56,64},{64,56},{72,... | collective-permute-start | bytes 491528 | tf_op jit(solution)/shard_map/ppermute | solution.py:396
  39.2 3.3 %collective-permute-start.8 = (f32[5,8,8,128]{3,2,1,0:T(8,128)S(1)}, f32[5,8,8,128]{3,2,1,0:T(8,128)S(1)}, u32[]{:S(2)}, u32[]{:S(2)}) collective-permute-start(f32[5,8,8,128]{3,2,1,0:T(8,128)S(1)} %get-tuple-element.69), channel_id=1, source_target_pairs={{0,8},{8,0},{16,24},{24,16},{32,40},{40,32},{48,56},{56,48},{64,72... | collective-permute-start | bytes 491528 | tf_op jit(solution)/shard_map/ppermute | solution.py:396

commit v6 on v5

--- a/solution.py
+++ b/solution.py
@@ -49,69 +49,81 @@
     return (1.0 - (ce + cw)) - 2.0 * ky
 
 
-def forward(src, coef, c, rows, bufs, dst):
-    sh = Shift()
+def inside(step):
+    return range(H + 1 + step, H + ROWS - 1 - step)
+
+
+INNER = sum(len(inside(step)) for step in range(STEPS))
+
+
+def slot(step, r):
+    return sum(len(inside(s)) for s in range(step)) + r - inside(step)[0]
+
+
+def march(row, src, rows, bufs, dst, inner, fill):
     for step in range(STEPS):
         lo, hi = step + 1, rows - step - 1
-
-        def get(r, step=step):
+        if fill:
+            lo, hi = inside(step).start, inside(step).stop
+        ready = inside(step) if inner is not None and not fill else ()
+
+        def get(l, r, step=step):
             if step == 0:
-                return [src(l, r) for l in range(L)]
-            return [bufs[(step - 1) % 2][l, r] for l in range(L)]
-
-        above, here = get(lo - 1), get(lo)
+                return src(l, r)
+            if inner is not None and r in inside(step - 1):
+                return inner[l, slot(step - 1, r)]
+            return bufs[(step - 1) % 2][l, r]
+
         for r in range(lo, hi):
-            below = get(r + 1)
-            ce, cw, ky = coef(0, r), coef(1, r), coef(2, r)
-            c0 = centre(ce, cw, ky)
-            for l in range(L):
-                v = here[l]
-                terms = [
-                    ce * sh.east(v),
-                    cw * sh.west(v),
-                    ky * (above[l] + below[l]),
-                    c0 * v,
-                ] + [c[L * l + m] * here[m] for m in range(L)]
-                out = total(terms)
-                if step == STEPS - 1:
+            if r in ready:
+                continue
+            for l, out in enumerate(row(get, r)):
+                if fill:
+                    inner[l, slot(step, r)] = out
+                elif step == STEPS - 1:
                     dst(l, r, out)
                 else:
                     bufs[step % 2][l, r] = out
-            above, here = here, below
-
-
-def adjoint(src, coef, c, rows, bufs, dst):
+
+
+def forward(src, coef, c, rows, bufs, dst, inner=None, fill=False):
     sh = Shift()
-    for step in range(STEPS):
-        lo, hi = step + 1, rows - step - 1
-
-        def get(r, step=step):
-            if step == 0:
-                v = [src(l, r) for l in range(L)]
-            else:
-                v = [bufs[(step - 1) % 2][l, r] for l in range(L)]
-            ky = coef(2, r)
-            return v, [ky * w for w in v]
-
-        (_, above), (here, q) = get(lo - 1), get(lo)
-        for r in range(lo, hi):
-            after, below = get(r + 1)
-            ce, cw, ky = coef(0, r), coef(1, r), coef(2, r)
-            c0 = centre(ce, cw, ky)
-            for l in range(L):
-                w = here[l]
-                terms = [
+
+    def row(get, r):
+        above, here, below = [[get(l, at) for l in range(L)] for at in (r - 1, r, r + 1)]
+        ce, cw, ky = coef(0, r), coef(1, r), coef(2, r)
+        c0 = centre(ce, cw, ky)
+        for l in range(L):
+            v = here[l]
+            yield total(
+                [ce * sh.east(v), cw * sh.west(v), ky * (above[l] + below[l]), c0 * v]
+                + [c[L * l + m] * here[m] for m in range(L)]
+            )
+
+    march(row, src, rows, bufs, dst, inner, fill)
+
+
+def adjoint(src, coef, c, rows, bufs, dst, inner=None, fill=False):
+    sh = Shift()
+
+    def row(get, r):
+        above, here, below = [[get(l, at) for l in range(L)] for at in (r - 1, r, r + 1)]
+        ce, cw, ky = coef(0, r), coef(1, r), coef(2, r)
+        ky_above, ky_below = coef(2, r - 1), coef(2, r + 1)
+        c0 = centre(ce, cw, ky)
+        for l in range(L):
+            w = here[l]
+            yield total(
+                [
                     sh.west(ce * w),
                     sh.east(cw * w),
-                    above[l] + below[l],
+                    ky_above * above[l] + ky_below * below[l],
                     c0 * w,
-                ] + [c[L * m + l] * here[m] for m in range(L)]
-                out = total(terms)
-                if step == STEPS - 1:
-                    dst(l, r, out)
-                else:
-                    bufs[step % 2][l, r] = out
-            above, here, q = q, after, below
+                ]
+                + [c[L * m + l] * here[m] for m in range(L)]
+            )
+
+    march(row, src, rows, bufs, dst, inner, fill)
 
 
 def banded(up, own, down, first):
@@ -191,17 +203,19 @@
             down[k, r] = jnp.where(below, first[k, r], second[k, r])
 
 
-def forward_kernel(c, first, second, own, up, down, moved, one, two, a, b):
+def forward_kernel(c, first, second, own, inner, up, down, moved, one, two, a, b):
     sides(first, second, L + 3, up, down)
-    send(c, up, own, down, up, own, down, moved, one, two, a, b)
-
-
-def forward_g_kernel(c, first, second, own, up_c, own_c, down_c, up, down, moved, one, two, a, b):
+    send(c, up, own, down, up, own, down, inner, moved, one, two, a, b)
+
+
+def forward_g_kernel(
+    c, first, second, own, up_c, own_c, down_c, inner, up, down, moved, one, two, a, b
+):
     sides(first, second, L, up, down)
-    send(c, up, own, down, up_c, own_c, down_c, moved, one, two, a, b)
-
-
-def send(c, up, own, down, up_c, own_c, down_c, moved, one, two, a, b):
+    send(c, up, own, down, up_c, own_c, down_c, inner, moved, one, two, a, b)
+
+
+def send(c, up, own, down, up_c, own_c, down_c, inner, moved, one, two, a, b):
     ahead = odd(TM[-1])
     field, coef = banded(up, own, down, 0), banded(up_c, own_c, down_c, L)
 
@@ -212,15 +226,17 @@
         one[l, r] = jnp.where(ahead, v, halo)
         two[l, r] = jnp.where(ahead, halo, v)
 
-    forward(lambda l, r: field(l, r + H), lambda k, r: coef(k, r + H), c, W, (a, b), dst)
-
-
-def halo_kernel(c, up, own, down, up_c, own_c, down_c, moved, a, b):
+    forward(lambda l, r: field(l, r + H), lambda k, r: coef(k, r + H), c, W, (a, b), dst, inner)
+
+
+def halo_kernel(
+    factor, c, after, moved, up, own, down, up_c, own_c, down_c, moved_halo, ahead, inner, a, b
+):
     field, coef = banded(up, own, down, 0), banded(up_c, own_c, down_c, L)
     for first, to in ((0, 0), (ROWS + H, H)):
 
         def dst(l, r, v, to=to):
-            moved[l, to + r - H] = v
+            moved_halo[l, to + r - H] = v
 
         forward(
             lambda l, r, first=first: field(l, first + r),
@@ -230,19 +246,26 @@
             (a, b),
             dst,
         )
-
-
-def receive(one, two, after, moved, moved_halo, factor, out):
-    ahead = odd(TM[-1])
+    factor = factor * place()[0]
     for l in range(L):
-        for r in range(W):
-            if H <= r < H + ROWS:
-                v = after[l, r - H] - moved[l, r - H]
-            else:
-                at = r if r < H else r - ROWS
-                v = jnp.where(ahead, one[l, at], two[l, at]) - moved_halo[l, at]
-            out[l, r] = factor * v
-    return lambda l, r: jnp.where(ahead, two[l, r], one[l, r])
+        for r in range(ROWS):
+            ahead[l, r] = factor * (after[l, r] - moved[l, r])
+    adjoint(
+        lambda l, r: ahead[l, r - H], lambda k, r: own_c[L + k, r - H], c, W, None, None, inner, True
+    )
+
+
+def receive(factor, one, two, ahead, moved_halo):
+    odd_one = odd(TM[-1])
+    factor = factor * place()[0]
+
+    def next_one(l, r):
+        if H <= r < H + ROWS:
+            return ahead[l, r - H]
+        at = r if r < H else r - ROWS
+        return factor * (jnp.where(odd_one, one[l, at], two[l, at]) - moved_halo[l, at])
+
+    return next_one, lambda l, r: jnp.where(odd_one, two[l, r], one[l, r])
 
 
 def picked(level, values):
@@ -252,43 +275,65 @@
     return out
 
 
-def back_kernel(
-    c, one, two, after, moved, moved_halo, up, own, down, bg, obs, level, weight, ahead, o1, d, g, a, b
-):
-    some, first = place()
-    came = receive(one, two, after, moved, moved_halo, 0.5 * some, ahead)
+def early_kernel(c, own, obs, level, weight, o1, inner):
     for r in range(ROWS):
         o1[r] = 0.5 * weight[r] * (picked(level[r], [own[l, r] for l in range(L)]) - obs[r])
+    forward(
+        lambda l, r: own[l, r - H], lambda k, r: own[L + k, r - H], c, W, None, None, inner, True
+    )
+
+
+def back_kernel(
+    c, one, two, ahead_own, moved_halo, inner, up, own, down, bg, level, o1, ahead, d, g, a, b
+):
+    first = place()[1]
+    next_one, came = receive(0.5, one, two, ahead_own, moved_halo)
+    for l in range(L):
+        for r in range(W):
+            ahead[l, r] = next_one(l, r)
     coef = banded(up, own, down, L)
 
     def dst(l, r, v):
         r = r - H
-        one = 0.5 * (own[l, r] - (came(l, r) + first * bg[l, r]))
-        d[l, r] = one
-        g[l, r] = one - v + jnp.where(level[r] == float(l), o1[r], 0.0)
-
-    adjoint(lambda l, r: ahead[l, r], lambda k, r: coef(k, r + H), c, W, (a, b), dst)
-
-
-def still_kernel(c, keep, d, ahead, up, own, down, level, o1, g, g0, g_out, a, b):
+        now = 0.5 * (own[l, r] - (came(l, r) + first * bg[l, r]))
+        d[l, r] = now
+        g[l, r] = now - v + jnp.where(level[r] == float(l), o1[r], 0.0)
+
+    adjoint(lambda l, r: ahead[l, r], lambda k, r: coef(k, r + H), c, W, (a, b), dst, inner)
+
+
+def still_kernel(
+    c, keep, d, ahead, up, own, down, level, weight, o1, g, g0, g_out, hg, inner, early, a, b
+):
     g_out[...] = g[...]
+    for r in range(ROWS):
+        hg[r] = weight[r] * picked(level[r], [g[l, r] for l in range(L)])
+    forward(
+        lambda l, r: g[l, r - H], lambda k, r: own[L + k, r - H], c, W, None, None, inner, True
+    )
     coef = banded(up, own, down, L)
+    sums = []
 
     def dst(l, r, v):
         r = r - H
-        g0[l, r] = keep[l] * d[l, r] - v + jnp.where(level[r] == float(l), 1.5 * o1[r], 0.0)
+        now = keep[l] * d[l, r] - v + jnp.where(level[r] == float(l), 1.5 * o1[r], 0.0)
+        g0[l, r] = now
+        sums.append(now * now)
 
     adjoint(lambda l, r: keep[l] * ahead[l, r], lambda k, r: coef(k, r + H), c, W, (a, b), dst)
+    early[0] = total([g[l, r] * g[l, r] for l in range(L) for r in range(ROWS)])
+    early[1] = total(sums)
 
 
 def back_g_kernel(
-    c, one, two, after, moved, moved_halo, up, own, down, g, level, weight, g0, u, g1, hg, part, ahead, a, b
-):
-    came = receive(one, two, after, moved, moved_halo, place()[0], ahead)
-    for r in range(ROWS):
-        hg[r] = weight[r] * picked(level[r], [g[l, r] for l in range(L)])
+    c, one, two, ahead_own, moved_halo, inner, up, own, down, g, level, hg, g0, early, u, g1, part, ahead, a, b
+):
+    next_one, came = receive(1.0, one, two, ahead_own, moved_halo)
+    for l in range(L):
+        for r in range(W):
+            ahead[l, r] = next_one(l, r)
     coef = banded(up, own, down, L)
-    sums = [[], [], [], []]
+    late = [[], []]
 
     def dst(l, r, v):
         r = r - H
@@ -296,16 +341,16 @@
         u[l, r] = now
         one = -0.5 * (now - v + jnp.where(level[r] == float(l), hg[r], 0.0))
         g1[l, r] = one
-        for k, term in enumerate((g[l, r] * g[l, r], g0[l, r] * g0[l, r], g0[l, r] * one, one * one)):
-            sums[k].append(term)
-            if len(sums[k]) == L:
-                sums[k] = [total(sums[k])]
-
-    adjoint(lambda l, r: ahead[l, r], lambda k, r: coef(k, r + H), c, W, (a, b), dst)
+        for k, term in enumerate((g0[l, r] * one, one * one)):
+            late[k].append(term)
+            if len(late[k]) == L:
+                late[k] = [total(late[k])]
+
+    adjoint(lambda l, r: ahead[l, r], lambda k, r: coef(k, r + H), c, W, (a, b), dst, inner)
     lane = lax.broadcasted_iota(jnp.int32, (1, TILE), 1)
     row = jnp.zeros((1, TILE), jnp.float32)
-    for k in range(4):
-        s = jnp.sum(jnp.sum(total(sums[k]), axis=0, keepdims=True), axis=1, keepdims=True)
+    for k, v in enumerate((early[0], early[1], total(late[0]), total(late[1]))):
+        s = jnp.sum(jnp.sum(v, axis=0, keepdims=True), axis=1, keepdims=True)
         row = jnp.where(lane == k, s, row)
     for i in range(part.shape[0]):
         part[i] = row
@@ -435,38 +480,45 @@
         aside_kernel, [band, band, cells, (L * L, *ROW), (L, *ROW), cells, cells]
     )(own, background, observed, coupling, model_var[None], obs_level, huber_class)
     after = shifted(x, TM, -1)
-    first, second, bg, obs, c, keep, level, weight = lax.optimization_barrier(
-        (first, second, bg, obs, c, keep, level, weight)
-    )
+    inside_rows = rows_of(L, INNER)
+    o1, inner = call(early_kernel, [cells, inside_rows], us=0.5)(c, own, obs, level, weight)
+    first, second, bg, keep, o1, inner = lax.optimization_barrier(
+        (first, second, bg, keep, o1, inner)
+    )
+
+    def half_way(factor):
+        return call(
+            lambda *refs: halo_kernel(factor, *refs), [band, band, inside_rows], [rows_of(L, 3 * H)] * 2
+        )
 
     three = rows_of(L + 3, ROWS)
-    short = [rows_of(L, 3 * H)] * 2
     up, down, moved, *sent = call(forward_kernel, [three, three, band, band, band], two_w)(
-        c, first, second, own
+        c, first, second, own, inner
     )
     swaps = swapped(*sent)
-    (moved_halo,) = call(halo_kernel, [band], short)(c, up, own, down, up, own, down)
-    ahead, o1, d, g = call(back_kernel, [wide, cells, band, band], two_w, 1.5)(
-        c, *swaps, after, moved, moved_halo, up, own, down, bg, obs, level, weight
+    moved_halo, ahead_own, inner = half_way(0.5)(c, after, moved, up, own, down, up, own, down)
+    *swaps, moved_halo = lax.optimization_barrier((*swaps, moved_halo))
+    ahead, d, g = call(back_kernel, [wide, band, band], two_w)(
+        c, *swaps, ahead_own, moved_halo, inner, up, own, down, bg, level, o1
     )
 
     first, second = swapped_rows(g)
-    g0, g_copy = call(still_kernel, [band, band], two_w, 1.5)(
-        c, keep, d, ahead, up, own, down, level, o1, g
-    )
+    g0, g_copy, hg, inner, early = call(
+        still_kernel, [band, band, cells, inside_rows, (2, *ROW)], two_w, 1.5
+    )(c, keep, d, ahead, up, own, down, level, weight, o1, g)
     after_g = shifted(g_copy, TM, -1)
     first, second, g0 = lax.optimization_barrier((first, second, g0))
     up_g, down_g, moved_g, *sent = call(forward_g_kernel, [band] * 5, two_w)(
-        c, first, second, g, up, own, down
+        c, first, second, g, up, own, down, inner
     )
     swaps = swapped(*sent)
-    (moved_g_halo,) = call(halo_kernel, [band], short)(c, up_g, g, down_g, up, own, down)
-    u, g1, hg, part = call(
-        back_g_kernel,
-        [band, band, cells, (lax.axis_size(NEAR), 1, TILE)],
-        [wide] + two_w,
-        1.5,
-    )(c, *swaps, after_g, moved_g, moved_g_halo, up, own, down, g, level, weight, g0)
+    moved_halo, ahead_own, inner = half_way(1.0)(
+        c, after_g, moved_g, up_g, g, down_g, up, own, down
+    )
+    *swaps, moved_halo = lax.optimization_barrier((*swaps, moved_halo))
+    u, g1, part = call(
+        back_g_kernel, [band, band, (lax.axis_size(NEAR), 1, TILE)], [wide] + two_w
+    )(c, *swaps, ahead_own, moved_halo, inner, up, own, down, g, level, hg, g0, early)
     (part,) = call(again_kernel, [(lax.axis_size(FAR), 1, TILE)], us=0.1)(exchanged(part, NEAR))
     part = exchanged(part, FAR)
 

time: 74 us -> 73.6 us (level)
    pallas_call x11 -> x12, Pallas kernels: 8.08 us -> 8.31 us  [run(): pl.pallas_call(kernel, out_shape=[jax.ShapeDtypeStruct(s, jnp.float32) fo...]
  transfers between devices with their start and end apart: 10 -> 10, of which waited for: 4 -> 3; matrix products, arithmetic and copies ran while one was open for 0% -> 0% of each run, Pallas kernels for 6% -> 7%
where the time goes in v6:
time: 73.6 us; the launch traced here: 72.5 us
  starting transfers between devices  29.9 us (41%)
  blocking collectives  28.6 us (39%)
  Pallas kernels  8.31 us (11%)
  waiting for transfers between devices  4.77 us (6%)
  between operations  0.9 us (1%)
    all_to_all x2, blocking collectives, exchanged(): return lax.all_to_all(x, axes, 0, 0, axis_index_groups=[order], tiled=True)  28.6 us
    ppermute x4, starting transfers between devices, swapped_rows(): out.append(lax.ppermute(x, (TM[-1], 'lat'), both_ways(lows)))  16 us
    ppermute x4, starting transfers between devices, swapped(): lax.ppermute(x, TM, both_ways(range(start, count - 1, 2)))  9.43 us
    pallas_call x12, Pallas kernels, run(): pl.pallas_call(kernel, out_shape=[jax.ShapeDtypeStruct(s, jnp.float32) fo...  8.31 us
    ppermute x2, starting transfers between devices, shifted(): lax.ppermute(x, axis, [(i, i + by) for i in range(count) if 0 <= i + by <...  4.47 us
    ppermute x4, waiting for transfers between devices, swapped_rows(): out.append(lax.ppermute(x, (TM[-1], 'lat'), both_ways(lows)))  2.93 us
    ppermute x4, waiting for transfers between devices, swapped(): lax.ppermute(x, TM, both_ways(range(start, count - 1, 2)))  1.83 us
  transfers between devices with their start and end apart: 10, of which 3 were waited for; matrix products, arithmetic and copies ran while one was open for 0% of the time, Pallas kernels for 7%

profile of v6, /device:TPU:1, one launch (start us, length us, event | category | flops | bytes accessed | tf_op | source)
XLA Modules:
  0.0 72.5 jit_solution(17528973109689899323)
XLA Ops:
  0.6 0.0 copy-start.1
  0.6 0.0 copy-start
  0.7 0.0 copy-start.2
  0.7 0.0 copy-start.3
  0.7 0.0 copy-start.4
  0.7 1.1 %shard_map.121.own.refs_4_.refs_7_.own_c.refs_2_ = f32[8,8,8,128]{3,2,1,0:T(8,128)S(1)} custom-call(f32[1,5,8,1024]{3,2,1,0:T(8,128)} %x_far.1, f32[1,8,1024]{2,1,0:T(8,128)} %kx_far.1, f32[1,8,1024]{2,1,0:T(8,128)} %ky_far.1, f32[1,8,1024]{2,1,0:T(8,128)} %ux_far.1), custom_call_target="tpu_custom_call" | custom-call | flops 4000000 | bytes 262144 | tf_op jit(solution)/shard_map/pallas_call | solution.py:410
  1.8 0.0 copy-start.5
  1.8 0.7 collective-permute-start.1
  2.5 8.2 %collective-permute-start = (f32[8,8,8,128]{3,2,1,0:T(8,128)S(1)}, f32[8,8,8,128]{3,2,1,0:T(8,128)S(1)}, u32[]{:S(2)}, u32[]{:S(2)}) collective-permute-start(f32[8,8,8,128]{3,2,1,0:T(8,128)S(1)} %shard_map.121.own.refs_4_.refs_7_.own_c.refs_2_), channel_id=1, source_target_pairs={{1,2},{2,1},{3,4},{4,3},{5,6},{6,5},{8,9},{9,8},{10,11},{11,10},{1... | collective-permute-start | bytes 786440 | tf_op jit(solution)/shard_map/ppermute | solution.py:452
  10.6 0.0 copy-done.1
  10.6 0.0 copy-done
  10.6 0.0 copy-done.2
  10.6 0.0 copy-done.3
  10.7 0.0 copy-done.4
  10.7 0.0 copy-done.5
  10.7 0.1 shard_map.122
  10.8 2.6 %collective-permute-start.4 = (f32[5,8,8,128]{3,2,1,0:T(8,128)S(1)}, f32[5,8,8,128]{3,2,1,0:T(8,128)S(1)}, u32[]{:S(2)}, u32[]{:S(2)}) collective-permute-start(f32[5,8,8,128]{3,2,1,0:T(8,128)S(1)} %get-tuple-element.67), channel_id=1, source_target_pairs={{8,0},{16,8},{24,16},{32,24},{40,32},{48,40},{56,48},{64,56},{72,6... | collective-permute-start | bytes 491528 | tf_op jit(solution)/shard_map/ppermute | solution.py:431
  13.4 0.3 shard_map.123
  13.6 0.0 collective-permute-done.1.second
  13.7 2.9 %collective-permute-done.first = f32[8,8,8,128]{3,2,1,0:T(8,128)S(1)} collective-permute-done((f32[8,8,8,128]{3,2,1,0:T(8,128)S(1)}, f32[8,8,8,128]{3,2,1,0:T(8,128)S(1)}, u32[]{:S(2)}, u32[]{:S(2)}) %collective-permute-start) | collective-permute-done | bytes 262176 | tf_op jit(solution)/shard_map/ppermute | solution.py:452
  16.6 0.6 shard_map.124
  17.2 1.9 %collective-permute-start.2 = (f32[5,8,8,128]{3,2,1,0:T(8,128)S(1)}, f32[5,8,8,128]{3,2,1,0:T(8,128)S(1)}, u32[]{:S(2)}, u32[]{:S(2)}) collective-permute-start(f32[5,8,8,128]{3,2,1,0:T(8,128)S(1)} %get-tuple-element.65), channel_id=1, source_target_pairs={{8,16},{16,8},{24,32},{32,24},{40,48},{48,40},{56,64},{64,56},{72,... | collective-permute-start | bytes 491528 | tf_op jit(solution)/shard_map/ppermute | solution.py:441
  19.1 1.9 %collective-permute-start.3 = (f32[5,8,8,128]{3,2,1,0:T(8,128)S(1)}, f32[5,8,8,128]{3,2,1,0:T(8,128)S(1)}, u32[]{:S(2)}, u32[]{:S(2)}) collective-permute-start(f32[5,8,8,128]{3,2,1,0:T(8,128)S(1)} %get-tuple-element.66), channel_id=1, source_target_pairs={{0,8},{8,0},{16,24},{24,16},{32,40},{40,32},{48,56},{56,48},{64,72... | collective-permute-start | bytes 491528 | tf_op jit(solution)/shard_map/ppermute | solution.py:441
  21.1 0.0 collective-permute-done.4.refs_1_
  21.1 1.1 %shard_map.125 = (f32[5,8,8,128]{3,2,1,0:T(8,128)S(1)}, f32[5,8,8,128]{3,2,1,0:T(8,128)S(1)}, f32[5,12,8,128]{3,2,1,0:T(8,128)S(1)}) custom-call(f32[25,8,128]{2,1,0:T(8,128)S(1)} %get-tuple-element.54.c.refs_0_, f32[5,8,8,128]{3,2,1,0:T(8,128)S(1)} %collective-permute-done.4.refs_1_, f32[5,8,8,128]{3,2,1,0:T(8,128)S(1)} %get-tuple-element.68.refs_2_, ...), custom_call_target="tpu_custom_call" | custom-call | flops 4000000 | bytes 2002944 | tf_op jit(solution)/shard_map/pallas_call | solution.py:410
  22.2 1.6 %collective-permute-done.2.one = f32[5,8,8,128]{3,2,1,0:T(8,128)S(1)} collective-permute-done((f32[5,8,8,128]{3,2,1,0:T(8,128)S(1)}, f32[5,8,8,128]{3,2,1,0:T(8,128)S(1)}, u32[]{:S(2)}, u32[]{:S(2)}) %collective-permute-start.2) | collective-permute-done | bytes 163872 | tf_op jit(solution)/shard_map/ppermute | solution.py:441
  23.8 0.0 collective-permute-done.3.two
  23.8 0.6 shard_map.126
  24.5 0.7 collective-permute-start.6
  25.1 6.5 %collective-permute-start.5 = (f32[5,8,8,128]{3,2,1,0:T(8,128)S(1)}, f32[5,8,8,128]{3,2,1,0:T(8,128)S(1)}, u32[]{:S(2)}, u32[]{:S(2)}) collective-permute-start(f32[5,8,8,128]{3,2,1,0:T(8,128)S(1)} %get-tuple-element.79.g.own.refs_4_.refs_3_), channel_id=1, source_target_pairs={{1,2},{2,1},{3,4},{4,3},{5,6},{6,5},{8,9},{9,8},{10,11},{11,10},{1... | collective-permute-start | bytes 491528 | tf_op jit(solution)/shard_map/ppermute | solution.py:452
  31.6 1.1 %shard_map.127 = (f32[5,8,8,128]{3,2,1,0:T(8,128)S(1)}, f32[5,8,8,128]{3,2,1,0:T(8,128)S(1)}, f32[8,8,128]{2,1,0:T(8,128)S(1)}, f32[5,12,8,128]{3,2,1,0:T(8,128)S(1)}, f32[2,8,128]{2,1,0:T(8,128)S(1)}) custom-call(f32[25,8,128]{2,1,0:T(8,128)S(1)} %get-tuple-element.54.c.refs_0_, f32[5,8,128]{2,1,0:T(8,128)S(1)} %get-tuple-element.80.keep.refs_1_, ...), custom_call_target="tpu_custom_call" | custom-call | flops 6000000 | bytes 1662976 | tf_op jit(solution)/shard_map/pallas_call | solution.py:410
  32.7 1.9 %collective-permute-start.9 = (f32[5,8,8,128]{3,2,1,0:T(8,128)S(1)}, f32[5,8,8,128]{3,2,1,0:T(8,128)S(1)}, u32[]{:S(2)}, u32[]{:S(2)}) collective-permute-start(f32[5,8,8,128]{3,2,1,0:T(8,128)S(1)} %get-tuple-element.89), channel_id=1, source_target_pairs={{8,0},{16,8},{24,16},{32,24},{40,32},{48,40},{56,48},{64,56},{72,6... | collective-permute-start | bytes 491528 | tf_op jit(solution)/shard_map/ppermute | solution.py:431
  34.6 0.0 collective-permute-done.6.second
  34.7 0.0 collective-permute-done.5.first
  34.7 0.6 shard_map.128
  35.2 3.6 %collective-permute-start.7 = (f32[5,8,8,128]{3,2,1,0:T(8,128)S(1)}, f32[5,8,8,128]{3,2,1,0:T(8,128)S(1)}, u32[]{:S(2)}, u32[]{:S(2)}) collective-permute-start(f32[5,8,8,128]{3,2,1,0:T(8,128)S(1)} %get-tuple-element.87), channel_id=1, source_target_pairs={{8,16},{16,8},{24,32},{32,24},{40,48},{48,40},{56,64},{64,56},{72,... | collective-permute-start | bytes 491528 | tf_op jit(solution)/shard_map/ppermute | solution.py:441
  38.9 1.9 %collective-permute-start.8 = (f32[5,8,8,128]{3,2,1,0:T(8,128)S(1)}, f32[5,8,8,128]{3,2,1,0:T(8,128)S(1)}, u32[]{:S(2)}, u32[]{:S(2)}) collective-permute-start(f32[5,8,8,128]{3,2,1,0:T(8,128)S(1)} %get-tuple-element.88), channel_id=1, source_target_pairs={{0,8},{8,0},{16,24},{24,16},{32,40},{40,32},{48,56},{56,48},{64,72... | collective-permute-start | bytes 491528 | tf_op jit(solution)/shard_map/ppermute | solution.py:441
  40.8 0.0 collective-permute-done.9.refs_1_
  40.8 1.1 %shard_map.129 = (f32[5,8,8,128]{3,2,1,0:T(8,128)S(1)}, f32[5,8,8,128]{3,2,1,0:T(8,128)S(1)}, f32[5,12,8,128]{3,2,1,0:T(8,128)S(1)}) custom-call(f32[25,8,128]{2,1,0:T(8,128)S(1)} %get-tuple-element.54.c.refs_0_, f32[5,8,8,128]{3,2,1,0:T(8,128)S(1)} %collective-permute-done.9.refs_1_, f32[5,8,8,128]{3,2,1,0:T(8,128)S(1)} %get-tuple-element.90.refs_2_, ...), custom_call_target="tpu_custom_call" | custom-call | flops 4000000 | bytes 1708032 | tf_op jit(solution)/shard_map/pallas_call | solution.py:410
  42.0 0.0 collective-permute-done.7.one
  42.0 0.2 collective-permute-done.8.two
  42.2 0.7 %shard_map.130 = (f32[5,8,8,128]{3,2,1,0:T(8,128)S(1)}, f32[5,8,8,128]{3,2,1,0:T(8,128)S(1)}, f32[16,1,128]{2,1,0:T(1,128)S(1)}) custom-call(f32[25,8,128]{2,1,0:T(8,128)S(1)} %get-tuple-element.54.c.refs_0_, f32[5,8,8,128]{3,2,1,0:T(8,128)S(1)} %collective-permute-done.7.one, f32[5,8,8,128]{3,2,1,0:T(8,128)S(1)} %collective-permute-done.8.two, ...), custom_call_target="tpu_custom_call" | custom-call | flops 4000000 | bytes 2191360 | tf_op jit(solution)/shard_map/pallas_call | solution.py:410
  42.9 12.4 %all_to_all.10.parts = f32[16,1,128]{2,1,0:T(1,128)S(1)} all-to-all(f32[16,1,128]{2,1,0:T(1,128)S(1)} %get-tuple-element.102), channel_id=1, replica_groups={{12,13,14,15,8,9,10,11,4,5,6,7,0,1,2,3},{28,29,30,31,24,25,26,27,20,21,..., dimensions={0} | all-to-all | bytes 16384 | tf_op jit(solution)/shard_map/all_to_all | solution.py:461
  55.4 16.2 %all_to_all.11.refs_0_ = f32[32,1,128]{2,1,0:T(1,128)S(1)} all-to-all(f32[32,1,128]{2,1,0:T(1,128)S(1)} %shard_map.131), channel_id=1, replica_groups={{320,336,352,368,256,272,288,304,448,464,480,496,384,400,416,432,64,80,..., dimensions={0} | all-to-all | bytes 32768 | tf_op jit(solution)/shard_map/all_to_all | solution.py:461
  71.5 0.9 %shard_map.132 = (f32[1,5,8,1024]{3,2,1,0:T(8,128)}, f32[1,5,8,1024]{3,2,1,0:T(8,128)}, f32[1,8,1024]{2,1,0:T(8,128)}) custom-call(f32[32,1,128]{2,1,0:T(1,128)S(1)} %all_to_all.11.refs_0_, f32[5,8,128]{2,1,0:T(8,128)S(1)} %get-tuple-element.80.keep.refs_1_, f32[8,8,8,128]{3,2,1,0:T(8,128)S(1)} %shard_map.121.own.refs_4_.refs_7_.own_c.refs_2_, ...), custom_call_target="tpu_custom_call" | custom-call | flops 4000000 | bytes 1183744 | tf_op jit(solution)/shard_map/pallas_call | solution.py:410
  (1 shorter events, 0.0 us)
Async XLA Ops:
  0.6 10.0 %copy-start.1 = (f32[1,8,1024]{2,1,0:T(8,128)S(1)}, f32[1,8,1024]{2,1,0:T(8,128)}, u32[]{:S(2)}) copy-start(f32[1,8,1024]{2,1,0:T(8,128)} %observed.1) | copy-start | bytes 98308
  0.6 10.0 %copy-start = (f32[5,8,1024]{2,1,0:T(8,128)S(1)}, f32[5,8,1024]{2,1,0:T(8,128)}, u32[]{:S(2)}) copy-start(f32[5,8,1024]{2,1,0:T(8,128)} %background.1) | copy-start | bytes 491524
  0.7 10.0 %copy-start.2 = (f32[5,5]{1,0:T(8,128)S(1)}, f32[5,5]{1,0:T(8,128)}, u32[]{:S(2)}) copy-start(f32[5,5]{1,0:T(8,128)} %coupling.1) | copy-start | bytes 304
  0.7 10.0 %copy-start.3 = (s32[1,8,8]{2,1,0:T(8,128)S(1)}, s32[1,8,8]{2,1,0:T(8,128)}, u32[]{:S(2)}) copy-start(s32[1,8,8]{2,1,0:T(8,128)} %obs_level.1) | copy-start | bytes 772
  0.7 10.0 %copy-start.4 = (s32[1,8,8]{2,1,0:T(8,128)S(1)}, s32[1,8,8]{2,1,0:T(8,128)}, u32[]{:S(2)}) copy-start(s32[1,8,8]{2,1,0:T(8,128)} %huber_class.1) | copy-start | bytes 772
  1.8 8.9 %copy-start.5 = (f32[5]{0:T(128)S(1)}, f32[5]{0:T(128)}, u32[]{:S(2)}) copy-start(f32[5]{0:T(128)} %param.17) | copy-start | bytes 64
  1.8 11.9 %collective-permute-start.1 = (f32[8,8,8,128]{3,2,1,0:T(8,128)S(1)}, f32[8,8,8,128]{3,2,1,0:T(8,128)S(1)}, u32[]{:S(2)}, u32[]{:S(2)}) collective-permute-start(f32[8,8,8,128]{3,2,1,0:T(8,128)S(1)} %shard_map.121.own.refs_4_.refs_7_.own_c.refs_2_), channel_id=1, source_target_pairs={{0,1},{1,0},{2,3},{3,2},{4,5},{5,4},{6,7},{7,6},{9,10},{10,9},{11,... | collective-permute-start | bytes 786440 | tf_op jit(solution)/shard_map/ppermute | solution.py:452
  2.5 14.1 %collective-permute-start = (f32[8,8,8,128]{3,2,1,0:T(8,128)S(1)}, f32[8,8,8,128]{3,2,1,0:T(8,128)S(1)}, u32[]{:S(2)}, u32[]{:S(2)}) collective-permute-start(f32[8,8,8,128]{3,2,1,0:T(8,128)S(1)} %shard_map.121.own.refs_4_.refs_7_.own_c.refs_2_), channel_id=1, source_target_pairs={{1,2},{2,1},{3,4},{4,3},{5,6},{6,5},{8,9},{9,8},{10,11},{11,10},{1... | collective-permute-start | bytes 786440 | tf_op jit(solution)/shard_map/ppermute | solution.py:452
  10.8 10.2 %collective-permute-start.4 = (f32[5,8,8,128]{3,2,1,0:T(8,128)S(1)}, f32[5,8,8,128]{3,2,1,0:T(8,128)S(1)}, u32[]{:S(2)}, u32[]{:S(2)}) collective-permute-start(f32[5,8,8,128]{3,2,1,0:T(8,128)S(1)} %get-tuple-element.67), channel_id=1, source_target_pairs={{8,0},{16,8},{24,16},{32,24},{40,32},{48,40},{56,48},{64,56},{72,6... | collective-permute-start | bytes 491528 | tf_op jit(solution)/shard_map/ppermute | solution.py:431
  17.2 6.6 %collective-permute-start.2 = (f32[5,8,8,128]{3,2,1,0:T(8,128)S(1)}, f32[5,8,8,128]{3,2,1,0:T(8,128)S(1)}, u32[]{:S(2)}, u32[]{:S(2)}) collective-permute-start(f32[5,8,8,128]{3,2,1,0:T(8,128)S(1)} %get-tuple-element.65), channel_id=1, source_target_pairs={{8,16},{16,8},{24,32},{32,24},{40,48},{48,40},{56,64},{64,56},{72,... | collective-permute-start | bytes 491528 | tf_op jit(solution)/shard_map/ppermute | solution.py:441
  19.1 4.7 %collective-permute-start.3 = (f32[5,8,8,128]{3,2,1,0:T(8,128)S(1)}, f32[5,8,8,128]{3,2,1,0:T(8,128)S(1)}, u32[]{:S(2)}, u32[]{:S(2)}) collective-permute-start(f32[5,8,8,128]{3,2,1,0:T(8,128)S(1)} %get-tuple-element.66), channel_id=1, source_target_pairs={{0,8},{8,0},{16,24},{24,16},{32,40},{40,32},{48,56},{56,48},{64,72... | collective-permute-start | bytes 491528 | tf_op jit(solution)/shard_map/ppermute | solution.py:441
  24.5 10.2 %collective-permute-start.6 = (f32[5,8,8,128]{3,2,1,0:T(8,128)S(1)}, f32[5,8,8,128]{3,2,1,0:T(8,128)S(1)}, u32[]{:S(2)}, u32[]{:S(2)}) collective-permute-start(f32[5,8,8,128]{3,2,1,0:T(8,128)S(1)} %get-tuple-element.79.g.own.refs_4_.refs_3_), channel_id=1, source_target_pairs={{0,1},{1,0},{2,3},{3,2},{4,5},{5,4},{6,7},{7,6},{9,10},{10,9},{11,... | collective-permute-start | bytes 491528 | tf_op jit(solution)/shard_map/ppermute | solution.py:452
  25.1 9.5 %collective-permute-start.5 = (f32[5,8,8,128]{3,2,1,0:T(8,128)S(1)}, f32[5,8,8,128]{3,2,1,0:T(8,128)S(1)}, u32[]{:S(2)}, u32[]{:S(2)}) collective-permute-start(f32[5,8,8,128]{3,2,1,0:T(8,128)S(1)} %get-tuple-element.79.g.own.refs_4_.refs_3_), channel_id=1, source_target_pairs={{1,2},{2,1},{3,4},{4,3},{5,6},{6,5},{8,9},{9,8},{10,11},{11,10},{1... | collective-permute-start | bytes 491528 | tf_op jit(solution)/shard_map/ppermute | solution.py:452
  32.7 8.1 %collective-permute-start.9 = (f32[5,8,8,128]{3,2,1,0:T(8,128)S(1)}, f32[5,8,8,128]{3,2,1,0:T(8,128)S(1)}, u32[]{:S(2)}, u32[]{:S(2)}) collective-permute-start(f32[5,8,8,128]{3,2,1,0:T(8,128)S(1)} %get-tuple-element.89), channel_id=1, source_target_pairs={{8,0},{16,8},{24,16},{32,24},{40,32},{48,40},{56,48},{64,56},{72,6... | collective-permute-start | bytes 491528 | tf_op jit(solution)/shard_map/ppermute | solution.py:431
  35.2 6.7 %collective-permute-start.7 = (f32[5,8,8,128]{3,2,1,0:T(8,128)S(1)}, f32[5,8,8,128]{3,2,1,0:T(8,128)S(1)}, u32[]{:S(2)}, u32[]{:S(2)}) collective-permute-start(f32[5,8,8,128]{3,2,1,0:T(8,128)S(1)} %get-tuple-element.87), channel_id=1, source_target_pairs={{8,16},{16,8},{24,32},{32,24},{40,48},{48,40},{56,64},{64,56},{72,... | collective-permute-start | bytes 491528 | tf_op jit(solution)/shard_map/ppermute | solution.py:441
  38.9 3.3 %collective-permute-start.8 = (f32[5,8,8,128]{3,2,1,0:T(8,128)S(1)}, f32[5,8,8,128]{3,2,1,0:T(8,128)S(1)}, u32[]{:S(2)}, u32[]{:S(2)}) collective-permute-start(f32[5,8,8,128]{3,2,1,0:T(8,128)S(1)} %get-tuple-element.88), channel_id=1, source_target_pairs={{0,8},{8,0},{16,24},{24,16},{32,40},{40,32},{48,56},{56,48},{64,72... | collective-permute-start | bytes 491528 | tf_op jit(solution)/shard_map/ppermute | solution.py:441

commit v7 on v6

--- a/solution.py
+++ b/solution.py
@@ -60,6 +60,17 @@
     return sum(len(inside(s)) for s in range(step)) + r - inside(step)[0]
 
 
+class Once:
+    def __init__(self, of):
+        self.of, self.kept = of, {}
+
+    def __call__(self, l, r, name=None, make=None):
+        key = (name, l, r)
+        if key not in self.kept:
+            self.kept[key] = self.of(l, r) if make is None else make()
+        return self.kept[key]
+
+
 def march(row, src, rows, bufs, dst, inner, fill):
     for step in range(STEPS):
         lo, hi = step + 1, rows - step - 1
@@ -67,12 +78,14 @@
             lo, hi = inside(step).start, inside(step).stop
         ready = inside(step) if inner is not None and not fill else ()
 
-        def get(l, r, step=step):
+        def load(l, r, step=step):
             if step == 0:
                 return src(l, r)
             if inner is not None and r in inside(step - 1):
                 return inner[l, slot(step - 1, r)]
             return bufs[(step - 1) % 2][l, r]
+
+        get = Once(load)
 
         for r in range(lo, hi):
             if r in ready:
@@ -96,8 +109,8 @@
         for l in range(L):
             v = here[l]
             yield total(
-                [ce * sh.east(v), cw * sh.west(v), ky * (above[l] + below[l]), c0 * v]
-                + [c[L * l + m] * here[m] for m in range(L)]
+                [ce * sh.east(v), cw * sh.west(v), ky * (above[l] + below[l]), (c0 + c[(L + 1) * l]) * v]
+                + [c[L * l + m] * here[m] for m in range(L) if m != l]
             )
 
     march(row, src, rows, bufs, dst, inner, fill)
@@ -107,9 +120,12 @@
     sh = Shift()
 
     def row(get, r):
-        above, here, below = [[get(l, at) for l in range(L)] for at in (r - 1, r, r + 1)]
+        here = [get(l, r) for l in range(L)]
         ce, cw, ky = coef(0, r), coef(1, r), coef(2, r)
-        ky_above, ky_below = coef(2, r - 1), coef(2, r + 1)
+
+        def flux(l, r):
+            return get(l, r, "ky", lambda: coef(2, r) * get(l, r))
+
         c0 = centre(ce, cw, ky)
         for l in range(L):
             w = here[l]
@@ -117,10 +133,10 @@
                 [
                     sh.west(ce * w),
                     sh.east(cw * w),
-                    ky_above * above[l] + ky_below * below[l],
-                    c0 * w,
+                    flux(l, r - 1) + flux(l, r + 1),
+                    (c0 + c[(L + 1) * l]) * w,
                 ]
-                + [c[L * m + l] * here[m] for m in range(L)]
+                + [c[L * m + l] * here[m] for m in range(L) if m != l]
             )
 
     march(row, src, rows, bufs, dst, inner, fill)

time: 73.6 us -> 73.3 us (level)
  transfers between devices with their start and end apart: 10 -> 10, of which waited for: 3 -> 3; matrix products, arithmetic and copies ran while one was open for 0% -> 0% of each run, Pallas kernels for 7% -> 6%
where the time goes in v7:
time: 73.3 us; the launch traced here: 72.3 us
  starting transfers between devices  29.9 us (41%)
  blocking collectives  28.6 us (39%)
  Pallas kernels  7.98 us (11%)
  waiting for transfers between devices  4.89 us (7%)
  between operations  0.9 us (1%)
    all_to_all x2, blocking collectives, exchanged(): return lax.all_to_all(x, axes, 0, 0, axis_index_groups=[order], tiled=True)  28.6 us
    ppermute x4, starting transfers between devices, swapped_rows(): out.append(lax.ppermute(x, (TM[-1], 'lat'), both_ways(lows)))  16 us
    ppermute x4, starting transfers between devices, swapped(): lax.ppermute(x, TM, both_ways(range(start, count - 1, 2)))  9.43 us
    pallas_call x12, Pallas kernels, run(): pl.pallas_call(kernel, out_shape=[jax.ShapeDtypeStruct(s, jnp.float32) fo...  7.98 us
    ppermute x2, starting transfers between devices, shifted(): lax.ppermute(x, axis, [(i, i + by) for i in range(count) if 0 <= i + by <...  4.47 us
    ppermute x4, waiting for transfers between devices, swapped_rows(): out.append(lax.ppermute(x, (TM[-1], 'lat'), both_ways(lows)))  2.93 us
    ppermute x4, waiting for transfers between devices, swapped(): lax.ppermute(x, TM, both_ways(range(start, count - 1, 2)))  1.95 us
  transfers between devices with their start and end apart: 10, of which 3 were waited for; matrix products, arithmetic and copies ran while one was open for 0% of the time, Pallas kernels for 6%

profile of v7, /device:TPU:1, one launch (start us, length us, event | category | flops | bytes accessed | tf_op | source)
XLA Modules:
  0.0 72.3 jit_solution(3872709015456840629)
XLA Ops:
  0.6 0.0 copy-start.1
  0.6 0.0 copy-start
  0.7 0.0 copy-start.2
  0.7 0.0 copy-start.3
  0.7 0.0 copy-start.4
  0.7 1.1 %shard_map.121.own.refs_4_.refs_7_.own_c.refs_2_ = f32[8,8,8,128]{3,2,1,0:T(8,128)S(1)} custom-call(f32[1,5,8,1024]{3,2,1,0:T(8,128)} %x_far.1, f32[1,8,1024]{2,1,0:T(8,128)} %kx_far.1, f32[1,8,1024]{2,1,0:T(8,128)} %ky_far.1, f32[1,8,1024]{2,1,0:T(8,128)} %ux_far.1), custom_call_target="tpu_custom_call" | custom-call | flops 4000000 | bytes 262144 | tf_op jit(solution)/shard_map/pallas_call | solution.py:426
  1.8 0.0 copy-start.5
  1.8 0.7 collective-permute-start.1
  2.5 8.2 %collective-permute-start = (f32[8,8,8,128]{3,2,1,0:T(8,128)S(1)}, f32[8,8,8,128]{3,2,1,0:T(8,128)S(1)}, u32[]{:S(2)}, u32[]{:S(2)}) collective-permute-start(f32[8,8,8,128]{3,2,1,0:T(8,128)S(1)} %shard_map.121.own.refs_4_.refs_7_.own_c.refs_2_), channel_id=1, source_target_pairs={{1,2},{2,1},{3,4},{4,3},{5,6},{6,5},{8,9},{9,8},{10,11},{11,10},{1... | collective-permute-start | bytes 786440 | tf_op jit(solution)/shard_map/ppermute | solution.py:468
  10.6 0.0 copy-done.1
  10.6 0.0 copy-done
  10.6 0.0 copy-done.2
  10.6 0.0 copy-done.3
  10.7 0.0 copy-done.4
  10.7 0.0 copy-done.5
  10.7 0.1 shard_map.122
  10.8 2.6 %collective-permute-start.4 = (f32[5,8,8,128]{3,2,1,0:T(8,128)S(1)}, f32[5,8,8,128]{3,2,1,0:T(8,128)S(1)}, u32[]{:S(2)}, u32[]{:S(2)}) collective-permute-start(f32[5,8,8,128]{3,2,1,0:T(8,128)S(1)} %get-tuple-element.67), channel_id=1, source_target_pairs={{8,0},{16,8},{24,16},{32,24},{40,32},{48,40},{56,48},{64,56},{72,6... | collective-permute-start | bytes 491528 | tf_op jit(solution)/shard_map/ppermute | solution.py:447
  13.4 0.3 shard_map.123
  13.6 0.0 collective-permute-done.1.second
  13.7 2.9 %collective-permute-done.first = f32[8,8,8,128]{3,2,1,0:T(8,128)S(1)} collective-permute-done((f32[8,8,8,128]{3,2,1,0:T(8,128)S(1)}, f32[8,8,8,128]{3,2,1,0:T(8,128)S(1)}, u32[]{:S(2)}, u32[]{:S(2)}) %collective-permute-start) | collective-permute-done | bytes 262176 | tf_op jit(solution)/shard_map/ppermute | solution.py:468
  16.6 0.6 shard_map.124
  17.1 1.9 %collective-permute-start.2 = (f32[5,8,8,128]{3,2,1,0:T(8,128)S(1)}, f32[5,8,8,128]{3,2,1,0:T(8,128)S(1)}, u32[]{:S(2)}, u32[]{:S(2)}) collective-permute-start(f32[5,8,8,128]{3,2,1,0:T(8,128)S(1)} %get-tuple-element.65), channel_id=1, source_target_pairs={{8,16},{16,8},{24,32},{32,24},{40,48},{48,40},{56,64},{64,56},{72,... | collective-permute-start | bytes 491528 | tf_op jit(solution)/shard_map/ppermute | solution.py:457
  19.1 1.9 %collective-permute-start.3 = (f32[5,8,8,128]{3,2,1,0:T(8,128)S(1)}, f32[5,8,8,128]{3,2,1,0:T(8,128)S(1)}, u32[]{:S(2)}, u32[]{:S(2)}) collective-permute-start(f32[5,8,8,128]{3,2,1,0:T(8,128)S(1)} %get-tuple-element.66), channel_id=1, source_target_pairs={{0,8},{8,0},{16,24},{24,16},{32,40},{40,32},{48,56},{56,48},{64,72... | collective-permute-start | bytes 491528 | tf_op jit(solution)/shard_map/ppermute | solution.py:457
  21.0 0.0 collective-permute-done.4.refs_1_
  21.0 1.1 %shard_map.125 = (f32[5,8,8,128]{3,2,1,0:T(8,128)S(1)}, f32[5,8,8,128]{3,2,1,0:T(8,128)S(1)}, f32[5,12,8,128]{3,2,1,0:T(8,128)S(1)}) custom-call(f32[25,8,128]{2,1,0:T(8,128)S(1)} %get-tuple-element.54.c.refs_0_, f32[5,8,8,128]{3,2,1,0:T(8,128)S(1)} %collective-permute-done.4.refs_1_, f32[5,8,8,128]{3,2,1,0:T(8,128)S(1)} %get-tuple-element.68.refs_2_, ...), custom_call_target="tpu_custom_call" | custom-call | flops 4000000 | bytes 2002944 | tf_op jit(solution)/shard_map/pallas_call | solution.py:426
  22.1 1.7 %collective-permute-done.2.one = f32[5,8,8,128]{3,2,1,0:T(8,128)S(1)} collective-permute-done((f32[5,8,8,128]{3,2,1,0:T(8,128)S(1)}, f32[5,8,8,128]{3,2,1,0:T(8,128)S(1)}, u32[]{:S(2)}, u32[]{:S(2)}) %collective-permute-start.2) | collective-permute-done | bytes 163872 | tf_op jit(solution)/shard_map/ppermute | solution.py:457
  23.8 0.0 collective-permute-done.3.two
  23.8 0.6 shard_map.126
  24.4 0.7 collective-permute-start.6
  25.1 6.5 %collective-permute-start.5 = (f32[5,8,8,128]{3,2,1,0:T(8,128)S(1)}, f32[5,8,8,128]{3,2,1,0:T(8,128)S(1)}, u32[]{:S(2)}, u32[]{:S(2)}) collective-permute-start(f32[5,8,8,128]{3,2,1,0:T(8,128)S(1)} %get-tuple-element.79.g.own.refs_4_.refs_3_), channel_id=1, source_target_pairs={{1,2},{2,1},{3,4},{4,3},{5,6},{6,5},{8,9},{9,8},{10,11},{11,10},{1... | collective-permute-start | bytes 491528 | tf_op jit(solution)/shard_map/ppermute | solution.py:468
  31.6 1.0 %shard_map.127 = (f32[5,8,8,128]{3,2,1,0:T(8,128)S(1)}, f32[5,8,8,128]{3,2,1,0:T(8,128)S(1)}, f32[8,8,128]{2,1,0:T(8,128)S(1)}, f32[5,12,8,128]{3,2,1,0:T(8,128)S(1)}, f32[2,8,128]{2,1,0:T(8,128)S(1)}) custom-call(f32[25,8,128]{2,1,0:T(8,128)S(1)} %get-tuple-element.54.c.refs_0_, f32[5,8,128]{2,1,0:T(8,128)S(1)} %get-tuple-element.80.keep.refs_1_, ...), custom_call_target="tpu_custom_call" | custom-call | flops 6000000 | bytes 1662976 | tf_op jit(solution)/shard_map/pallas_call | solution.py:426
  32.6 1.9 %collective-permute-start.9 = (f32[5,8,8,128]{3,2,1,0:T(8,128)S(1)}, f32[5,8,8,128]{3,2,1,0:T(8,128)S(1)}, u32[]{:S(2)}, u32[]{:S(2)}) collective-permute-start(f32[5,8,8,128]{3,2,1,0:T(8,128)S(1)} %get-tuple-element.89), channel_id=1, source_target_pairs={{8,0},{16,8},{24,16},{32,24},{40,32},{48,40},{56,48},{64,56},{72,6... | collective-permute-start | bytes 491528 | tf_op jit(solution)/shard_map/ppermute | solution.py:447
  34.5 0.0 collective-permute-done.6.second
  34.5 0.0 collective-permute-done.5.first
  34.5 0.5 shard_map.128
  35.1 3.6 %collective-permute-start.7 = (f32[5,8,8,128]{3,2,1,0:T(8,128)S(1)}, f32[5,8,8,128]{3,2,1,0:T(8,128)S(1)}, u32[]{:S(2)}, u32[]{:S(2)}) collective-permute-start(f32[5,8,8,128]{3,2,1,0:T(8,128)S(1)} %get-tuple-element.87), channel_id=1, source_target_pairs={{8,16},{16,8},{24,32},{32,24},{40,48},{48,40},{56,64},{64,56},{72,... | collective-permute-start | bytes 491528 | tf_op jit(solution)/shard_map/ppermute | solution.py:457
  38.7 1.9 %collective-permute-start.8 = (f32[5,8,8,128]{3,2,1,0:T(8,128)S(1)}, f32[5,8,8,128]{3,2,1,0:T(8,128)S(1)}, u32[]{:S(2)}, u32[]{:S(2)}) collective-permute-start(f32[5,8,8,128]{3,2,1,0:T(8,128)S(1)} %get-tuple-element.88), channel_id=1, source_target_pairs={{0,8},{8,0},{16,24},{24,16},{32,40},{40,32},{48,56},{56,48},{64,72... | collective-permute-start | bytes 491528 | tf_op jit(solution)/shard_map/ppermute | solution.py:457
  40.6 0.0 collective-permute-done.9.refs_1_
  40.7 1.1 %shard_map.129 = (f32[5,8,8,128]{3,2,1,0:T(8,128)S(1)}, f32[5,8,8,128]{3,2,1,0:T(8,128)S(1)}, f32[5,12,8,128]{3,2,1,0:T(8,128)S(1)}) custom-call(f32[25,8,128]{2,1,0:T(8,128)S(1)} %get-tuple-element.54.c.refs_0_, f32[5,8,8,128]{3,2,1,0:T(8,128)S(1)} %collective-permute-done.9.refs_1_, f32[5,8,8,128]{3,2,1,0:T(8,128)S(1)} %get-tuple-element.90.refs_2_, ...), custom_call_target="tpu_custom_call" | custom-call | flops 4000000 | bytes 1708032 | tf_op jit(solution)/shard_map/pallas_call | solution.py:426
  41.7 0.0 collective-permute-done.7.one
  41.7 0.3 collective-permute-done.8.two
  42.0 0.7 shard_map.130
  42.7 12.5 %all_to_all.10.parts = f32[16,1,128]{2,1,0:T(1,128)S(1)} all-to-all(f32[16,1,128]{2,1,0:T(1,128)S(1)} %get-tuple-element.102), channel_id=1, replica_groups={{12,13,14,15,8,9,10,11,4,5,6,7,0,1,2,3},{28,29,30,31,24,25,26,27,20,21,..., dimensions={0} | all-to-all | bytes 16384 | tf_op jit(solution)/shard_map/all_to_all | solution.py:477
  55.2 16.1 %all_to_all.11.refs_0_ = f32[32,1,128]{2,1,0:T(1,128)S(1)} all-to-all(f32[32,1,128]{2,1,0:T(1,128)S(1)} %shard_map.131), channel_id=1, replica_groups={{320,336,352,368,256,272,288,304,448,464,480,496,384,400,416,432,64,80,..., dimensions={0} | all-to-all | bytes 32768 | tf_op jit(solution)/shard_map/all_to_all | solution.py:477
  71.3 0.9 %shard_map.132 = (f32[1,5,8,1024]{3,2,1,0:T(8,128)}, f32[1,5,8,1024]{3,2,1,0:T(8,128)}, f32[1,8,1024]{2,1,0:T(8,128)}) custom-call(f32[32,1,128]{2,1,0:T(1,128)S(1)} %all_to_all.11.refs_0_, f32[5,8,128]{2,1,0:T(8,128)S(1)} %get-tuple-element.80.keep.refs_1_, f32[8,8,8,128]{3,2,1,0:T(8,128)S(1)} %shard_map.121.own.refs_4_.refs_7_.own_c.refs_2_, ...), custom_call_target="tpu_custom_call" | custom-call | flops 4000000 | bytes 1183744 | tf_op jit(solution)/shard_map/pallas_call | solution.py:426
  (1 shorter events, 0.0 us)
Async XLA Ops:
  0.6 10.0 %copy-start.1 = (f32[1,8,1024]{2,1,0:T(8,128)S(1)}, f32[1,8,1024]{2,1,0:T(8,128)}, u32[]{:S(2)}) copy-start(f32[1,8,1024]{2,1,0:T(8,128)} %observed.1) | copy-start | bytes 98308
  0.6 10.0 %copy-start = (f32[5,8,1024]{2,1,0:T(8,128)S(1)}, f32[5,8,1024]{2,1,0:T(8,128)}, u32[]{:S(2)}) copy-start(f32[5,8,1024]{2,1,0:T(8,128)} %background.1) | copy-start | bytes 491524
  0.7 10.0 %copy-start.2 = (f32[5,5]{1,0:T(8,128)S(1)}, f32[5,5]{1,0:T(8,128)}, u32[]{:S(2)}) copy-start(f32[5,5]{1,0:T(8,128)} %coupling.1) | copy-start | bytes 304
  0.7 10.0 %copy-start.3 = (s32[1,8,8]{2,1,0:T(8,128)S(1)}, s32[1,8,8]{2,1,0:T(8,128)}, u32[]{:S(2)}) copy-start(s32[1,8,8]{2,1,0:T(8,128)} %obs_level.1) | copy-start | bytes 772
  0.7 10.0 %copy-start.4 = (s32[1,8,8]{2,1,0:T(8,128)S(1)}, s32[1,8,8]{2,1,0:T(8,128)}, u32[]{:S(2)}) copy-start(s32[1,8,8]{2,1,0:T(8,128)} %huber_class.1) | copy-start | bytes 772
  1.8 8.9 %copy-start.5 = (f32[5]{0:T(128)S(1)}, f32[5]{0:T(128)}, u32[]{:S(2)}) copy-start(f32[5]{0:T(128)} %param.17) | copy-start | bytes 64
  1.8 11.9 %collective-permute-start.1 = (f32[8,8,8,128]{3,2,1,0:T(8,128)S(1)}, f32[8,8,8,128]{3,2,1,0:T(8,128)S(1)}, u32[]{:S(2)}, u32[]{:S(2)}) collective-permute-start(f32[8,8,8,128]{3,2,1,0:T(8,128)S(1)} %shard_map.121.own.refs_4_.refs_7_.own_c.refs_2_), channel_id=1, source_target_pairs={{0,1},{1,0},{2,3},{3,2},{4,5},{5,4},{6,7},{7,6},{9,10},{10,9},{11,... | collective-permute-start | bytes 786440 | tf_op jit(solution)/shard_map/ppermute | solution.py:468
  2.5 14.1 %collective-permute-start = (f32[8,8,8,128]{3,2,1,0:T(8,128)S(1)}, f32[8,8,8,128]{3,2,1,0:T(8,128)S(1)}, u32[]{:S(2)}, u32[]{:S(2)}) collective-permute-start(f32[8,8,8,128]{3,2,1,0:T(8,128)S(1)} %shard_map.121.own.refs_4_.refs_7_.own_c.refs_2_), channel_id=1, source_target_pairs={{1,2},{2,1},{3,4},{4,3},{5,6},{6,5},{8,9},{9,8},{10,11},{11,10},{1... | collective-permute-start | bytes 786440 | tf_op jit(solution)/shard_map/ppermute | solution.py:468
  10.8 10.2 %collective-permute-start.4 = (f32[5,8,8,128]{3,2,1,0:T(8,128)S(1)}, f32[5,8,8,128]{3,2,1,0:T(8,128)S(1)}, u32[]{:S(2)}, u32[]{:S(2)}) collective-permute-start(f32[5,8,8,128]{3,2,1,0:T(8,128)S(1)} %get-tuple-element.67), channel_id=1, source_target_pairs={{8,0},{16,8},{24,16},{32,24},{40,32},{48,40},{56,48},{64,56},{72,6... | collective-permute-start | bytes 491528 | tf_op jit(solution)/shard_map/ppermute | solution.py:447
  17.1 6.6 %collective-permute-start.2 = (f32[5,8,8,128]{3,2,1,0:T(8,128)S(1)}, f32[5,8,8,128]{3,2,1,0:T(8,128)S(1)}, u32[]{:S(2)}, u32[]{:S(2)}) collective-permute-start(f32[5,8,8,128]{3,2,1,0:T(8,128)S(1)} %get-tuple-element.65), channel_id=1, source_target_pairs={{8,16},{16,8},{24,32},{32,24},{40,48},{48,40},{56,64},{64,56},{72,... | collective-permute-start | bytes 491528 | tf_op jit(solution)/shard_map/ppermute | solution.py:457
  19.1 4.7 %collective-permute-start.3 = (f32[5,8,8,128]{3,2,1,0:T(8,128)S(1)}, f32[5,8,8,128]{3,2,1,0:T(8,128)S(1)}, u32[]{:S(2)}, u32[]{:S(2)}) collective-permute-start(f32[5,8,8,128]{3,2,1,0:T(8,128)S(1)} %get-tuple-element.66), channel_id=1, source_target_pairs={{0,8},{8,0},{16,24},{24,16},{32,40},{40,32},{48,56},{56,48},{64,72... | collective-permute-start | bytes 491528 | tf_op jit(solution)/shard_map/ppermute | solution.py:457
  24.4 10.1 %collective-permute-start.6 = (f32[5,8,8,128]{3,2,1,0:T(8,128)S(1)}, f32[5,8,8,128]{3,2,1,0:T(8,128)S(1)}, u32[]{:S(2)}, u32[]{:S(2)}) collective-permute-start(f32[5,8,8,128]{3,2,1,0:T(8,128)S(1)} %get-tuple-element.79.g.own.refs_4_.refs_3_), channel_id=1, source_target_pairs={{0,1},{1,0},{2,3},{3,2},{4,5},{5,4},{6,7},{7,6},{9,10},{10,9},{11,... | collective-permute-start | bytes 491528 | tf_op jit(solution)/shard_map/ppermute | solution.py:468
  25.1 9.4 %collective-permute-start.5 = (f32[5,8,8,128]{3,2,1,0:T(8,128)S(1)}, f32[5,8,8,128]{3,2,1,0:T(8,128)S(1)}, u32[]{:S(2)}, u32[]{:S(2)}) collective-permute-start(f32[5,8,8,128]{3,2,1,0:T(8,128)S(1)} %get-tuple-element.79.g.own.refs_4_.refs_3_), channel_id=1, source_target_pairs={{1,2},{2,1},{3,4},{4,3},{5,6},{6,5},{8,9},{9,8},{10,11},{11,10},{1... | collective-permute-start | bytes 491528 | tf_op jit(solution)/shard_map/ppermute | solution.py:468
  32.6 8.1 %collective-permute-start.9 = (f32[5,8,8,128]{3,2,1,0:T(8,128)S(1)}, f32[5,8,8,128]{3,2,1,0:T(8,128)S(1)}, u32[]{:S(2)}, u32[]{:S(2)}) collective-permute-start(f32[5,8,8,128]{3,2,1,0:T(8,128)S(1)} %get-tuple-element.89), channel_id=1, source_target_pairs={{8,0},{16,8},{24,16},{32,24},{40,32},{48,40},{56,48},{64,56},{72,6... | collective-permute-start | bytes 491528 | tf_op jit(solution)/shard_map/ppermute | solution.py:447
  35.1 6.7 %collective-permute-start.7 = (f32[5,8,8,128]{3,2,1,0:T(8,128)S(1)}, f32[5,8,8,128]{3,2,1,0:T(8,128)S(1)}, u32[]{:S(2)}, u32[]{:S(2)}) collective-permute-start(f32[5,8,8,128]{3,2,1,0:T(8,128)S(1)} %get-tuple-element.87), channel_id=1, source_target_pairs={{8,16},{16,8},{24,32},{32,24},{40,48},{48,40},{56,64},{64,56},{72,... | collective-permute-start | bytes 491528 | tf_op jit(solution)/shard_map/ppermute | solution.py:457
  38.7 3.3 %collective-permute-start.8 = (f32[5,8,8,128]{3,2,1,0:T(8,128)S(1)}, f32[5,8,8,128]{3,2,1,0:T(8,128)S(1)}, u32[]{:S(2)}, u32[]{:S(2)}) collective-permute-start(f32[5,8,8,128]{3,2,1,0:T(8,128)S(1)} %get-tuple-element.88), channel_id=1, source_target_pairs={{0,8},{8,0},{16,24},{24,16},{32,40},{40,32},{48,56},{56,48},{64,72... | collective-permute-start | bytes 491528 | tf_op jit(solution)/shard_map/ppermute | solution.py:457
